TPU v7x, 32 devices: a whole 2x2x4 slice. The times are simulated.
32 devices in a mesh: fsdp: 4 (over y, x), ctx: 8 (over z, core).
Axes of the slice: x: 2, y: 2, z: 4, core: 2. Of those that a mesh axis runs over, the one named last changes fastest.
Arguments:
- tokens: bfloat16 [12288, 768], P(('fsdp', 'ctx')), may hold values from -6 to 6
- cotangent: bfloat16 [12288, 768], P(('fsdp', 'ctx')), may hold values from -6 to 6
- w_qkv: bfloat16 [768, 2304], P('fsdp'), may hold values from -0.21875 to 0.21875
- b_query: bfloat16 [768], P('fsdp'), may hold values from -1.75 to 1.75
- b_value: bfloat16 [768], P('fsdp'), may hold values from -1.75 to 1.75
- w_out: bfloat16 [768, 768], P('fsdp'), may hold values from -3.5 to 3.5
- b_out: bfloat16 [768], P('fsdp'), may hold values from -1.75 to 1.75
- w_fc: bfloat16 [768, 3072], P('fsdp'), may hold values from -0.21875 to 0.21875
- b_fc: bfloat16 [3072], P('fsdp'), may hold values from -1.75 to 1.75
- w_proj: bfloat16 [3072, 768], P('fsdp'), may hold values from -0.109375 to 0.109375
- b_proj: bfloat16 [768], P('fsdp'), may hold values from -1.75 to 1.75
- gain1: bfloat16 [768], P('fsdp'), may hold values from 0.5 to 1.5
- shift1: bfloat16 [768], P('fsdp'), may hold values from -1.75 to 1.75
- gain2: bfloat16 [768], P('fsdp'), may hold values from 0.5 to 1.5
- shift2: bfloat16 [768], P('fsdp'), may hold values from -1.75 to 1.75
- counts: int32 [4, 8], P('fsdp'), may hold values from 192 to 384, as said below
- seq_lengths: int32 [4, 3], P('fsdp'), may hold values from 1 to 3070, as said below
Outputs:
- block_out: bfloat16 [12288, 768], P(('fsdp', 'ctx'))
- d_tokens: float32 [12288, 768], P(('fsdp', 'ctx'))
- d_w_qkv: float32 [768, 2304], P('fsdp')
- d_b_query: float32 [768], P('fsdp')
- d_b_value: float32 [768], P('fsdp')
- d_w_out: float32 [768, 768], P('fsdp')
- d_b_out: float32 [768], P('fsdp')
- d_w_fc: float32 [768, 3072], P('fsdp')
- d_b_fc: float32 [3072], P('fsdp')
- d_w_proj: float32 [3072, 768], P('fsdp')
- d_b_proj: float32 [768], P('fsdp')
- d_gain1: float32 [768], P('fsdp')
- d_shift1: float32 [768], P('fsdp')
- d_gain2: float32 [768], P('fsdp')
- d_shift2: float32 [768], P('fsdp')
Inputs may be any that keep to these rules, and one draw needn't show every extreme that they name: `counts`: each device holds between 192 and 384 live slots, its first ones; in every group some device holds exactly 384. `seq_lengths`: the lengths of a group sum to its live slots; in every group one sequence, at a position that varies, holds a slot of the first device and of the last device of the group; the other two have fewer than 96 tokens each.
All inputs are finite; a program needn't handle non-finite values.
Results may differ from a plain program's by a relative error of at most 0.018.
Values may be sent and summed in bfloat16 or wider, within the bound.
No kernel may reach another device: no remote copies, remote signals or barrier semaphores. Data moves between devices by JAX's collectives and lax.ppermute only.
A program may use at most 192 MiB of HBM per device.

v0:
```python
import functools

import jax
import jax.numpy as jnp
from jax import lax
from jax.experimental import pallas as pl
from jax.experimental.pallas import tpu as pltpu
from jax.sharding import PartitionSpec as P

HEADS = 12


EPS = 1e-05


def layer_norm(values, gain_row, shift_row):
    centre = values - jnp.mean(values, axis=1, keepdims=True)
    inverse = lax.rsqrt(jnp.mean(centre * centre, axis=1, keepdims=True) + EPS)
    normed = centre * inverse
    return (normed * gain_row + shift_row, normed, inverse)


def norm_back(grad_in, normed, inverse, gain_row):
    scaled = grad_in * gain_row
    inner_grad = inverse * (
        scaled
        - jnp.mean(scaled, axis=1, keepdims=True)
        - normed * jnp.mean(scaled * normed, axis=1, keepdims=True)
    )
    return (inner_grad, jnp.sum(grad_in * normed, axis=0), jnp.sum(grad_in, axis=0))


def contract_rows(left_side, right_side):
    return lax.dot_general(
        left_side, right_side, (((0,), (0,)), ((), ())), preferred_element_type=jnp.float32
    )


def times_transpose(left_side, right_side):
    return lax.dot_general(
        left_side, right_side, (((1,), (1,)), ((), ())), preferred_element_type=jnp.float32
    )


def gelu_tanh(values):
    return jax.nn.gelu(values, approximate=True)


def describe(slot_ids, row_count, count_row, offsets, seq_ends):
    peer_count = count_row.shape[0]
    device = slot_ids // row_count
    within = slot_ids - device * row_count
    matches = device[:, None] == jnp.arange(peer_count, dtype=jnp.int32)[None, :]
    live_count = jnp.sum(jnp.where(matches, count_row[None, :], 0), axis=1)
    first_place = jnp.sum(jnp.where(matches, offsets[None, :], 0), axis=1)
    places = first_place + within
    segment = jnp.sum((places[:, None] >= seq_ends[None, :]).astype(jnp.int32), axis=1)
    return (within < live_count, places, segment, slot_ids)


def allowed(query_info, key_info):
    q_live, q_place, q_seg, q_slot = query_info
    k_live, k_place, k_seg, k_slot = key_info
    same_seq = (
        q_live[:, None]
        & k_live[None, :]
        & (q_seg[:, None] == k_seg[None, :])
        & (k_place[None, :] <= q_place[:, None])
    )
    return same_seq | (q_slot[:, None] == k_slot[None, :])


def over_blocks(step_fn, status, pieces, row_count):
    total_rows = pieces[0].shape[0]
    block_total = total_rows // row_count
    stacked = tuple((piece.reshape((block_total, row_count) + piece.shape[1:]) for piece in pieces))

    def scan_body(state_now, scan_item):
        block_index, block_parts = scan_item
        return (step_fn(state_now, block_parts, block_index * row_count), None)

    status, unused = lax.scan(
        scan_body, status, (jnp.arange(block_total, dtype=jnp.int32), stacked)
    )
    return status


def score_grads(
    query_heads, key_heads, value_heads, grad_heads, lse_rows, delta_rows, permitted, scaling
):
    scores = (
        jnp.einsum("qhd,khd->hqk", query_heads, key_heads, preferred_element_type=jnp.float32)
        * scaling
    )
    probabilities = jnp.where(permitted[None], jnp.exp(scores - lse_rows[:, :, None]), 0.0)
    grad_probs = jnp.einsum(
        "qhd,khd->hqk", grad_heads, value_heads, preferred_element_type=jnp.float32
    )
    grad_scores = (probabilities * (grad_probs - delta_rows[:, :, None])).astype(jnp.bfloat16)
    return (probabilities.astype(jnp.bfloat16), grad_scores)


def general_body(
    tokens,
    cotangent,
    w_qkv,
    b_query,
    b_value,
    w_out,
    b_out,
    w_fc,
    b_fc,
    w_proj,
    b_proj,
    gain1,
    shift1,
    gain2,
    shift2,
    counts,
    seq_lengths,
):
    row_count, feature_count = tokens.shape
    peer_count = lax.axis_size("ctx")
    my_index = lax.axis_index("ctx")
    head_count = HEADS
    head_width = feature_count // head_count
    scaling = head_width ** (-0.5)
    count_row = counts[0]
    offsets = jnp.cumsum(count_row) - count_row
    seq_ends = jnp.cumsum(seq_lengths[0])

    def locate(first_slot, length):
        return describe(
            first_slot + jnp.arange(length, dtype=jnp.int32),
            row_count,
            count_row,
            offsets,
            seq_ends,
        )

    own_rows = locate(my_index * row_count, row_count)
    fp32 = jnp.float32
    bf16 = jnp.bfloat16
    (
        qkv_full,
        query_bias,
        value_bias,
        out_full,
        out_bias,
        fc_full,
        fc_bias,
        proj_full,
        proj_bias,
        gain_one,
        shift_one,
        gain_two,
        shift_two,
    ) = (
        lax.all_gather(w_qkv, "fsdp", axis=0, tiled=True),
        lax.all_gather(b_query, "fsdp", axis=0, tiled=True),
        lax.all_gather(b_value, "fsdp", axis=0, tiled=True),
        lax.all_gather(w_out, "fsdp", axis=0, tiled=True),
        lax.all_gather(b_out, "fsdp", axis=0, tiled=True),
        lax.all_gather(w_fc, "fsdp", axis=0, tiled=True),
        lax.all_gather(b_fc, "fsdp", axis=0, tiled=True),
        lax.all_gather(w_proj, "fsdp", axis=0, tiled=True),
        lax.all_gather(b_proj, "fsdp", axis=0, tiled=True),
        lax.all_gather(gain1, "fsdp", axis=0, tiled=True),
        lax.all_gather(shift1, "fsdp", axis=0, tiled=True),
        lax.all_gather(gain2, "fsdp", axis=0, tiled=True),
        lax.all_gather(shift2, "fsdp", axis=0, tiled=True),
    )
    inputs = tokens.astype(fp32)
    normed_one, unit_one, inverse_one = layer_norm(
        inputs, gain_one.astype(fp32), shift_one.astype(fp32)
    )
    normed_low = normed_one.astype(bf16)
    bias_row = jnp.concatenate([query_bias, jnp.zeros_like(query_bias), value_bias]).astype(fp32)
    packed = (jnp.dot(normed_low, qkv_full, preferred_element_type=fp32) + bias_row).astype(bf16)
    query_rows = packed[:, :feature_count]
    key_rows = packed[:, feature_count : 2 * feature_count]
    value_rows = packed[:, 2 * feature_count :]
    query_heads = query_rows.reshape(row_count, head_count, head_width)

    def forward_step(status, pieces, first_row):
        running_max, running_sum, running_acc = status
        key_piece, value_piece = pieces
        length = key_piece.shape[0]
        key_heads = key_piece.reshape(length, head_count, head_width)
        value_heads = value_piece.reshape(length, head_count, head_width)
        scores = (
            jnp.einsum("qhd,khd->hqk", query_heads, key_heads, preferred_element_type=fp32)
            * scaling
        )
        permitted = allowed(own_rows, locate(first_row, length))
        scores = jnp.where(permitted[None], scores, -jnp.inf)
        new_max = jnp.maximum(running_max, jnp.max(scores, axis=2))
        fading = jnp.exp(running_max - new_max)
        weights = jnp.exp(scores - new_max[:, :, None])
        running_sum = running_sum * fading + jnp.sum(weights, axis=2)
        update = jnp.einsum(
            "hqk,khd->qhd", weights.astype(bf16), value_heads, preferred_element_type=fp32
        )
        running_acc = running_acc * jnp.transpose(fading)[:, :, None] + update
        return (new_max, running_sum, running_acc)

    start_state = (
        jnp.full((head_count, row_count), -1e30, fp32),
        jnp.zeros((head_count, row_count), fp32),
        jnp.zeros((row_count, head_count, head_width), fp32),
    )
    final_max, final_sum, final_acc = over_blocks(
        forward_step,
        start_state,
        (
            lax.all_gather(key_rows, "ctx", axis=0, tiled=True),
            lax.all_gather(value_rows, "ctx", axis=0, tiled=True),
        ),
        row_count,
    )
    attended_heads = final_acc / jnp.transpose(final_sum)[:, :, None]
    attended = attended_heads.reshape(row_count, feature_count)
    log_total = final_max + jnp.log(final_sum)
    attended_low = attended.astype(bf16)
    middle = (
        inputs
        + jnp.dot(attended_low, out_full, preferred_element_type=fp32)
        + out_bias.astype(fp32)
    )
    normed_two, unit_two, inverse_two = layer_norm(
        middle, gain_two.astype(fp32), shift_two.astype(fp32)
    )
    normed_two_low = normed_two.astype(bf16)
    hidden = jnp.dot(normed_two_low, fc_full, preferred_element_type=fp32) + fc_bias.astype(fp32)
    activated = gelu_tanh(hidden).astype(bf16)
    output = (
        middle + jnp.dot(activated, proj_full, preferred_element_type=fp32) + proj_bias.astype(fp32)
    )
    output_low = output.astype(bf16)
    qkv_full, out_full, fc_full, proj_full, gain_one, gain_two = (
        lax.all_gather(w_qkv, "fsdp", axis=0, tiled=True),
        lax.all_gather(w_out, "fsdp", axis=0, tiled=True),
        lax.all_gather(w_fc, "fsdp", axis=0, tiled=True),
        lax.all_gather(w_proj, "fsdp", axis=0, tiled=True),
        lax.all_gather(gain1, "fsdp", axis=0, tiled=True),
        lax.all_gather(gain2, "fsdp", axis=0, tiled=True),
    )
    live_rows = own_rows[0].astype(fp32)[:, None]
    grad_out = cotangent.astype(fp32) * live_rows
    grad_out_low = grad_out.astype(bf16)
    grad_proj = contract_rows(activated, grad_out_low)
    grad_proj_bias = jnp.sum(grad_out, axis=0)
    grad_act = times_transpose(grad_out_low, proj_full)
    grad_hidden = jax.vjp(gelu_tanh, hidden)[1](grad_act)[0]
    grad_hidden_low = grad_hidden.astype(bf16)
    grad_fc = contract_rows(normed_two_low, grad_hidden_low)
    grad_fc_bias = jnp.sum(grad_hidden_low.astype(fp32), axis=0)
    grad_normed_two = times_transpose(grad_hidden_low, fc_full)
    grad_mid_norm, grad_gain_two, grad_shift_two = norm_back(
        grad_normed_two, unit_two, inverse_two, gain_two.astype(fp32)
    )
    grad_middle = grad_out + grad_mid_norm
    grad_middle_low = grad_middle.astype(bf16)
    grad_out_proj = contract_rows(attended_low, grad_middle_low)
    grad_out_bias = jnp.sum(grad_middle_low.astype(fp32), axis=0)
    grad_attended = times_transpose(grad_middle_low, out_full).astype(bf16)
    grad_heads = grad_attended.reshape(row_count, head_count, head_width)
    delta_rows = jnp.transpose(jnp.sum(grad_heads.astype(fp32) * attended_heads, axis=2))

    def back_step(status, pieces, first_row):
        grad_query, grad_keys = status
        key_piece, value_piece = pieces
        length = key_piece.shape[0]
        key_heads = key_piece.reshape(length, head_count, head_width)
        value_heads = value_piece.reshape(length, head_count, head_width)
        permitted = allowed(own_rows, locate(first_row, length))
        probs_low, grad_scores = score_grads(
            query_heads,
            key_heads,
            value_heads,
            grad_heads,
            log_total,
            delta_rows,
            permitted,
            scaling,
        )
        grad_query = (
            grad_query
            + jnp.einsum("hqk,khd->qhd", grad_scores, key_heads, preferred_element_type=fp32)
            * scaling
        )
        grad_key_part = (
            jnp.einsum("hqk,qhd->khd", grad_scores, query_heads, preferred_element_type=fp32)
            * scaling
        )
        grad_value_part = jnp.einsum(
            "hqk,qhd->khd", probs_low, grad_heads, preferred_element_type=fp32
        )
        joined = jnp.concatenate(
            [
                grad_key_part.reshape(length, feature_count),
                grad_value_part.reshape(length, feature_count),
            ],
            axis=1,
        )
        current = lax.dynamic_slice_in_dim(grad_keys, first_row, length, 0)
        grad_keys = lax.dynamic_update_slice_in_dim(grad_keys, current + joined, first_row, 0)
        return (grad_query, grad_keys)

    keys_start = jnp.zeros((peer_count * row_count, 2 * feature_count), fp32)
    grad_query, grad_keys = over_blocks(
        back_step,
        (jnp.zeros((row_count, head_count, head_width), fp32), keys_start),
        (
            lax.all_gather(key_rows, "ctx", axis=0, tiled=True),
            lax.all_gather(value_rows, "ctx", axis=0, tiled=True),
        ),
        row_count,
    )
    grad_kv = lax.psum_scatter(
        grad_keys.astype(jnp.bfloat16), "ctx", scatter_dimension=0, tiled=True
    ).astype(jnp.float32)
    grad_packed = jnp.concatenate(
        [grad_query.reshape(row_count, feature_count), grad_kv], axis=1
    ).astype(bf16)
    grad_packed_wide = grad_packed.astype(fp32)
    grad_query_bias = jnp.sum(grad_packed_wide[:, :feature_count], axis=0)
    grad_value_bias = jnp.sum(grad_packed_wide[:, 2 * feature_count :], axis=0)
    grad_qkv = contract_rows(normed_low, grad_packed)
    grad_normed_one = times_transpose(grad_packed, qkv_full)
    grad_in_norm, grad_gain_one, grad_shift_one = norm_back(
        grad_normed_one, unit_one, inverse_one, gain_one.astype(fp32)
    )
    grad_tokens = grad_middle + grad_in_norm
    (
        sum_qkv,
        sum_qbias,
        sum_vbias,
        sum_out,
        sum_obias,
        sum_fc,
        sum_fbias,
        sum_proj,
        sum_pbias,
        sum_gain_one,
        sum_shift_one,
        sum_gain_two,
        sum_shift_two,
    ) = (
        lax.psum_scatter(
            grad_qkv.astype(jnp.bfloat16), "fsdp", scatter_dimension=0, tiled=True
        ).astype(jnp.float32),
        lax.psum_scatter(
            grad_query_bias.astype(jnp.bfloat16), "fsdp", scatter_dimension=0, tiled=True
        ).astype(jnp.float32),
        lax.psum_scatter(
            grad_value_bias.astype(jnp.bfloat16), "fsdp", scatter_dimension=0, tiled=True
        ).astype(jnp.float32),
        lax.psum_scatter(
            grad_out_proj.astype(jnp.bfloat16), "fsdp", scatter_dimension=0, tiled=True
        ).astype(jnp.float32),
        lax.psum_scatter(
            grad_out_bias.astype(jnp.bfloat16), "fsdp", scatter_dimension=0, tiled=True
        ).astype(jnp.float32),
        lax.psum_scatter(
            grad_fc.astype(jnp.bfloat16), "fsdp", scatter_dimension=0, tiled=True
        ).astype(jnp.float32),
        lax.psum_scatter(
            grad_fc_bias.astype(jnp.bfloat16), "fsdp", scatter_dimension=0, tiled=True
        ).astype(jnp.float32),
        lax.psum_scatter(
            grad_proj.astype(jnp.bfloat16), "fsdp", scatter_dimension=0, tiled=True
        ).astype(jnp.float32),
        lax.psum_scatter(
            grad_proj_bias.astype(jnp.bfloat16), "fsdp", scatter_dimension=0, tiled=True
        ).astype(jnp.float32),
        lax.psum_scatter(
            grad_gain_one.astype(jnp.bfloat16), "fsdp", scatter_dimension=0, tiled=True
        ).astype(jnp.float32),
        lax.psum_scatter(
            grad_shift_one.astype(jnp.bfloat16), "fsdp", scatter_dimension=0, tiled=True
        ).astype(jnp.float32),
        lax.psum_scatter(
            grad_gain_two.astype(jnp.bfloat16), "fsdp", scatter_dimension=0, tiled=True
        ).astype(jnp.float32),
        lax.psum_scatter(
            grad_shift_two.astype(jnp.bfloat16), "fsdp", scatter_dimension=0, tiled=True
        ).astype(jnp.float32),
    )
    totals = (
        lax.psum(sum_qkv.astype(jnp.bfloat16), "ctx").astype(jnp.float32),
        lax.psum(sum_qbias.astype(jnp.bfloat16), "ctx").astype(jnp.float32),
        lax.psum(sum_vbias.astype(jnp.bfloat16), "ctx").astype(jnp.float32),
        lax.psum(sum_out.astype(jnp.bfloat16), "ctx").astype(jnp.float32),
        lax.psum(sum_obias.astype(jnp.bfloat16), "ctx").astype(jnp.float32),
        lax.psum(sum_fc.astype(jnp.bfloat16), "ctx").astype(jnp.float32),
        lax.psum(sum_fbias.astype(jnp.bfloat16), "ctx").astype(jnp.float32),
        lax.psum(sum_proj.astype(jnp.bfloat16), "ctx").astype(jnp.float32),
        lax.psum(sum_pbias.astype(jnp.bfloat16), "ctx").astype(jnp.float32),
        lax.psum(sum_gain_one.astype(jnp.bfloat16), "ctx").astype(jnp.float32),
        lax.psum(sum_shift_one.astype(jnp.bfloat16), "ctx").astype(jnp.float32),
        lax.psum(sum_gain_two.astype(jnp.bfloat16), "ctx").astype(jnp.float32),
        lax.psum(sum_shift_two.astype(jnp.bfloat16), "ctx").astype(jnp.float32),
    )
    return (
        output_low,
        grad_tokens,
        totals[0],
        totals[1],
        totals[2],
        totals[3],
        totals[4],
        totals[5],
        totals[6],
        totals[7],
        totals[8],
        totals[9],
        totals[10],
        totals[11],
        totals[12],
    )


FP32 = jnp.float32
BF16 = jnp.bfloat16
FLOOR = -1e30
NEVER = 1 << 30


def dot_nt(left_side, right_side):
    return lax.dot_general(
        left_side, right_side, (((1,), (1,)), ((), ())), preferred_element_type=FP32
    )


def dot_nn(left_side, right_side):
    return lax.dot_general(
        left_side, right_side, (((1,), (0,)), ((), ())), preferred_element_type=FP32
    )


def spread(column_tile, width):
    return jnp.concatenate([column_tile] * (width // column_tile.shape[1]), axis=1)


def masked_scores(scores, key_ids, first_row, last_row):
    permitted = key_ids >= first_row
    if last_row is not None:
        permitted = permitted & (key_ids <= last_row)
    return jnp.where(permitted, scores, -jnp.inf)


def project_block(
    tokens_ref, wq_ref, wk_ref, wv_ref, bq_ref, bv_ref, gain_ref, shift_ref, stores, position, wanted
):
    q_ref, k_ref, kt_ref, v_ref, vt_ref, normed_ref = stores
    normed = layer_norm(tokens_ref[...].astype(FP32), gain_ref[...], shift_ref[...])[0]
    normed = normed.astype(BF16)
    keys = dot_nn(normed, wk_ref[...])
    values = dot_nn(normed, wv_ref[...]) + bv_ref[...]
    k_ref[position] = keys.astype(BF16)
    v_ref[position] = values.astype(BF16)
    kt_ref[position] = keys.T.astype(BF16)
    vt_ref[position] = values.T.astype(BF16)
    if wanted:
        queries = (dot_nn(normed, wq_ref[...]) + bq_ref[...]).astype(BF16)
        q_ref[position // 2] = (queries.astype(FP32) * 0.125).astype(BF16)
        normed_ref[position // 2] = normed


def project_kernel(where, t0, t1, t2, t3, wq, wk, wv, bq, bv, gain, shift, q, k, kt, v, vt, normed):
    core, chip = where[1], where[2]
    stores = (q, k, kt, v, vt, normed)
    for n, block in enumerate((t0, t1, t2, t3)):
        owner = (chip ^ (n // 2)) % 2
        position = 2 * owner + (core if n % 2 == 0 else 1 - core)
        project_block(block, wq, wk, wv, bq, bv, gain, shift, stores, position, n % 2 == 0)


def attend_kernel(
    where,
    t0,
    t1,
    t2,
    t3,
    wq_ref,
    wk_ref,
    wv_ref,
    bq_ref,
    bv_ref,
    gain_ref,
    shift_ref,
    q_half,
    k_half,
    kt_half,
    v_half,
    vt_half,
    normed_half,
    key_ref,
    low_ref,
    high_ref,
    far_ref,
    q_ref,
    k_ref,
    kt_ref,
    v_ref,
    normed_ref,
    o0_ref,
    o1_ref,
    o2_ref,
    o3_ref,
    ot_ref,
    lse_ref,
    zero_ref,
    vt_ref,
    acc_ref,
    o_ref,
):
    blocks, rows, width = q_ref.shape
    heads = width // 64
    core, chip = where[1], where[2]
    side = chip // 2
    zero_ref[...] = jnp.zeros_like(zero_ref)
    stores = (q_ref, k_ref, kt_ref, v_ref, vt_ref, normed_ref)
    for n, block in enumerate((t0, t1, t2, t3)):
        owner = chip ^ (2 + n // 2)
        position = 2 * owner + (core if n % 2 == 0 else 1 - core)
        project_block(
            block,
            wq_ref,
            wk_ref,
            wv_ref,
            bq_ref,
            bv_ref,
            gain_ref,
            shift_ref,
            stores,
            position,
            n % 2 == 0,
        )
    for n in range(blocks):
        for source, target in ((k_half, k_ref), (kt_half, kt_ref), (v_half, v_ref), (vt_half, vt_ref)):
            target[side * blocks + n] = source[n]
    for n in range(blocks // 2):
        q_ref[side * (blocks // 2) + n] = q_half[n]
        normed_ref[side * (blocks // 2) + n] = normed_half[n]

    def query_block(index, unused):
        queries = [q_ref[index, :, 64 * h : 64 * h + 64] for h in range(heads)]
        acc_ref[...] = jnp.zeros_like(acc_ref)

        def key_step(key_block, carry, first_row, last_row):
            ids = spread(key_ref[key_block], rows)
            result = []
            for h in range(heads):
                span = slice(64 * h, 64 * h + 64)
                top, total = carry[h]
                scores = dot_nt(k_ref[key_block, :, span], queries[h])
                scores = masked_scores(scores, ids, first_row, last_row)
                new_top = jnp.maximum(top, jnp.max(scores, axis=0, keepdims=True))
                fade = jnp.exp(top - new_top)
                weights = jnp.exp(scores - new_top)
                total = total * fade + jnp.sum(weights, axis=0, keepdims=True)
                acc_ref[span, :] = acc_ref[span, :] * fade + dot_nn(
                    vt_ref[key_block, span, :], weights.astype(BF16)
                )
                result.append((new_top, total))
            return tuple(result)

        start = tuple(
            (jnp.full((1, rows), FLOOR, FP32), jnp.zeros((1, rows), FP32)) for h in range(heads)
        )
        own = 2 * index + core
        far_row = far_ref[index]
        carry = lax.fori_loop(0, own, lambda j, c: key_step(j, c, far_row, None), start)
        carry = key_step(own, carry, low_ref[index], high_ref[index])
        for h in range(heads):
            span = slice(64 * h, 64 * h + 64)
            top, total = carry[h]
            attended = acc_ref[span, :] / total
            ot_ref[index, span, :] = attended
            o_ref[index, :, span] = attended.T.astype(BF16)
            lse_ref[index, h : h + 1, :] = top + jnp.log(total)
        return unused

    lax.fori_loop(0, blocks, query_block, 0)
    for s, ref in enumerate((o0_ref, o1_ref, o2_ref, o3_ref)):
        ref[...] = o_ref[chip ^ s]


def attend_back_kernel(
    where,
    q_ref,
    k_ref,
    kt_ref,
    v_ref,
    d0_ref,
    d1_ref,
    d2_ref,
    d3_ref,
    key_ref,
    low_ref,
    high_ref,
    far_ref,
    ot_ref,
    lse_ref,
    dq_ref,
    keep_ref,
    send_ref,
    acc_ref,
    dk_ref,
    dv_ref,
    da_ref,
):
    blocks, rows, width = q_ref.shape
    heads = width // 64
    core, chip = where[1], where[2]
    for s, ref in enumerate((d0_ref, d1_ref, d2_ref, d3_ref)):
        da_ref[chip ^ s] = ref[...]
    dk_ref[...] = jnp.zeros_like(dk_ref)
    dv_ref[...] = jnp.zeros_like(dv_ref)

    def query_block(index, unused):
        queries = [q_ref[index, :, 64 * h : 64 * h + 64] for h in range(heads)]
        grads = [da_ref[index, :, 64 * h : 64 * h + 64] for h in range(heads)]
        deltas = [
            jnp.sum(
                grads[h].astype(FP32).T * ot_ref[index, 64 * h : 64 * h + 64, :],
                axis=0,
                keepdims=True,
            )
            for h in range(heads)
        ]
        logs = [lse_ref[index, h : h + 1, :] for h in range(heads)]
        acc_ref[...] = jnp.zeros_like(acc_ref)

        def key_step(key_block, first_row, last_row):
            ids = spread(key_ref[key_block], rows)
            for h in range(heads):
                span = slice(64 * h, 64 * h + 64)
                scores = dot_nt(k_ref[key_block, :, span], queries[h])
                scores = masked_scores(scores, ids, first_row, last_row)
                weights = jnp.exp(scores - logs[h])
                slopes = dot_nt(v_ref[key_block, :, span], grads[h])
                dscores = (weights * (slopes - deltas[h])).astype(BF16)
                dv_ref[h, key_block] += dot_nn(weights.astype(BF16), grads[h])
                dk_ref[h, key_block] += dot_nn(dscores, queries[h])
                acc_ref[span, :] += dot_nn(kt_ref[key_block, span, :], dscores)

        own = 2 * index + core
        far_row = far_ref[index]

        def far_step(key_block, state):
            key_step(key_block, far_row, None)
            return state

        lax.fori_loop(0, own, far_step, 0)
        key_step(own, low_ref[index], high_ref[index])
        for h in range(heads):
            span = slice(64 * h, 64 * h + 64)
            dq_ref[index, :, span] = (acc_ref[span, :] * 0.125).T.astype(BF16)
        return unused

    lax.fori_loop(0, blocks, query_block, 0)

    def write_block(index, unused):
        mine = 2 * index + core
        theirs = 2 * index + 1 - core
        for h in range(heads):
            left = slice(64 * h, 64 * h + 64)
            right = slice(width + 64 * h, width + 64 * h + 64)
            keep_ref[index, :, left] = dk_ref[h, mine]
            keep_ref[index, :, right] = dv_ref[h, mine]
            send_ref[index, :, left] = dk_ref[h, theirs].astype(BF16)
            send_ref[index, :, right] = dv_ref[h, theirs].astype(BF16)
        return unused

    lax.fori_loop(0, blocks, write_block, 0)


def kernel_call(kernel, outputs, scratch, operands, cost, special={}, after=()):
    whole = pl.BlockSpec(memory_space=pltpu.VMEM)
    in_specs = [pl.BlockSpec(memory_space=pltpu.SMEM)]
    in_specs += [special.get(n, whole) for n in range(1, len(operands))]
    in_specs += [pl.BlockSpec(memory_space=pl.ANY) for unused in after]
    count = len(operands)

    def ordered(*refs):
        return kernel(*refs[:count], *refs[count + len(after) :])

    moved = sum(v.size * v.dtype.itemsize for v in list(operands) + list(outputs))
    return pl.pallas_call(
        ordered,
        out_shape=outputs,
        in_specs=in_specs,
        out_specs=[pl.BlockSpec(memory_space=pltpu.VMEM) for unused in outputs],
        scratch_shapes=scratch,
        compiler_params=pltpu.CompilerParams(vmem_limit_bytes=56 * 1024 * 1024),
        cost_estimate=pl.CostEstimate(
            flops=cost * 1153 * 10**6, bytes_accessed=moved, transcendentals=0
        ),
    )(*operands, *after)


def pack_kernel(where, dq_ref, keep_ref, arrived_ref, p0, p1, p2, p3):
    chip = where[2]
    width = dq_ref.shape[2]
    for s, ref in enumerate((p0, p1, p2, p3)):
        owner = chip ^ s
        ref[:, 0:width] = dq_ref[owner]
        ref[:, width:] = (keep_ref[owner] + arrived_ref[owner].astype(FP32)).astype(BF16)


def middle_kernel(
    where,
    a0_ref,
    a1_ref,
    a2_ref,
    a3_ref,
    tokens_ref,
    cotangent_ref,
    live_ref,
    bias_out_ref,
    gain_ref,
    shift_ref,
    bias_fc_ref,
    bias_proj_ref,
    bundle_own,
    bundle_other,
    block_ref,
    dx_ref,
    d0_ref,
    d1_ref,
    d2_ref,
    d3_ref,
    mine_ref,
    send_ref,
    sums_ref,
    wo_ref,
    wf_ref,
    wp_ref,
    g_ref,
    dz_ref,
    sems,
):
    rows, features = tokens_ref.shape
    parts = wf_ref.shape[0]
    shard, hidden_width = features // parts, wp_ref.shape[0]
    columns = hidden_width // parts
    half, half_columns = shard // 2, columns // 2
    core, chip = where[1], where[2]

    starts = {"proj": [], "out": [], "fc": []}

    def fetch(kind, source, target):
        number = sum(len(v) for v in starts.values())
        starts[kind].append(pltpu.make_async_copy(source, target, sems.at[number]))

    def rows_at(owner, which, size):
        return pl.ds(pl.multiple_of(owner * 2 * size + which * size, 16), size)

    pieces = []
    for owner in range(parts):
        pieces.append((bundle_own.at[owner], owner, core))
        pieces.append((bundle_other.at[owner], owner, 1 - core))
    for piece, owner, which in pieces:
        fetch("out", piece.at[half_columns : half_columns + half, :], wo_ref.at[rows_at(owner, which, half), :])
    for piece, owner, which in pieces:
        for j in range(parts):
            first = half_columns + half * (j + 1)
            fetch("fc", piece.at[first : first + half, :], wf_ref.at[j, rows_at(owner, which, half), :])
    for piece, owner, which in pieces:
        fetch("proj", piece.at[0:half_columns, :], wp_ref.at[rows_at(owner, which, half_columns), :])
    for kind in ("out", "fc", "proj"):
        for copy in starts[kind]:
            copy.start()
    for copy in starts["out"]:
        copy.wait()

    attended = [a0_ref, a1_ref, a2_ref, a3_ref]
    middle = tokens_ref[...].astype(FP32) + bias_out_ref[...]
    a_start = 2 * parts * half_columns + features
    for s in range(parts):
        span = pl.ds(pl.multiple_of((chip ^ s) * shard, 16), shard)
        middle = middle + dot_nn(attended[s][...], wo_ref[span, :])
        mine_ref[:, a_start + shard * s : a_start + shard * (s + 1)] = attended[s][...]
        send_ref[:, a_start + shard * s : a_start + shard * (s + 1)] = attended[s][...]
    normed, unit, inverse = layer_norm(middle, gain_ref[...], shift_ref[...])
    normed_low = normed.astype(BF16)
    h_start = 2 * parts * half_columns
    mine_ref[:, h_start : h_start + features] = normed_low
    send_ref[:, h_start : h_start + features] = normed_low
    grad_out = cotangent_ref[...].astype(FP32) * live_ref[...]
    grad_out_low = grad_out.astype(BF16)
    y_start = a_start + features
    mine_ref[:, y_start : y_start + features] = grad_out_low
    send_ref[:, y_start : y_start + features] = grad_out_low
    for copy in starts["fc"] + starts["proj"]:
        copy.wait()

    sums_ref[...] = jnp.zeros_like(sums_ref)
    output = middle + bias_proj_ref[...]
    grad_normed = jnp.zeros((rows, features), FP32)
    scale, cubic = 0.7978845608028654, 0.044715
    for j in range(parts):
        span = slice(columns * j, columns * (j + 1))
        hidden = dot_nn(normed_low, wf_ref[j]) + bias_fc_ref[:, span]
        square = hidden * hidden
        bent = jnp.tanh(scale * hidden * (1.0 + cubic * square))
        active = 0.5 * hidden * (1.0 + bent)
        slope = 0.5 * (1.0 + bent) + 0.5 * hidden * (1.0 - bent * bent) * (
            scale * (1.0 + 3.0 * cubic * square)
        )
        g_ref[...] = active.astype(BF16)
        grad_hidden = (dot_nt(grad_out_low, wp_ref[span, :]) * slope).astype(BF16)
        output = output + dot_nn(g_ref[...], wp_ref[span, :])
        grad_normed = grad_normed + dot_nt(grad_hidden, wf_ref[j])
        sums_ref[j, 1:2, :] = jnp.sum(grad_hidden.astype(FP32), axis=0, keepdims=True)
        g_span = slice(half_columns * j, half_columns * (j + 1))
        mine_ref[:, g_span] = g_ref[:, pl.ds(pl.multiple_of(core * half_columns, 128), half_columns)]
        send_ref[:, g_span] = g_ref[
            :, pl.ds(pl.multiple_of((1 - core) * half_columns, 128), half_columns)
        ]
        first = parts * half_columns + columns * (j % 2)

        @pl.when(core == j // 2)
        def keep_hidden():
            mine_ref[:, first : first + columns] = grad_hidden

        @pl.when(core != j // 2)
        def give_hidden():
            send_ref[:, first : first + columns] = grad_hidden

    block_ref[...] = output.astype(BF16)
    inner, gain_sum, shift_sum = norm_back(grad_normed, unit, inverse, gain_ref[...])
    grad_middle = grad_out + inner
    dx_ref[...] = grad_middle
    dz_ref[...] = grad_middle.astype(BF16)
    z_start = y_start + features
    part_width = features // 2
    mine_ref[:, z_start : z_start + part_width] = dz_ref[
        :, pl.ds(pl.multiple_of(core * part_width, 128), part_width)
    ]
    send_ref[:, z_start : z_start + part_width] = dz_ref[
        :, pl.ds(pl.multiple_of((1 - core) * part_width, 128), part_width)
    ]
    for s, ref in enumerate((d0_ref, d1_ref, d2_ref, d3_ref)):
        span = pl.ds(pl.multiple_of((chip ^ s) * shard, 16), shard)
        ref[...] = dot_nt(dz_ref[...], wo_ref[span, :]).astype(BF16)
    rows_of_sums = (
        jnp.sum(dz_ref[...].astype(FP32), axis=0, keepdims=True),
        jnp.sum(grad_out, axis=0, keepdims=True),
        gain_sum[None, :],
        shift_sum[None, :],
    )
    for n, row in enumerate(rows_of_sums):
        for f in range(parts):
            sums_ref[f, 0:1, shard * n : shard * (n + 1)] = row[:, shard * f : shard * (f + 1)]


def weight_grad_kernel(where, mine_ref, other_ref, small_ref, keep_ref, send_ref, fc_ref):
    rows = mine_ref.shape[0]
    features = keep_ref.shape[2]
    part, core, chip = where[0], where[1], where[2]
    near, across = 1 + core, 2 - core
    parts = 4
    shard, half_columns = features // parts, features // 2
    h_start = 2 * parts * half_columns
    a_start = h_start + features
    y_start = a_start + features
    z_start = y_start + features

    def product(left, right):
        return contract_rows(mine_ref[:, left], mine_ref[:, right]) + contract_rows(
            other_ref[:, left], other_ref[:, right]
        )

    targets = [(keep_ref, 0, part), (keep_ref, 1, part ^ across)]
    targets += [(send_ref, 0, part ^ near), (send_ref, 1, part ^ 3)]
    fc_base = parts * half_columns
    for j in range(2):
        fc_ref[j] = product(
            pl.ds(h_start, features), pl.ds(fc_base + features * j, features)
        ).astype(BF16)
    out_base = half_columns + 2 * shard
    small_base = out_base + shard // 2
    for ref, slot, owner in targets:
        g_span = pl.ds(pl.multiple_of(owner * half_columns, 128), half_columns)
        ref[slot, 0:half_columns, :] = product(g_span, pl.ds(y_start, features)).astype(BF16)
        for j in range(2):
            first = half_columns + shard * j
            ref[slot, first : first + shard, :] = fc_ref[
                j, pl.ds(pl.multiple_of(owner * shard, 16), shard), :
            ]
        ref[slot, small_base : small_base + 16, :] = small_ref[owner].astype(BF16)
        ref[slot, small_base + 16 :, :] = jnp.zeros_like(ref[slot, small_base + 16 :, :])
    for s in range(parts):
        block = product(
            pl.ds(a_start + shard * s, shard), pl.ds(z_start, half_columns)
        ).astype(BF16)
        owner = chip ^ s
        for ref, slot, wanted in targets:

            @pl.when(owner == wanted)
            def store_block():
                ref[slot, out_base:small_base, 0:half_columns] = block[: shard // 2]
                ref[slot, out_base:small_base, half_columns:] = block[shard // 2 :]


def qkv_grad_kernel(
    where,
    normed_ref,
    p0,
    p1,
    p2,
    p3,
    wq_ref,
    wk_ref,
    wv_ref,
    gain_ref,
    shift_ref,
    keep_ref,
    send_ref,
    total_ref,
):
    blocks, rows, features = normed_ref.shape
    width = wq_ref.shape[1]
    part, core, chip = where[0], where[1], where[2]
    near, across = 1 + core, 2 - core
    parts = 4
    shard = features // parts
    half = shard // 2
    column_sums = [jnp.zeros((1, width), FP32) for n in range(3)]
    for n in range(3):
        total = jnp.zeros((features, width), FP32)
        for b in range(blocks):
            grads = (p0, p1, p2, p3)[b][:, width * n : width * (n + 1)]
            total = total + contract_rows(normed_ref[chip ^ b], grads)
            column_sums[n] = column_sums[n] + jnp.sum(grads.astype(FP32), axis=0, keepdims=True)
        total_ref[:, width * n : width * (n + 1)] = total
    sums = jnp.concatenate(column_sums, axis=1)
    shift_grad = jnp.zeros((features, 1), FP32)
    gain_grad = jnp.zeros((features, 1), FP32)
    for n, ref in enumerate((wq_ref, wk_ref, wv_ref)):
        wide = ref[...].astype(FP32)
        shift_grad = shift_grad + jnp.sum(wide * column_sums[n], axis=1, keepdims=True)
        gain_grad = gain_grad + jnp.sum(
            wide * total_ref[:, width * n : width * (n + 1)], axis=1, keepdims=True
        )
    gain_grad = (gain_grad - shift_ref[...] * shift_grad) / gain_ref[...]
    columns = jnp.concatenate(
        [gain_grad, shift_grad, jnp.zeros((features, 126), FP32)], axis=1
    )
    norm_rows = columns.T[0:8]
    order = [part, part ^ across, part ^ near, part ^ 3]
    other_order = [part, part ^ near, part ^ across, part ^ 3]
    for ref, which, owners in ((keep_ref, core, order), (send_ref, 1 - core, other_order)):
        for slot in range(parts):
            owner = owners[slot]
            first = pl.multiple_of(owner * shard + which * half, 16)
            ref[slot, 0:half, :] = total_ref[pl.ds(first, half), :].astype(ref.dtype)
            picked = jnp.zeros((8, shard), FP32)
            for f in range(parts):
                picked = jnp.where(owner == f, norm_rows[:, shard * f : shard * (f + 1)], picked)
            row = lax.broadcasted_iota(jnp.int32, (8, 3 * width), 0)
            packed = jnp.concatenate([picked, jnp.zeros((8, 3 * width - shard), FP32)], axis=1)
            tail = jnp.where(row < 2, packed, jnp.where(row == 2, sums, 0.0))
            tail = jnp.concatenate([tail, jnp.zeros_like(tail)], axis=0)
            ref[slot, half : half + 16, :] = tail.astype(ref.dtype)


def relay_kernel(where, keep_ref, theirs_ref, relay_ref):
    relay_ref[...] = (keep_ref[1].astype(FP32) + theirs_ref[1].astype(FP32)).astype(BF16)


def pair_kernel(where, keep_ref, theirs_ref, last_ref, stay_ref, give_ref):
    low = where[2] % 2
    count = stay_ref.shape[0]
    for ref, which in ((stay_ref, low), (give_ref, 1 - low)):
        span = pl.ds(pl.multiple_of(which * count, 16), count)
        total = keep_ref[0, span, :].astype(FP32) + theirs_ref[0, span, :].astype(FP32)
        ref[...] = (total + last_ref[span, :].astype(FP32)).astype(ref.dtype)


def quad_kernel(where, stay_ref, arrived_ref, keep_ref, give_ref):
    high = where[2] // 2
    count = keep_ref.shape[0]
    for ref, which in ((keep_ref, high), (give_ref, 1 - high)):
        span = pl.ds(pl.multiple_of(which * count, 16), count)
        total = stay_ref[span, :] + arrived_ref[span, :].astype(FP32)
        ref[...] = total.astype(ref.dtype)


def total_kernel(where, keep_ref, arrived_ref, out_ref):
    out_ref[...] = (keep_ref[...] + arrived_ref[...].astype(FP32)).astype(BF16)


def join_kernel(where, mine_ref, arrived_ref, out_ref):
    high = where[2] // 2
    count = mine_ref.shape[0]
    out_ref[pl.ds(pl.multiple_of(high * count, 16), count), :] = mine_ref[...]
    out_ref[pl.ds(pl.multiple_of((1 - high) * count, 16), count), :] = arrived_ref[...]


def input_grad_kernel(
    where, p0, p1, p2, p3, w_ref, tokens_ref, dx_ref, gain_ref, shift_ref, out_ref, packed_ref
):
    chip = where[2]
    features = w_ref.shape[0]
    width = p0.shape[1] // 3
    for z in range(4):
        for s, piece in enumerate((p0, p1, p2, p3)):

            @pl.when(chip == z ^ s)
            def place_piece():
                for n in range(3):
                    first = features * n + width * z
                    packed_ref[:, first : first + width] = piece[:, width * n : width * (n + 1)]

    total = dot_nt(packed_ref[...], w_ref[...])
    unit, inverse = layer_norm(tokens_ref[...].astype(FP32), gain_ref[...], shift_ref[...])[1:]
    out_ref[...] = dx_ref[...] + norm_back(total, unit, inverse, gain_ref[...])[0]


def output_kernel(
    where, m0, m1, t0, t1, proj_ref, fc_ref, out_ref, sums_ref, mine_ref, other_ref
):
    core, low = where[1], where[2] % 2
    count = m0.shape[0]
    for n, (mine, other) in enumerate(((m0, t0), (m1, t1))):
        span = pl.ds(pl.multiple_of((low if n == 0 else 1 - low) * count, 16), count)
        mine_ref[span, :] = mine[...]
        other_ref[span, :] = other[...]
    half_columns = proj_ref.shape[0] // 2
    shard, features = out_ref.shape
    out_rows = half_columns + 2 * shard
    small_at = out_rows + shard // 2
    sums_ref[...] = mine_ref[small_at : small_at + 16, :].astype(FP32) + other_ref[
        small_at : small_at + 16, :
    ].astype(FP32)

    def place(ref, which):
        proj_ref[which * half_columns : (which + 1) * half_columns, :] = ref[
            0:half_columns, :
        ].astype(FP32)
        for j in range(2):
            first = half_columns + shard * j
            column = features * (2 * which + j)
            fc_ref[:, column : column + features] = ref[first : first + shard, :].astype(FP32)
        span = slice(features // 2 * which, features // 2 * (which + 1))
        middle = out_rows + shard // 2
        out_ref[0 : shard // 2, span] = ref[out_rows:middle, 0 : features // 2].astype(FP32)
        out_ref[shard // 2 :, span] = ref[out_rows:middle, features // 2 :].astype(FP32)

    @pl.when(core == 0)
    def first_core():
        place(mine_ref, 0)
        place(other_ref, 1)

    @pl.when(core == 1)
    def second_core():
        place(mine_ref, 1)
        place(other_ref, 0)


def qkv_output_kernel(where, h0, h1, h2, h3, out_ref, extra_ref):
    core, chip = where[1], where[2]
    shard, wide = out_ref.shape
    features = wide // 3
    half = shard // 2
    width = h0.shape[2] // 3
    for s, ref in enumerate((h0, h1, h2, h3)):
        extra_ref[chip ^ s] = jnp.where(
            core == 0, ref[0, half : half + 16, :], ref[1, half : half + 16, :]
        ).astype(FP32)
        for z in range(4):

            @pl.when(chip == z ^ s)
            def place_piece():
                for n in range(3):
                    first = features * n + width * z
                    for slot, which in ((0, core), (1, 1 - core)):
                        rows = pl.ds(pl.multiple_of(which * half, 8), half)
                        out_ref[rows, first : first + width] = ref[
                            slot, 0:half, width * n : width * (n + 1)
                        ].astype(FP32)


def fast_body(
    tokens,
    cotangent,
    w_qkv,
    b_query,
    b_value,
    w_out,
    b_out,
    w_fc,
    b_fc,
    w_proj,
    b_proj,
    gain1,
    shift1,
    gain2,
    shift2,
    counts,
    seq_lengths,
):
    rows, features = tokens.shape
    ctx = lax.axis_size("ctx")
    fsdp = lax.axis_size("fsdp")
    chips = ctx // 2
    group_heads = HEADS // chips
    width = features // chips
    shard = features // fsdp
    hidden_width = w_fc.shape[1]
    columns = hidden_width // fsdp
    place = lax.axis_index("ctx")
    chip = place // 2
    core = place % 2
    part = lax.axis_index("fsdp")
    near = 1 + core
    across = 2 - core
    where = jnp.stack([part, core, chip]).astype(jnp.int32)

    def exchange(value, partner):
        pairs = [
            (f * ctx + c, g * ctx + d)
            for f in range(fsdp)
            for c in range(ctx)
            for g, d in [partner(f, c)]
        ]
        return lax.ppermute(value, ("fsdp", "ctx"), pairs)

    def to_near(value):
        return exchange(value, lambda f, c: (f ^ (1 + c % 2), c))

    def to_across(value):
        return exchange(value, lambda f, c: (f ^ (2 - c % 2), c))

    def to_core(value):
        return exchange(value, lambda f, c: (f, c ^ 1))

    def to_chip(value, step):
        return exchange(value, lambda f, c: (f, c ^ (2 * step)))

    def pick(array, index, axis=0):
        return lax.dynamic_index_in_dim(array, index, axis, keepdims=False)

    def place_all(shape, dtype, items):
        buffer = jnp.zeros(shape, dtype)
        for index, value in items:
            full = value.reshape((1,) * (len(shape) - value.ndim) + value.shape)
            starts = tuple(index) + (0,) * (len(shape) - len(index))
            buffer = lax.dynamic_update_slice(buffer, full.astype(dtype), starts)
        return buffer

    half = shard // 2
    fc_half = lax.dynamic_slice_in_dim(w_fc, core * half, half, 0)
    bundle = jnp.concatenate(
        [
            lax.dynamic_slice_in_dim(w_proj, core * (columns // 2), columns // 2, 0),
            lax.dynamic_slice_in_dim(w_out, core * half, half, 0),
        ]
        + [fc_half[:, columns * j : columns * (j + 1)] for j in range(fsdp)],
        axis=0,
    )

    blocks = [tokens] + [to_chip(tokens, s) for s in (1, 2, 3)]
    near_pair = to_core(jnp.stack(blocks[:2]))
    far_pair = to_core(jnp.stack(blocks[2:]))
    beside = [near_pair[0], near_pair[1], far_pair[0], far_pair[1]]
    bundles = lax.all_gather(bundle, "fsdp", axis=0)

    count_row = counts[0]
    offsets = jnp.cumsum(count_row) - count_row
    seq_ends = jnp.cumsum(seq_lengths[0])
    within = jnp.arange(rows, dtype=jnp.int32)
    slot = jnp.arange(ctx, dtype=jnp.int32)[:, None] * rows + within[None, :]
    live = within[None, :] < count_row[:, None]
    places = offsets[:, None] + within[None, :]
    starts = jnp.max(
        jnp.where(places[:, :, None] >= seq_ends[None, None, :], seq_ends[None, None, :], 0), axis=2
    )
    dead_id = -1 - slot
    key_ids = jnp.where(live, places, dead_id)
    lows = jnp.where(live, starts, dead_id)
    fars = jnp.where(live, starts, NEVER)
    key_tile = jnp.broadcast_to(key_ids[:, :, None], (ctx, rows, 128))

    def own_parity(array):
        return pick(array.reshape((chips, 2) + array.shape[1:]), core, 1)

    low_rows = own_parity(lows)[:, None, :]
    high_rows = own_parity(key_ids)[:, None, :]
    far_rows = own_parity(fars)[:, None, :]
    live_rows = (within < pick(count_row, place)).astype(FP32)[:, None]

    smalls = jnp.concatenate(
        [b_query, b_value, b_out, b_proj, gain1, shift1, gain2, shift2, b_fc]
    ).reshape(1, -1)
    mine = jnp.concatenate(
        [
            lax.dynamic_slice_in_dim(w_qkv, core * half, half, 0),
            jnp.pad(smalls, ((0, 15), (0, 0))),
        ],
        axis=0,
    )
    from_near, from_across = to_near(mine), to_across(mine)
    from_far = to_across(from_near)
    swapped = to_core(jnp.stack([from_near, from_across, from_far])[:, :half])
    qkv_full = place_all(
        (fsdp, 2, half, 3 * features),
        BF16,
        [
            ((part, 0), w_qkv.reshape(2, half, -1)),
            ((part ^ near, core), from_near[:half]),
            ((part ^ across, core), from_across[:half]),
            ((part ^ 3, core), from_far[:half]),
            ((part ^ across, 1 - core), swapped[0]),
            ((part ^ near, 1 - core), swapped[1]),
            ((part ^ 3, 1 - core), swapped[2]),
        ],
    ).reshape(features, 3 * features)
    own_weights = tuple(
        lax.dynamic_slice(qkv_full, (0, features * n + width * chip), (features, width))
        for n in range(3)
    )
    small_all = place_all(
        (fsdp, smalls.shape[1]),
        BF16,
        [
            ((part,), smalls[0]),
            ((part ^ near,), from_near[half]),
            ((part ^ across,), from_across[half]),
            ((part ^ 3,), from_far[half]),
        ],
    ).astype(FP32)
    vectors = [small_all[:, n * shard : (n + 1) * shard].reshape(1, -1) for n in range(8)]
    bias_q, bias_v, bias_out, bias_proj, gain_one, shift_one, gain_two, shift_two = vectors
    bias_fc = small_all[:, 8 * shard :].reshape(1, -1)

    own_bias_q = lax.dynamic_slice_in_dim(bias_q, chip * width, width, 1)
    own_bias_v = lax.dynamic_slice_in_dim(bias_v, chip * width, width, 1)
    normal = own_weights + (own_bias_q, own_bias_v, gain_one, shift_one)
    half_stores = kernel_call(
        project_kernel,
        [
            jax.ShapeDtypeStruct((chips // 2, rows, width), BF16),
            jax.ShapeDtypeStruct((chips, rows, width), BF16),
            jax.ShapeDtypeStruct((chips, width, rows), BF16),
            jax.ShapeDtypeStruct((chips, rows, width), BF16),
            jax.ShapeDtypeStruct((chips, width, rows), BF16),
            jax.ShapeDtypeStruct((chips // 2, rows, features), BF16),
        ],
        [],
        (where, blocks[0], beside[0], blocks[1], beside[1]) + normal,
        5,
    )
    queries, keys, keys_t, values, normed_mine, *rest = kernel_call(
        attend_kernel,
        [
            jax.ShapeDtypeStruct((chips, rows, width), BF16),
            jax.ShapeDtypeStruct((ctx, rows, width), BF16),
            jax.ShapeDtypeStruct((ctx, width, rows), BF16),
            jax.ShapeDtypeStruct((ctx, rows, width), BF16),
            jax.ShapeDtypeStruct((chips, rows, features), BF16),
        ]
        + [jax.ShapeDtypeStruct((rows, width), BF16)] * 4
        + [
            jax.ShapeDtypeStruct((chips, width, rows), FP32),
            jax.ShapeDtypeStruct((chips, 8, rows), FP32),
            jax.ShapeDtypeStruct((16, 128), BF16),
        ],
        [
            pltpu.VMEM((ctx, width, rows), BF16),
            pltpu.VMEM((width, rows), FP32),
            pltpu.VMEM((chips, rows, width), BF16),
        ],
        (where, blocks[2], beside[2], blocks[3], beside[3])
        + normal
        + tuple(half_stores)
        + (key_tile, low_rows, high_rows, far_rows),
        30,
    )
    attended_t, logs, zeros = rest[4:]

    def swap_chips(pieces):
        return [pieces[0]] + [to_chip(pieces[s], s) for s in (1, 2, 3)]

    bundles = lax.dynamic_update_slice(bundles, (bundles[0, :16, :128] + zeros)[None], (0, 0, 0))
    bundles_other = to_core(bundles)
    attended = swap_chips(rest[:4])
    bundle_width = 2 * hidden_width // 2 + 3 * features + features // 2
    hbm = pl.BlockSpec(memory_space=pl.ANY)
    block_out, grad_middle, d0, d1, d2, d3, bundle_mine, bundle_send, small_rows = kernel_call(
        middle_kernel,
        [
            jax.ShapeDtypeStruct((rows, features), BF16),
            jax.ShapeDtypeStruct((rows, features), FP32),
        ]
        + [jax.ShapeDtypeStruct((rows, width), BF16)] * 4
        + [
            jax.ShapeDtypeStruct((rows, bundle_width), BF16),
            jax.ShapeDtypeStruct((rows, bundle_width), BF16),
            jax.ShapeDtypeStruct((fsdp, 16, features), FP32),
        ],
        [
            pltpu.VMEM((features, features), BF16),
            pltpu.VMEM((fsdp, features, columns), BF16),
            pltpu.VMEM((hidden_width, features), BF16),
            pltpu.VMEM((rows, columns), BF16),
            pltpu.VMEM((rows, features), BF16),
            pltpu.SemaphoreType.DMA((8 * 6,)),
        ],
        tuple([where] + attended)
        + (
            tokens,
            cotangent,
            live_rows,
            bias_out,
            gain_two,
            shift_two,
            bias_fc,
            bias_proj,
            bundles,
            bundles_other,
        ),
        21,
        special={13: hbm, 14: hbm},
    )

    grad_blocks = swap_chips([d0, d1, d2, d3])

    bundle_other = to_core(bundle_send)
    out_rows = columns // 2 + 2 * shard
    small_at = out_rows + half
    block_rows = small_at + 32
    pair_shape = jax.ShapeDtypeStruct((2, block_rows, features), BF16)
    grads_keep, grads_send = kernel_call(
        weight_grad_kernel,
        [pair_shape, pair_shape],
        [pltpu.VMEM((2, features, features), BF16)],
        (where, bundle_mine, bundle_other, small_rows),
        14,
        after=(grad_blocks[1],),
    )

    grad_query, grad_keep, grad_send = kernel_call(
        attend_back_kernel,
        [
            jax.ShapeDtypeStruct((chips, rows, width), BF16),
            jax.ShapeDtypeStruct((chips, rows, 2 * width), FP32),
            jax.ShapeDtypeStruct((chips, rows, 2 * width), BF16),
        ],
        [
            pltpu.VMEM((width, rows), FP32),
            pltpu.VMEM((group_heads, ctx, rows, 64), FP32),
            pltpu.VMEM((group_heads, ctx, rows, 64), FP32),
            pltpu.VMEM((chips, rows, width), BF16),
        ],
        (
            where,
            queries,
            keys,
            keys_t,
            values,
            *grad_blocks,
            key_tile,
            low_rows,
            high_rows,
            far_rows,
            attended_t,
            logs,
        ),
        30,
    )
    packed = kernel_call(
        pack_kernel,
        [jax.ShapeDtypeStruct((rows, 3 * width), BF16)] * 4,
        [],
        (where, grad_query, grad_keep, to_core(grad_send)),
        2,
    )

    arrived = swap_chips(packed)
    (grad_tokens,) = kernel_call(
        input_grad_kernel,
        [jax.ShapeDtypeStruct((rows, features), FP32)],
        [pltpu.VMEM((rows, 3 * features), BF16)],
        tuple([where] + arrived) + (qkv_full, tokens, grad_middle, gain_one, shift_one),
        5,
    )

    def add_up(left_side, right_side):
        return left_side.astype(FP32) + right_side.astype(FP32)

    def scatter_parts(keep, send):
        theirs = to_near(send)
        last = to_across(add_up(keep[1], theirs[1]).astype(BF16))
        return (add_up(keep[0], theirs[0]) + last.astype(FP32)).astype(BF16)

    theirs = to_near(grads_send)
    block = jax.ShapeDtypeStruct((block_rows, features), BF16)

    def shaped(count, dtype):
        return jax.ShapeDtypeStruct((count, features), dtype)

    (relay,) = kernel_call(
        relay_kernel, [block], [], (where, grads_keep, theirs), 1, after=(grad_query,)
    )
    stay, give = kernel_call(
        pair_kernel,
        [shaped(block_rows // 2, FP32), shaped(block_rows // 2, BF16)],
        [],
        (where, grads_keep, theirs, to_across(relay)),
        2,
    )
    stay, give = kernel_call(
        quad_kernel,
        [shaped(block_rows // 4, FP32), shaped(block_rows // 4, BF16)],
        [],
        (where, stay, to_chip(give, 1)),
        2,
    )
    (quad,) = kernel_call(
        total_kernel, [shaped(block_rows // 4, BF16)], [], (where, stay, to_chip(give, 2)), 1
    )
    (joined,) = kernel_call(
        join_kernel, [shaped(block_rows // 2, BF16)], [], (where, quad, to_chip(quad, 2)), 1
    )
    joined_next = to_chip(joined, 1)
    d_proj, d_fc, d_out, small_sums = kernel_call(
        output_kernel,
        [
            jax.ShapeDtypeStruct((columns, features), FP32),
            jax.ShapeDtypeStruct((shard, hidden_width), FP32),
            jax.ShapeDtypeStruct((shard, features), FP32),
            jax.ShapeDtypeStruct((16, features), FP32),
        ],
        [pltpu.VMEM((block_rows, features), BF16), pltpu.VMEM((block_rows, features), BF16)],
        (where, joined, joined_next, to_core(joined), to_core(joined_next)),
        2,
    )
    d_bias_out, d_bias_proj, d_gain_two, d_shift_two = (
        small_sums[0, n * shard : (n + 1) * shard] for n in range(4)
    )
    d_bias_fc = small_sums[1]

    block_shape = (fsdp, half + 16, 3 * width)
    qkv_keep, qkv_send = kernel_call(
        qkv_grad_kernel,
        [jax.ShapeDtypeStruct(block_shape, FP32), jax.ShapeDtypeStruct(block_shape, BF16)],
        [pltpu.VMEM((features, 3 * width), FP32)],
        (
            where,
            normed_mine,
            *packed,
            *own_weights,
            gain_one.reshape(-1, 1),
            shift_one.reshape(-1, 1),
        ),
        8,
        after=tuple(arrived[1:]),
    )
    qkv_blocks = add_up(qkv_keep, to_core(qkv_send)).astype(BF16)
    qkv_half = scatter_parts(qkv_blocks[:2], qkv_blocks[2:])
    halves = swap_chips([jnp.stack([qkv_half, to_core(qkv_half)])] * 4)
    d_qkv, extra = kernel_call(
        qkv_output_kernel,
        [
            jax.ShapeDtypeStruct((shard, 3 * features), FP32),
            jax.ShapeDtypeStruct((chips, 16, 3 * width), FP32),
        ],
        [],
        tuple([where] + halves),
        2,
    )
    owner_extra = pick(extra, part)
    d_bias_q = owner_extra[2, :width]
    d_bias_v = owner_extra[2, 2 * width :]
    norm_total = jnp.sum(extra[:, :2, :shard], axis=0)
    d_gain_one = norm_total[0]
    d_shift_one = norm_total[1]

    return (
        block_out,
        grad_tokens,
        d_qkv,
        d_bias_q,
        d_bias_v,
        d_out,
        d_bias_out,
        d_fc,
        d_bias_fc,
        d_proj,
        d_bias_proj,
        d_gain_one,
        d_shift_one,
        d_gain_two,
        d_shift_two,
    )


def solution(mesh):
    in_specs = (
        P(("fsdp", "ctx"), None),
        P(("fsdp", "ctx"), None),
        P("fsdp", None),
        P("fsdp"),
        P("fsdp"),
        P("fsdp", None),
        P("fsdp"),
        P("fsdp", None),
        P("fsdp"),
        P("fsdp", None),
        P("fsdp"),
        P("fsdp"),
        P("fsdp"),
        P("fsdp"),
        P("fsdp"),
        P("fsdp", None),
        P("fsdp", None),
    )
    out_specs = (
        P(("fsdp", "ctx"), None),
        P(("fsdp", "ctx"), None),
        P("fsdp", None),
        P("fsdp"),
        P("fsdp"),
        P("fsdp", None),
        P("fsdp"),
        P("fsdp", None),
        P("fsdp"),
        P("fsdp", None),
        P("fsdp"),
        P("fsdp"),
        P("fsdp"),
        P("fsdp"),
        P("fsdp"),
    )
    ctx = mesh.shape["ctx"]
    four_by_four = mesh.shape["fsdp"] == 4 and ctx == 8 and HEADS % (ctx // 2) == 0
    body = fast_body if four_by_four else general_body
    return jax.shard_map(body, mesh=mesh, in_specs=in_specs, out_specs=out_specs, check_vma=False)
```

profile of v0, /device:TPU:0, one launch (start us, length us, event | category | flops | bytes accessed | tf_op | source)
XLA Modules:
  0.0 444.9 jit_solution(624493843421364397)
XLA Ops:
  7.3 6.2 %concatenate.9 = bf16[2304]{0:T(1024)(128)(2,1)S(1)} concatenate(bf16[192]{0:T(256)(128)(2,1)} %param.20, bf16[192]{0:T(256)(128)(2,1)} %param.21, bf16[192]{0:T(256)(128)(2,1)} %param.23, bf16[192]{0:T(256)(128)(2,1)} %param.27, bf16[192]{0:T(256)(128)(2,1)} %param.28, bf16[192]{0:T(256)(128)(2,1)} %param.29, bf16[192]{0:T(256)(128)(2,1)} %param.30, bf16[192]{0:T(256)(128)(2,1)} %param.31, ...), dimensions={0} | concatenate | bytes 9216 | tf_op jit(solution)/shard_map/concatenate | solution.py:1198
  15.4 2.9 collective-permute-start.3
  18.3 1.5 collective-permute-start.4
  19.8 1.6 collective-permute-start.7
  21.4 2.6 collective-permute-start
  37.4 1.4 slice.183
  38.8 1.4 dynamic_update_slice.44
  40.2 1.4 slice.184
  41.5 1.4 dynamic_update_slice.45
  42.9 3.4 collective-permute-done.7.refs_3_
  46.3 2.4 pad_maximum_fusion.3
  48.6 15.6 %collective-permute-done.refs_1_ = bf16[384,768]{1,0:T(8,128)(2,1)} collective-permute-done((bf16[384,768]{1,0:T(8,128)(2,1)}, bf16[384,768]{1,0:T(8,128)(2,1)}, u32[]{:S(2)}, u32[]{:S(2)}) %collective-permute-start) | collective-permute-done | bytes 589856 | tf_op jit(solution)/shard_map/ppermute | solution.py:1132
  64.2 2.4 pad_maximum_fusion.2
  66.6 2.4 pad_maximum_fusion
  69.5 1.4 slice.185
  70.9 1.4 dynamic_update_slice.46
  72.2 1.5 fusion.17
  73.7 1.4 reshape.282
  80.8 2.4 slice_bitcast_fusion
  83.2 2.3 slice_bitcast_fusion.2
  88.7 2.0 constant_dynamic-slice_fusion.7
  90.6 6.6 %shard_map.280 = (bf16[2,384,192]{2,1,0:T(8,128)(2,1)}, bf16[4,384,192]{2,1,0:T(8,128)(2,1)}, bf16[4,192,384]{2,1,0:T(8,128)(2,1)}, bf16[4,384,192]{2,1,0:T(8,12...) custom-call(s32[3]{0:T(128)} %pad_add_fusion.refs_0_, bf16[384,768]{1,0:T(8,128)(2,1)} %refs_6_.3, ...), custom_call_target="tpu_custom_call" | custom-call | flops 5765000192 | bytes 7085580 | tf_op jit(solution)/shard_map/pallas_call | solution.py:692
  97.2 1.7 broadcast_in_dim.24.refs_18_.refs_9_
  98.9 32.0 %shard_map.281 = (bf16[4,384,192]{2,1,0:T(8,128)(2,1)}, bf16[8,384,192]{2,1,0:T(8,128)(2,1)}, bf16[8,192,384]{2,1,0:T(8,128)(2,1)}, bf16[8,384,192]{2,1,0:T(8,12...) custom-call(s32[3]{0:T(128)} %pad_add_fusion.refs_0_, ...), custom_call_target="tpu_custom_call" | custom-call | flops 34589999104 | bytes 16987660 | tf_op jit(solution)/shard_map/pallas_call | solution.py:692
  132.2 5.2 %collective-permute-start.12 = (bf16[4,864,768]{2,1,0:T(8,128)(2,1)}, bf16[4,864,768]{2,1,0:T(8,128)(2,1)}, u32[]{:S(2)}, u32[]{:S(2)}) collective-permute-start(bf16[4,864,768]{2,1,0:T(8,128)(2,1)} %constant_dynamic-update-slice_fusion.refs_13_), channel_id=1, source_target_pairs={{0,1},{1,0},{2,3},{3,2},{4,5},{5,4},{6,7},{7,6},{8,9},{9,8},{10,11... | collective-permute-start | bytes 15925256 | tf_op jit(solution)/shard_map/ppermute | solution.py:1132
  139.3 12.3 %collective-permute-start.10 = (bf16[384,192]{1,0:T(8,128)(2,1)}, bf16[384,192]{1,0:T(8,128)(2,1)S(1)}, u32[]{:S(2)}, u32[]{:S(2)}) collective-permute-start(bf16[384,192]{1,0:T(8,128)(2,1)} %get-tuple-element.71), channel_id=1, source_target_pairs={{0,4},{1,5},{2,6},{3,7},{4,0},{5,1},{6,2},{7,3},{8,12},{9,13},{10,... | collective-permute-start | bytes 442376 | tf_op jit(solution)/shard_map/ppermute | solution.py:1132
  156.3 9.7 %collective-permute-done.10.refs_3_ = bf16[384,192]{1,0:T(8,128)(2,1)S(1)} collective-permute-done((bf16[384,192]{1,0:T(8,128)(2,1)}, bf16[384,192]{1,0:T(8,128)(2,1)S(1)}, u32[]{:S(2)}, u32[]{:S(2)}) %collective-permute-start.10) | collective-permute-done | bytes 147488 | tf_op jit(solution)/shard_map/ppermute | solution.py:1132
  167.4 21.7 %shard_map.282 = (bf16[384,768]{1,0:T(8,128)(2,1)}, f32[384,768]{1,0:T(8,128)}, bf16[384,192]{1,0:T(8,128)(2,1)}, bf16[384,192]{1,0:T(8,128)(2,1)}, bf16[384,192...) custom-call(s32[3]{0:T(128)} %pad_add_fusion.refs_0_, ...), custom_call_target="tpu_custom_call" | custom-call | flops 24213000192 | bytes 23815692 | tf_op jit(solution)/shard_map/pallas_call | solution.py:692
  189.2 3.6 collective-permute-start.13
  192.8 2.5 collective-permute-start.15
  195.2 6.2 %collective-permute-done.13.refs_6_.refs_4_ = bf16[384,192]{1,0:T(8,128)(2,1)S(1)} collective-permute-done((bf16[384,192]{1,0:T(8,128)(2,1)}, bf16[384,192]{1,0:T(8,128)(2,1)S(1)}, u32[]{:S(2)}, u32[]{:S(2)}) %collective-permute-start.13) | collective-permute-done | bytes 147488 | tf_op jit(solution)/shard_map/ppermute | solution.py:1132
  202.1 1.5 copy-done.17
  203.6 13.4 %shard_map.288 = (bf16[2,896,768]{2,1,0:T(8,128)(2,1)}, bf16[2,896,768]{2,1,0:T(8,128)(2,1)}) custom-call(s32[3]{0:T(128)} %pad_add_fusion.refs_0_, bf16[384,5760]{1,0:T(8,128)(2,1)} %get-tuple-element.98.refs_1_, bf16[384,5760]{1,0:T(8,128)(2,1)} %copy-done.17, f32[4,16,768]{2,1,0:T(8,128)} %get-tuple-element.100.refs_3_, bf16[384,192]{1,0:T(8,128)(2,1)} %copy-done.34), custom_call_target="tpu_custom_call" | custom-call | flops 16142000128 | bytes 14549004 | tf_op jit(solution)/shard_map/pallas_call | solution.py:692
  218.3 30.3 %shard_map.283 = (bf16[4,384,192]{2,1,0:T(8,128)(2,1)}, f32[4,384,384]{2,1,0:T(8,128)}, bf16[4,384,384]{2,1,0:T(8,128)(2,1)}) custom-call(s32[3]{0:T(128)} %pad_add_fusion.refs_0_, bf16[4,384,192]{2,1,0:T(8,128)(2,1)} %get-tuple-element.75.refs_1_, bf16[8,384,192]{2,1,0:T(8,128)(2,1)} %get-tuple-element.76.refs_2_, ...), custom_call_target="tpu_custom_call" | custom-call | flops 34589999104 | bytes 11667468 | tf_op jit(solution)/shard_map/pallas_call | solution.py:692
  248.5 4.8 %collective-permute-start.16 = (bf16[4,384,384]{2,1,0:T(8,128)(2,1)}, bf16[4,384,384]{2,1,0:T(8,128)(2,1)S(1)}, u32[]{:S(2)}, u32[]{:S(2)}) collective-permute-start(bf16[4,384,384]{2,1,0:T(8,128)(2,1)} %get-tuple-element.87), channel_id=1, source_target_pairs={{0,1},{1,0},{2,3},{3,2},{4,5},{5,4},{6,7},{7,6},{8,9},{9,8},{10,11... | collective-permute-start | bytes 3538952 | tf_op jit(solution)/shard_map/ppermute | solution.py:1132
  253.4 1.5 copy-done.2
  254.9 4.0 shard_map.289
  258.9 1.5 collective-permute-start.29
  261.4 3.8 shard_map.284
  265.3 2.7 collective-permute-start.18
  268.0 1.7 collective-permute-start.19
  271.7 15.0 %collective-permute-done.17.refs_2_.refs_11_ = bf16[384,576]{1,0:T(8,128)(2,1)S(1)} collective-permute-done((bf16[384,576]{1,0:T(8,128)(2,1)}, bf16[384,576]{1,0:T(8,128)(2,1)S(1)}, u32[]{:S(2)}, u32[]{:S(2)}) %collective-permute-start.17) | collective-permute-done | bytes 442400 | tf_op jit(solution)/shard_map/ppermute | solution.py:1132
  286.7 14.9 %collective-permute-done.18.refs_3_.refs_12_ = bf16[384,576]{1,0:T(8,128)(2,1)S(1)} collective-permute-done((bf16[384,576]{1,0:T(8,128)(2,1)}, bf16[384,576]{1,0:T(8,128)(2,1)S(1)}, u32[]{:S(2)}, u32[]{:S(2)}) %collective-permute-start.18) | collective-permute-done | bytes 442400 | tf_op jit(solution)/shard_map/ppermute | solution.py:1132
  302.6 8.8 %shard_map.286 = (f32[4,112,576]{2,1,0:T(8,128)}, bf16[4,112,576]{2,1,0:T(8,128)(2,1)}) custom-call(s32[3]{0:T(128)} %pad_add_fusion.refs_0_, bf16[4,384,768]{2,1,0:T(8,128)(2,1)} %get-tuple-element.93.refs_1_, bf16[384,576]{1,0:T(8,128)(2,1)} %get-tuple-element.88.refs_1_.refs_2_, bf16[384,576]{1,0:T(8,128)(2,1)} %get-tuple-element.89.refs_3_, ...), custom_call_target="tpu_custom_call" | custom-call | flops 9223999488 | bytes 6567948 | tf_op jit(solution)/shard_map/pallas_call | solution.py:692
  312.5 4.5 %shard_map.290 = (f32[448,768]{1,0:T(8,128)}, bf16[448,768]{1,0:T(8,128)(2,1)}) custom-call(s32[3]{0:T(128)} %pad_add_fusion.refs_0_, bf16[2,896,768]{2,1,0:T(8,128)(2,1)} %get-tuple-element.101.refs_1_, bf16[2,896,768]{2,1,0:T(8,128)(2,1)} %copy-done.2, bf16[896,768]{1,0:T(8,128)(2,1)} %copy-done.18), custom_call_target="tpu_custom_call" | custom-call | flops 2305999872 | bytes 8945676 | tf_op jit(solution)/shard_map/pallas_call | solution.py:692
  317.0 8.7 %collective-permute-start.30 = (bf16[448,768]{1,0:T(8,128)(2,1)}, bf16[448,768]{1,0:T(8,128)(2,1)S(1)}, u32[]{:S(2)}, u32[]{:S(2)}) collective-permute-start(bf16[448,768]{1,0:T(8,128)(2,1)} %get-tuple-element.104), channel_id=1, source_target_pairs={{0,2},{1,3},{2,0},{3,1},{4,6},{5,7},{6,4},{7,5},{8,10},{9,11},{10,... | collective-permute-start | bytes 2064392 | tf_op jit(solution)/shard_map/ppermute | solution.py:1132
  325.9 1.6 collective-permute-start.21
  327.4 14.6 %collective-permute-done.30.refs_2_ = bf16[448,768]{1,0:T(8,128)(2,1)S(1)} collective-permute-done((bf16[448,768]{1,0:T(8,128)(2,1)}, bf16[448,768]{1,0:T(8,128)(2,1)S(1)}, u32[]{:S(2)}, u32[]{:S(2)}) %collective-permute-start.30) | collective-permute-done | bytes 688160 | tf_op jit(solution)/shard_map/ppermute | solution.py:1132
  342.9 2.6 shard_map.291
  345.5 2.4 collective-permute-start.31
  347.9 1.6 collective-permute-start.22
  349.5 14.3 %collective-permute-done.31.refs_2_ = bf16[224,768]{1,0:T(8,128)(2,1)S(1)} collective-permute-done((bf16[224,768]{1,0:T(8,128)(2,1)}, bf16[224,768]{1,0:T(8,128)(2,1)S(1)}, u32[]{:S(2)}, u32[]{:S(2)}) %collective-permute-start.31) | collective-permute-done | bytes 344096 | tf_op jit(solution)/shard_map/ppermute | solution.py:1132
  364.6 2.0 shard_map.292.refs_1_
  366.7 16.9 %collective-permute-done.32.refs_2_ = bf16[224,768]{1,0:T(8,128)(2,1)S(1)} collective-permute-done((bf16[224,768]{1,0:T(8,128)(2,1)}, bf16[224,768]{1,0:T(8,128)(2,1)S(1)}, u32[]{:S(2)}, u32[]{:S(2)}) %collective-permute-start.32) | collective-permute-done | bytes 344096 | tf_op jit(solution)/shard_map/ppermute | solution.py:1132
  384.3 2.0 shard_map.293.refs_1_
  386.4 2.1 collective-permute-start.24
  388.8 2.1 collective-permute-start.26
  390.9 6.9 %shard_map.285 = f32[384,768]{1,0:T(8,128)} custom-call(s32[3]{0:T(128)} %pad_add_fusion.refs_0_, bf16[384,576]{1,0:T(8,128)(2,1)} %get-tuple-element.88.refs_1_.refs_2_, bf16[384,576]{1,0:T(8,128)(2,1)} %copy-done.25, bf16[384,576]{1,0:T(8,128)(2,1)} %copy-done.26, bf16[384,576]{1,0:T(8,128)(2,1)} %copy-done.27, bf16[768,2304]{1,0:T(8,128)(2,1)} %bitcast.89, ...), custom_call_target="tpu_custom_call" | custom-call | flops 5765000192 | bytes 8263692 | tf_op jit(solution)/shard_map/pallas_call | solution.py:692
  397.9 13.0 %collective-permute-done.33.refs_2_ = bf16[448,768]{1,0:T(8,128)(2,1)S(1)} collective-permute-done((bf16[448,768]{1,0:T(8,128)(2,1)}, bf16[448,768]{1,0:T(8,128)(2,1)S(1)}, u32[]{:S(2)}, u32[]{:S(2)}) %collective-permute-start.33) | collective-permute-done | bytes 688160 | tf_op jit(solution)/shard_map/ppermute | solution.py:1132
  411.0 5.8 %collective-permute-done.24.refs_2_ = bf16[2,112,576]{2,1,0:T(8,128)(2,1)S(1)} collective-permute-done((bf16[2,112,576]{2,1,0:T(8,128)(2,1)S(1)}, bf16[2,112,576]{2,1,0:T(8,128)(2,1)S(1)}, u32[]{:S(2)}, u32[]{:S(2)}) %collective-permute-start.24) | collective-permute-done | bytes 258080 | tf_op jit(solution)/shard_map/ppermute | solution.py:1132
  416.8 5.5 %collective-permute-done.26.refs_4_ = bf16[2,112,576]{2,1,0:T(8,128)(2,1)S(1)} collective-permute-done((bf16[2,112,576]{2,1,0:T(8,128)(2,1)S(1)}, bf16[2,112,576]{2,1,0:T(8,128)(2,1)S(1)}, u32[]{:S(2)}, u32[]{:S(2)}) %collective-permute-start.26) | collective-permute-done | bytes 258080 | tf_op jit(solution)/shard_map/ppermute | solution.py:1132
  423.0 3.0 shard_map.287
  430.4 4.6 %shard_map.294 = (f32[768,768]{1,0:T(8,128)}, f32[192,3072]{1,0:T(8,128)}, f32[192,768]{1,0:T(8,128)}, f32[16,768]{1,0:T(8,128)}) custom-call(s32[3]{0:T(128)} %pad_add_fusion.refs_0_, bf16[448,768]{1,0:T(8,128)(2,1)} %shard_map.293.refs_1_, bf16[448,768]{1,0:T(8,128)(2,1)} %copy-done.21, bf16[448,768]{1,0:T(8,128)(2,1)} %copy-done.22, ...), custom_call_target="tpu_custom_call" | custom-call | flops 2305999872 | bytes 8110092 | tf_op jit(solution)/shard_map/pallas_call | solution.py:692
  435.0 1.4 fusion.15
  (187 shorter events, 50.6 us)
Async XLA Ops:
  7.2 17.1 %copy-start.5 = (bf16[768,768]{1,0:T(8,128)(2,1)S(1)}, bf16[768,768]{1,0:T(8,128)(2,1)}, u32[]{:S(2)}) copy-start(bf16[768,768]{1,0:T(8,128)(2,1)} %param.26) | copy-start | bytes 3538948
  7.2 123.7 %all-gather.3.cloned.1.call-start = ((), (), s32[]{:S(2)}) async-start(), calls=%async_computation | async-start | bytes 6635520 | tf_op jit(solution)/shard_map/all_gather | solution.py:1172
  13.5 10.8 %copy-start.9 = (bf16[192,768]{1,0:T(8,128)(2,1)S(1)}, bf16[192,768]{1,0:T(8,128)(2,1)}, u32[]{:S(2)}) copy-start(bf16[192,768]{1,0:T(8,128)(2,1)} %param.22) | copy-start | bytes 884740
  15.4 19.2 %collective-permute-start.3 = (bf16[112,2304]{1,0:T(8,128)(2,1)}, bf16[112,2304]{1,0:T(8,128)(2,1)}, u32[]{:S(2)}, u32[]{:S(2)}) collective-permute-start(bf16[112,2304]{1,0:T(8,128)(2,1)} %fusion.1), channel_id=1, source_target_pairs={{0,8},{1,17},{2,10},{3,19},{4,12},{5,21},{6,14},{7,23},{8,0},{9,25... | collective-permute-start | bytes 1548296 | tf_op jit(solution)/shard_map/ppermute | solution.py:1132
  18.3 18.0 %collective-permute-start.4 = (bf16[112,2304]{1,0:T(8,128)(2,1)}, bf16[112,2304]{1,0:T(8,128)(2,1)}, u32[]{:S(2)}, u32[]{:S(2)}) collective-permute-start(bf16[112,2304]{1,0:T(8,128)(2,1)} %fusion.1), channel_id=1, source_target_pairs={{0,16},{1,9},{2,18},{3,11},{4,20},{5,13},{6,22},{7,15},{8,24},{9,1... | collective-permute-start | bytes 1548296 | tf_op jit(solution)/shard_map/ppermute | solution.py:1132
  19.8 26.4 %collective-permute-start.7 = (bf16[384,768]{1,0:T(8,128)(2,1)}, bf16[384,768]{1,0:T(8,128)(2,1)}, u32[]{:S(2)}, u32[]{:S(2)}) collective-permute-start(bf16[384,768]{1,0:T(8,128)(2,1)} %refs_6_.3), channel_id=1, source_target_pairs={{0,2},{1,3},{2,0},{3,1},{4,6},{5,7},{6,4},{7,5},{8,10},{9,11},{10,... | collective-permute-start | bytes 1769480 | tf_op jit(solution)/shard_map/ppermute | solution.py:1132
  21.4 42.8 %collective-permute-start = (bf16[384,768]{1,0:T(8,128)(2,1)}, bf16[384,768]{1,0:T(8,128)(2,1)}, u32[]{:S(2)}, u32[]{:S(2)}) collective-permute-start(bf16[384,768]{1,0:T(8,128)(2,1)} %refs_6_.3), channel_id=1, source_target_pairs={{0,4},{1,5},{2,6},{3,7},{4,0},{5,1},{6,2},{7,3},{8,12},{9,13},{10,... | collective-permute-start | bytes 1769480 | tf_op jit(solution)/shard_map/ppermute | solution.py:1132
  24.0 40.2 %collective-permute-start.1 = (bf16[384,768]{1,0:T(8,128)(2,1)}, bf16[384,768]{1,0:T(8,128)(2,1)}, u32[]{:S(2)}, u32[]{:S(2)}) collective-permute-start(bf16[384,768]{1,0:T(8,128)(2,1)} %refs_6_.3), channel_id=1, source_target_pairs={{0,6},{1,7},{2,4},{3,5},{4,2},{5,3},{6,0},{7,1},{8,14},{9,15},{10,... | collective-permute-start | bytes 1769480 | tf_op jit(solution)/shard_map/ppermute | solution.py:1132
  24.3 4.8 %copy-start.15 = (s32[1,8]{1,0:T(1,128)S(1)}, s32[1,8]{1,0:T(1,128)}, u32[]{:S(2)}) copy-start(s32[1,8]{1,0:T(1,128)} %param.32) | copy-start | bytes 100
  24.3 7.2 %copy-start.39 = (s32[1,3]{1,0:T(1,128)S(1)}, s32[1,3]{1,0:T(1,128)}, u32[]{:S(2)}) copy-start(s32[1,3]{1,0:T(1,128)} %param.33) | copy-start | bytes 40
  28.1 1.1 copy-start.1
  33.4 1.2 copy-start.3
  34.6 31.9 %collective-permute-start.5 = (bf16[112,2304]{1,0:T(8,128)(2,1)}, bf16[112,2304]{1,0:T(8,128)(2,1)}, u32[]{:S(2)}, u32[]{:S(2)}) collective-permute-start(bf16[112,2304]{1,0:T(8,128)(2,1)} %collective-permute-done.3), channel_id=1, source_target_pairs={{0,16},{1,9},{2,18},{3,11},{4,20},{5,13},{6,22},{7,15},{8,24},{9,1... | collective-permute-start | bytes 1548296 | tf_op jit(solution)/shard_map/ppermute | solution.py:1132
  48.6 32.2 %collective-permute-start.8 = (bf16[2,384,768]{2,1,0:T(8,128)(2,1)}, bf16[2,384,768]{2,1,0:T(8,128)(2,1)}, u32[]{:S(2)}, u32[]{:S(2)}) collective-permute-start(bf16[2,384,768]{2,1,0:T(8,128)(2,1)} %pad_maximum_fusion.3), channel_id=1, source_target_pairs={{0,1},{1,0},{2,3},{3,2},{4,5},{5,4},{6,7},{7,6},{8,9},{9,8},{10,11... | collective-permute-start | bytes 3538952 | tf_op jit(solution)/shard_map/ppermute | solution.py:1132
  66.6 16.6 %collective-permute-start.2 = (bf16[2,384,768]{2,1,0:T(8,128)(2,1)}, bf16[2,384,768]{2,1,0:T(8,128)(2,1)}, u32[]{:S(2)}, u32[]{:S(2)}) collective-permute-start(bf16[2,384,768]{2,1,0:T(8,128)(2,1)} %pad_maximum_fusion.2), channel_id=1, source_target_pairs={{0,1},{1,0},{2,3},{3,2},{4,5},{5,4},{6,7},{7,6},{8,9},{9,8},{10,11... | collective-permute-start | bytes 3538952 | tf_op jit(solution)/shard_map/ppermute | solution.py:1132
  69.0 16.5 %collective-permute-start.6 = (bf16[3,96,2304]{2,1,0:T(8,128)(2,1)}, bf16[3,96,2304]{2,1,0:T(8,128)(2,1)}, u32[]{:S(2)}, u32[]{:S(2)}) collective-permute-start(bf16[3,96,2304]{2,1,0:T(8,128)(2,1)} %pad_maximum_fusion), channel_id=1, source_target_pairs={{0,1},{1,0},{2,3},{3,2},{4,5},{5,4},{6,7},{7,6},{8,9},{9,8},{10,11... | collective-permute-start | bytes 3981320 | tf_op jit(solution)/shard_map/ppermute | solution.py:1132
  88.7 8.6 %copy-start = (bf16[4,2,96,2304]{3,2,1,0:T(8,128)(2,1)}, bf16[4,2,96,2304]{3,2,1,0:T(8,128)(2,1)S(1)}, u32[]{:S(2)}) copy-start(bf16[4,2,96,2304]{3,2,1,0:T(8,128)(2,1)S(1)} %fusion.2) | copy-start | bytes 10616836
  98.9 38.5 %copy-start.16 = (s32[1,8]{1,0:T(1,128)S(1)}, s32[1,8]{1,0:T(1,128)}, u32[]{:S(2)}) copy-start(s32[1,8]{1,0:T(1,128)} %param.32) | copy-start | bytes 100
  98.9 40.4 %copy-start.8 = (bf16[4,2304]{1,0:T(4,128)(2,1)S(1)}, bf16[4,2304]{1,0:T(4,128)(2,1)}, u32[]{:S(2)}) copy-start(bf16[4,2304]{1,0:T(4,128)(2,1)} %dynamic_update_slice.46) | copy-start | bytes 55300
  98.9 54.7 %copy-start.14 = (f32[4,192]{1,0:T(4,128)S(1)}, f32[4,192]{1,0:T(4,128)}, u32[]{:S(2)}) copy-start(f32[4,192]{1,0:T(4,128)} %get-tuple-element.127) | copy-start | bytes 9220
  98.9 55.4 %copy-start.13 = (f32[4,192]{1,0:T(4,128)S(1)}, f32[4,192]{1,0:T(4,128)}, u32[]{:S(2)}) copy-start(f32[4,192]{1,0:T(4,128)} %get-tuple-element.126) | copy-start | bytes 9220
  98.9 56.0 %copy-start.12 = (f32[4,192]{1,0:T(4,128)S(1)}, f32[4,192]{1,0:T(4,128)}, u32[]{:S(2)}) copy-start(f32[4,192]{1,0:T(4,128)} %get-tuple-element.125) | copy-start | bytes 9220
  98.9 56.7 %copy-start.11 = (f32[4,192]{1,0:T(4,128)S(1)}, f32[4,192]{1,0:T(4,128)}, u32[]{:S(2)}) copy-start(f32[4,192]{1,0:T(4,128)} %get-tuple-element.124) | copy-start | bytes 9220
  132.2 34.5 %collective-permute-start.12 = (bf16[4,864,768]{2,1,0:T(8,128)(2,1)}, bf16[4,864,768]{2,1,0:T(8,128)(2,1)}, u32[]{:S(2)}, u32[]{:S(2)}) collective-permute-start(bf16[4,864,768]{2,1,0:T(8,128)(2,1)} %constant_dynamic-update-slice_fusion.refs_13_), channel_id=1, source_target_pairs={{0,1},{1,0},{2,3},{3,2},{4,5},{5,4},{6,7},{7,6},{8,9},{9,8},{10,11... | collective-permute-start | bytes 15925256 | tf_op jit(solution)/shard_map/ppermute | solution.py:1132
  139.3 26.7 %collective-permute-start.10 = (bf16[384,192]{1,0:T(8,128)(2,1)}, bf16[384,192]{1,0:T(8,128)(2,1)S(1)}, u32[]{:S(2)}, u32[]{:S(2)}) collective-permute-start(bf16[384,192]{1,0:T(8,128)(2,1)} %get-tuple-element.71), channel_id=1, source_target_pairs={{0,4},{1,5},{2,6},{3,7},{4,0},{5,1},{6,2},{7,3},{8,12},{9,13},{10,... | collective-permute-start | bytes 442376 | tf_op jit(solution)/shard_map/ppermute | solution.py:1132
  151.6 14.4 %collective-permute-start.11 = (bf16[384,192]{1,0:T(8,128)(2,1)}, bf16[384,192]{1,0:T(8,128)(2,1)S(1)}, u32[]{:S(2)}, u32[]{:S(2)}) collective-permute-start(bf16[384,192]{1,0:T(8,128)(2,1)} %get-tuple-element.72), channel_id=1, source_target_pairs={{0,6},{1,7},{2,4},{3,5},{4,2},{5,3},{6,0},{7,1},{8,14},{9,15},{10,... | collective-permute-start | bytes 442376 | tf_op jit(solution)/shard_map/ppermute | solution.py:1132
  153.0 13.7 %collective-permute-start.9 = (bf16[384,192]{1,0:T(8,128)(2,1)}, bf16[384,192]{1,0:T(8,128)(2,1)S(1)}, u32[]{:S(2)}, u32[]{:S(2)}) collective-permute-start(bf16[384,192]{1,0:T(8,128)(2,1)} %get-tuple-element.70), channel_id=1, source_target_pairs={{0,2},{1,3},{2,0},{3,1},{4,6},{5,7},{6,4},{7,5},{8,10},{9,11},{10,... | collective-permute-start | bytes 442376 | tf_op jit(solution)/shard_map/ppermute | solution.py:1132
  189.1 12.3 %collective-permute-start.27 = (bf16[384,5760]{1,0:T(8,128)(2,1)}, bf16[384,5760]{1,0:T(8,128)(2,1)S(1)}, u32[]{:S(2)}, u32[]{:S(2)}) collective-permute-start(bf16[384,5760]{1,0:T(8,128)(2,1)} %get-tuple-element.99), channel_id=1, source_target_pairs={{0,1},{1,0},{2,3},{3,2},{4,5},{5,4},{6,7},{7,6},{8,9},{9,8},{10,11... | collective-permute-start | bytes 13271048 | tf_op jit(solution)/shard_map/ppermute | solution.py:1132
  189.2 12.3 %collective-permute-start.13 = (bf16[384,192]{1,0:T(8,128)(2,1)}, bf16[384,192]{1,0:T(8,128)(2,1)S(1)}, u32[]{:S(2)}, u32[]{:S(2)}) collective-permute-start(bf16[384,192]{1,0:T(8,128)(2,1)} %get-tuple-element.80), channel_id=1, source_target_pairs={{0,2},{1,3},{2,0},{3,1},{4,6},{5,7},{6,4},{7,5},{8,10},{9,11},{10,... | collective-permute-start | bytes 442376 | tf_op jit(solution)/shard_map/ppermute | solution.py:1132
  192.7 24.8 %collective-permute-start.14 = (bf16[384,192]{1,0:T(8,128)(2,1)}, bf16[384,192]{1,0:T(8,128)(2,1)S(1)}, u32[]{:S(2)}, u32[]{:S(2)}) collective-permute-start(bf16[384,192]{1,0:T(8,128)(2,1)} %get-tuple-element.81), channel_id=1, source_target_pairs={{0,4},{1,5},{2,6},{3,7},{4,0},{5,1},{6,2},{7,3},{8,12},{9,13},{10,... | collective-permute-start | bytes 442376 | tf_op jit(solution)/shard_map/ppermute | solution.py:1132
  192.8 24.8 %collective-permute-start.15 = (bf16[384,192]{1,0:T(8,128)(2,1)}, bf16[384,192]{1,0:T(8,128)(2,1)S(1)}, u32[]{:S(2)}, u32[]{:S(2)}) collective-permute-start(bf16[384,192]{1,0:T(8,128)(2,1)} %get-tuple-element.82), channel_id=1, source_target_pairs={{0,6},{1,7},{2,4},{3,5},{4,2},{5,3},{6,0},{7,1},{8,14},{9,15},{10,... | collective-permute-start | bytes 442376 | tf_op jit(solution)/shard_map/ppermute | solution.py:1132
  201.4 2.1 copy-start.17
  217.0 36.4 %collective-permute-start.28 = (bf16[2,896,768]{2,1,0:T(8,128)(2,1)}, bf16[2,896,768]{2,1,0:T(8,128)(2,1)S(1)}, u32[]{:S(2)}, u32[]{:S(2)}) collective-permute-start(bf16[2,896,768]{2,1,0:T(8,128)(2,1)} %get-tuple-element.102), channel_id=1, source_target_pairs={{0,8},{1,17},{2,10},{3,19},{4,12},{5,21},{6,14},{7,23},{8,0},{9,25... | collective-permute-start | bytes 8257544 | tf_op jit(solution)/shard_map/ppermute | solution.py:1132
  248.5 11.9 %collective-permute-start.16 = (bf16[4,384,384]{2,1,0:T(8,128)(2,1)}, bf16[4,384,384]{2,1,0:T(8,128)(2,1)S(1)}, u32[]{:S(2)}, u32[]{:S(2)}) collective-permute-start(bf16[4,384,384]{2,1,0:T(8,128)(2,1)} %get-tuple-element.87), channel_id=1, source_target_pairs={{0,1},{1,0},{2,3},{3,2},{4,5},{5,4},{6,7},{7,6},{8,9},{9,8},{10,11... | collective-permute-start | bytes 3538952 | tf_op jit(solution)/shard_map/ppermute | solution.py:1132
  253.4 1.5 copy-start.2
  258.9 52.5 %collective-permute-start.29 = (bf16[896,768]{1,0:T(8,128)(2,1)}, bf16[896,768]{1,0:T(8,128)(2,1)S(1)}, u32[]{:S(2)}, u32[]{:S(2)}) collective-permute-start(bf16[896,768]{1,0:T(8,128)(2,1)} %shard_map.289), channel_id=1, source_target_pairs={{0,16},{1,9},{2,18},{3,11},{4,20},{5,13},{6,22},{7,15},{8,24},{9,1... | collective-permute-start | bytes 4128776 | tf_op jit(solution)/shard_map/ppermute | solution.py:1132
  260.4 1.0 copy-start.19
  261.4 8.2 %copy-start.10 = (f32[4,192]{1,0:T(4,128)S(1)}, f32[4,192]{1,0:T(4,128)}, u32[]{:S(2)}) copy-start(f32[4,192]{1,0:T(4,128)} %get-tuple-element.129) | copy-start | bytes 9220
  265.3 21.4 %collective-permute-start.17 = (bf16[384,576]{1,0:T(8,128)(2,1)}, bf16[384,576]{1,0:T(8,128)(2,1)S(1)}, u32[]{:S(2)}, u32[]{:S(2)}) collective-permute-start(bf16[384,576]{1,0:T(8,128)(2,1)} %get-tuple-element.89.refs_3_), channel_id=1, source_target_pairs={{0,2},{1,3},{2,0},{3,1},{4,6},{5,7},{6,4},{7,5},{8,10},{9,11},{10,... | collective-permute-start | bytes 1327112 | tf_op jit(solution)/shard_map/ppermute | solution.py:1132
  265.3 36.3 %collective-permute-start.18 = (bf16[384,576]{1,0:T(8,128)(2,1)}, bf16[384,576]{1,0:T(8,128)(2,1)S(1)}, u32[]{:S(2)}, u32[]{:S(2)}) collective-permute-start(bf16[384,576]{1,0:T(8,128)(2,1)} %get-tuple-element.90.refs_4_), channel_id=1, source_target_pairs={{0,4},{1,5},{2,6},{3,7},{4,0},{5,1},{6,2},{7,3},{8,12},{9,13},{10,... | collective-permute-start | bytes 1327112 | tf_op jit(solution)/shard_map/ppermute | solution.py:1132
  268.0 33.6 %collective-permute-start.19 = (bf16[384,576]{1,0:T(8,128)(2,1)}, bf16[384,576]{1,0:T(8,128)(2,1)S(1)}, u32[]{:S(2)}, u32[]{:S(2)}) collective-permute-start(bf16[384,576]{1,0:T(8,128)(2,1)} %get-tuple-element.91.refs_5_), channel_id=1, source_target_pairs={{0,6},{1,7},{2,4},{3,5},{4,2},{5,3},{6,0},{7,1},{8,14},{9,15},{10,... | collective-permute-start | bytes 1327112 | tf_op jit(solution)/shard_map/ppermute | solution.py:1132
  286.7 14.9 %copy-start.25 = (bf16[384,576]{1,0:T(8,128)(2,1)}, bf16[384,576]{1,0:T(8,128)(2,1)S(1)}, u32[]{:S(2)}) copy-start(bf16[384,576]{1,0:T(8,128)(2,1)S(1)} %collective-permute-done.17.refs_2_.refs_11_) | copy-start | bytes 1327108
  301.6 1.0 copy-start.27
  311.4 14.3 %copy-start.4 = (f32[4,112,576]{2,1,0:T(8,128)S(1)}, f32[4,112,576]{2,1,0:T(8,128)}, u32[]{:S(2)}) copy-start(f32[4,112,576]{2,1,0:T(8,128)} %get-tuple-element.94) | copy-start | bytes 3096580
  311.4 14.3 %collective-permute-start.20 = (bf16[4,112,576]{2,1,0:T(8,128)(2,1)}, bf16[4,112,576]{2,1,0:T(8,128)(2,1)S(1)}, u32[]{:S(2)}, u32[]{:S(2)}) collective-permute-start(bf16[4,112,576]{2,1,0:T(8,128)(2,1)} %get-tuple-element.95), channel_id=1, source_target_pairs={{0,1},{1,0},{2,3},{3,2},{4,5},{5,4},{6,7},{7,6},{8,9},{9,8},{10,11... | collective-permute-start | bytes 1548296 | tf_op jit(solution)/shard_map/ppermute | solution.py:1132
  311.4 1.1 copy-start.18
  317.0 25.0 %collective-permute-start.30 = (bf16[448,768]{1,0:T(8,128)(2,1)}, bf16[448,768]{1,0:T(8,128)(2,1)S(1)}, u32[]{:S(2)}, u32[]{:S(2)}) collective-permute-start(bf16[448,768]{1,0:T(8,128)(2,1)} %get-tuple-element.104), channel_id=1, source_target_pairs={{0,2},{1,3},{2,0},{3,1},{4,6},{5,7},{6,4},{7,5},{8,10},{9,11},{10,... | collective-permute-start | bytes 2064392 | tf_op jit(solution)/shard_map/ppermute | solution.py:1132
  325.9 22.0 %collective-permute-start.21 = (bf16[2,112,576]{2,1,0:T(8,128)(2,1)S(1)}, bf16[2,112,576]{2,1,0:T(8,128)(2,1)S(1)}, u32[]{:S(2)}, u32[]{:S(2)}) collective-permute-start(bf16[2,112,576]{2,1,0:T(8,128)(2,1)S(1)} %slice.199), channel_id=1, source_target_pairs={{0,8},{1,17},{2,10},{3,19},{4,12},{5,21},{6,14},{7,23},{8,0},{9,25... | collective-permute-start | bytes 774152 | tf_op jit(solution)/shard_map/ppermute | solution.py:1132
  345.5 18.4 %collective-permute-start.31 = (bf16[224,768]{1,0:T(8,128)(2,1)}, bf16[224,768]{1,0:T(8,128)(2,1)S(1)}, u32[]{:S(2)}, u32[]{:S(2)}) collective-permute-start(bf16[224,768]{1,0:T(8,128)(2,1)} %get-tuple-element.106), channel_id=1, source_target_pairs={{0,4},{1,5},{2,6},{3,7},{4,0},{5,1},{6,2},{7,3},{8,12},{9,13},{10,... | collective-permute-start | bytes 1032200 | tf_op jit(solution)/shard_map/ppermute | solution.py:1132
  347.9 18.6 %collective-permute-start.22 = (bf16[112,576]{1,0:T(8,128)(2,1)S(1)}, bf16[112,576]{1,0:T(8,128)(2,1)S(1)}, u32[]{:S(2)}, u32[]{:S(2)}) collective-permute-start(bf16[112,576]{1,0:T(8,128)(2,1)S(1)} %fusion.10), channel_id=1, source_target_pairs={{0,16},{1,9},{2,18},{3,11},{4,20},{5,13},{6,22},{7,15},{8,24},{9,1... | collective-permute-start | bytes 387080 | tf_op jit(solution)/shard_map/ppermute | solution.py:1132
  366.5 17.0 %collective-permute-start.32 = (bf16[224,768]{1,0:T(8,128)(2,1)}, bf16[224,768]{1,0:T(8,128)(2,1)S(1)}, u32[]{:S(2)}, u32[]{:S(2)}) collective-permute-start(bf16[224,768]{1,0:T(8,128)(2,1)} %shard_map.292.refs_1_), channel_id=1, source_target_pairs={{0,4},{1,5},{2,6},{3,7},{4,0},{5,1},{6,2},{7,3},{8,12},{9,13},{10,... | collective-permute-start | bytes 1032200 | tf_op jit(solution)/shard_map/ppermute | solution.py:1132
  366.6 19.7 %collective-permute-start.23 = (bf16[112,576]{1,0:T(8,128)(2,1)S(1)}, bf16[112,576]{1,0:T(8,128)(2,1)S(1)}, u32[]{:S(2)}, u32[]{:S(2)}) collective-permute-start(bf16[112,576]{1,0:T(8,128)(2,1)S(1)} %fusion.8), channel_id=1, source_target_pairs={{0,1},{1,0},{2,3},{3,2},{4,5},{5,4},{6,7},{7,6},{8,9},{9,8},{10,11... | collective-permute-start | bytes 387080 | tf_op jit(solution)/shard_map/ppermute | solution.py:1132
  386.3 24.6 %collective-permute-start.33 = (bf16[448,768]{1,0:T(8,128)(2,1)}, bf16[448,768]{1,0:T(8,128)(2,1)S(1)}, u32[]{:S(2)}, u32[]{:S(2)}) collective-permute-start(bf16[448,768]{1,0:T(8,128)(2,1)} %shard_map.293.refs_1_), channel_id=1, source_target_pairs={{0,2},{1,3},{2,0},{3,1},{4,6},{5,7},{6,4},{7,5},{8,10},{9,11},{10,... | collective-permute-start | bytes 2064392 | tf_op jit(solution)/shard_map/ppermute | solution.py:1132
  386.4 11.5 %copy-start.6 = (bf16[2,112,576]{2,1,0:T(8,128)(2,1)}, bf16[2,112,576]{2,1,0:T(8,128)(2,1)S(1)}, u32[]{:S(2)}) copy-start(bf16[2,112,576]{2,1,0:T(8,128)(2,1)S(1)} %pad_maximum_fusion.4.refs_1_) | copy-start | bytes 774148
  386.4 30.4 %collective-permute-start.24 = (bf16[2,112,576]{2,1,0:T(8,128)(2,1)S(1)}, bf16[2,112,576]{2,1,0:T(8,128)(2,1)S(1)}, u32[]{:S(2)}, u32[]{:S(2)}) collective-permute-start(bf16[2,112,576]{2,1,0:T(8,128)(2,1)S(1)} %pad_maximum_fusion.4.refs_1_), channel_id=1, source_target_pairs={{0,2},{1,3},{2,0},{3,1},{4,6},{5,7},{6,4},{7,5},{8,10},{9,11},{10,... | collective-permute-start | bytes 774152 | tf_op jit(solution)/shard_map/ppermute | solution.py:1132
  388.5 28.3 %collective-permute-start.25 = (bf16[2,112,576]{2,1,0:T(8,128)(2,1)S(1)}, bf16[2,112,576]{2,1,0:T(8,128)(2,1)S(1)}, u32[]{:S(2)}, u32[]{:S(2)}) collective-permute-start(bf16[2,112,576]{2,1,0:T(8,128)(2,1)S(1)} %pad_maximum_fusion.4.refs_1_), channel_id=1, source_target_pairs={{0,4},{1,5},{2,6},{3,7},{4,0},{5,1},{6,2},{7,3},{8,12},{9,13},{10,... | collective-permute-start | bytes 774152 | tf_op jit(solution)/shard_map/ppermute | solution.py:1132
  388.8 33.5 %collective-permute-start.26 = (bf16[2,112,576]{2,1,0:T(8,128)(2,1)S(1)}, bf16[2,112,576]{2,1,0:T(8,128)(2,1)S(1)}, u32[]{:S(2)}, u32[]{:S(2)}) collective-permute-start(bf16[2,112,576]{2,1,0:T(8,128)(2,1)S(1)} %pad_maximum_fusion.4.refs_1_), channel_id=1, source_target_pairs={{0,6},{1,7},{2,4},{3,5},{4,2},{5,3},{6,0},{7,1},{8,14},{9,15},{10,... | collective-permute-start | bytes 774152 | tf_op jit(solution)/shard_map/ppermute | solution.py:1132
  390.9 6.9 %copy-start.20 = (bf16[448,768]{1,0:T(8,128)(2,1)S(1)}, bf16[448,768]{1,0:T(8,128)(2,1)}, u32[]{:S(2)}) copy-start(bf16[448,768]{1,0:T(8,128)(2,1)} %shard_map.293.refs_1_) | copy-start | bytes 2064388
  397.8 30.9 %collective-permute-start.34 = (bf16[448,768]{1,0:T(8,128)(2,1)S(1)}, bf16[448,768]{1,0:T(8,128)(2,1)S(1)}, u32[]{:S(2)}, u32[]{:S(2)}) collective-permute-start(bf16[448,768]{1,0:T(8,128)(2,1)S(1)} %copy-done.20), channel_id=1, source_target_pairs={{0,1},{1,0},{2,3},{3,2},{4,5},{5,4},{6,7},{7,6},{8,9},{9,8},{10,11... | collective-permute-start | bytes 2064392 | tf_op jit(solution)/shard_map/ppermute | solution.py:1132
  410.9 15.1 %copy-start.21 = (bf16[448,768]{1,0:T(8,128)(2,1)}, bf16[448,768]{1,0:T(8,128)(2,1)S(1)}, u32[]{:S(2)}) copy-start(bf16[448,768]{1,0:T(8,128)(2,1)S(1)} %collective-permute-done.33.refs_2_) | copy-start | bytes 2064388
  410.9 17.8 %collective-permute-start.35 = (bf16[448,768]{1,0:T(8,128)(2,1)S(1)}, bf16[448,768]{1,0:T(8,128)(2,1)S(1)}, u32[]{:S(2)}, u32[]{:S(2)}) collective-permute-start(bf16[448,768]{1,0:T(8,128)(2,1)S(1)} %collective-permute-done.33.refs_2_), channel_id=1, source_target_pairs={{0,1},{1,0},{2,3},{3,2},{4,5},{5,4},{6,7},{7,6},{8,9},{9,8},{10,11... | collective-permute-start | bytes 2064392 | tf_op jit(solution)/shard_map/ppermute | solution.py:1132
  416.8 5.5 %copy-start.30 = (bf16[2,112,576]{2,1,0:T(8,128)(2,1)}, bf16[2,112,576]{2,1,0:T(8,128)(2,1)S(1)}, u32[]{:S(2)}) copy-start(bf16[2,112,576]{2,1,0:T(8,128)(2,1)S(1)} %collective-permute-done.24.refs_2_) | copy-start | bytes 774148
  416.8 5.5 %copy-start.31 = (bf16[2,112,576]{2,1,0:T(8,128)(2,1)}, bf16[2,112,576]{2,1,0:T(8,128)(2,1)S(1)}, u32[]{:S(2)}) copy-start(bf16[2,112,576]{2,1,0:T(8,128)(2,1)S(1)} %collective-permute-done.25.refs_3_) | copy-start | bytes 774148
  429.5 0.9 copy-start.23
  (13 other events, 9.4 us)
Sparse Core Ops, SparseCore 0:
  29.3 64.6 all-gather.2
where the time goes:
time: 452 us; the launch traced here: 445 us
  Pallas kernels  146 us (32%)
  waiting for transfers between devices  136 us (30%)
  local copies, waits for them, and re-layouts  68.2 us (15%)
  starting transfers between devices  65.1 us (14%)
  other arithmetic  14.9 us (3%)
  between operations  14.7 us (3%)
    pallas_call x15, Pallas kernels, kernel_call(): pl.pallas_call(ordered, out_shape=outputs, in_specs=in_specs, out_specs=[...  146 us
    ppermute x36, waiting for transfers between devices, exchange(): return lax.ppermute(value, ('fsdp', 'ctx'), pairs)  136 us
    ppermute x36, starting transfers between devices, exchange(): return lax.ppermute(value, ('fsdp', 'ctx'), pairs)  65.1 us
    unnamed x88, local copies, waits for them, and re-layouts  18.9 us
    dynamic_update_slice x11, local copies, waits for them, and re-layouts, place_all(): buffer = lax.dynamic_update_slice(buffer, full.astype(dtype), starts)  10.7 us
  transfers between devices with their start and end apart: 37, of which 13 were waited for; matrix products, arithmetic and copies ran while one was open for 13% of the time, Pallas kernels for 27%

commit v1 on v0

--- a/solution.py
+++ b/solution.py
@@ -450,31 +450,86 @@
     return jnp.where(permitted, scores, -jnp.inf)
 
 
+def whole_vector(small_ref, number):
+    parts = [small_ref[f, number : number + 1, :] for f in range(small_ref.shape[0])]
+    return jnp.concatenate(parts, axis=1)
+
+
 def project_block(
-    tokens_ref, wq_ref, wk_ref, wv_ref, bq_ref, bv_ref, gain_ref, shift_ref, stores, position, wanted
+    tokens_ref, wq_ref, wk_ref, wv_ref, small_ref, chip, stores, position, wanted
 ):
     q_ref, k_ref, kt_ref, v_ref, vt_ref, normed_ref = stores
-    normed = layer_norm(tokens_ref[...].astype(FP32), gain_ref[...], shift_ref[...])[0]
+    gain, shift = whole_vector(small_ref, 4), whole_vector(small_ref, 5)
+    normed = layer_norm(tokens_ref[...].astype(FP32), gain, shift)[0]
     normed = normed.astype(BF16)
     keys = dot_nn(normed, wk_ref[...])
-    values = dot_nn(normed, wv_ref[...]) + bv_ref[...]
+    values = dot_nn(normed, wv_ref[...]) + small_ref[chip, 1:2, :]
     k_ref[position] = keys.astype(BF16)
     v_ref[position] = values.astype(BF16)
     kt_ref[position] = keys.T.astype(BF16)
     vt_ref[position] = values.T.astype(BF16)
     if wanted:
-        queries = (dot_nn(normed, wq_ref[...]) + bq_ref[...]).astype(BF16)
+        queries = (dot_nn(normed, wq_ref[...]) + small_ref[chip, 0:1, :]).astype(BF16)
         q_ref[position // 2] = (queries.astype(FP32) * 0.125).astype(BF16)
         normed_ref[position // 2] = normed
 
 
-def project_kernel(where, t0, t1, t2, t3, wq, wk, wv, bq, bv, gain, shift, q, k, kt, v, vt, normed):
-    core, chip = where[1], where[2]
+def project_kernel(
+    where,
+    t0,
+    t1,
+    t2,
+    t3,
+    w_ref,
+    smalls_ref,
+    near_ref,
+    across_ref,
+    far_ref,
+    near_other,
+    across_other,
+    far_other,
+    q,
+    k,
+    kt,
+    v,
+    vt,
+    normed,
+    full_ref,
+    wq,
+    wk,
+    wv,
+    small_ref,
+):
+    part, core, chip = where[0], where[1], where[2]
+    near, across = 1 + core, 2 - core
+    shard, wide = w_ref.shape
+    features, half, width = wide // 3, shard // 2, wq.shape[1]
+    full_ref[pl.ds(pl.multiple_of(part * shard, 16), shard), :] = w_ref[...]
+    small_ref[part] = smalls_ref[...].astype(FP32)
+    for ref, owner in ((near_ref, part ^ near), (across_ref, part ^ across), (far_ref, part ^ 3)):
+        first = pl.multiple_of(owner * shard + core * half, 16)
+        full_ref[pl.ds(first, half), :] = ref[0:half, :]
+        small_ref[owner] = ref[half:, 0:width].astype(FP32)
+    for ref, owner in (
+        (near_other, part ^ across),
+        (across_other, part ^ near),
+        (far_other, part ^ 3),
+    ):
+        first = pl.multiple_of(owner * shard + (1 - core) * half, 16)
+        full_ref[pl.ds(first, half), :] = ref[0:half, :]
+    for z in range(features // width):
+
+        @pl.when(chip == z)
+        def own_columns():
+            for n, ref in enumerate((wq, wk, wv)):
+                first = features * n + width * z
+                ref[...] = full_ref[:, first : first + width]
+
     stores = (q, k, kt, v, vt, normed)
     for n, block in enumerate((t0, t1, t2, t3)):
         owner = (chip ^ (n // 2)) % 2
         position = 2 * owner + (core if n % 2 == 0 else 1 - core)
-        project_block(block, wq, wk, wv, bq, bv, gain, shift, stores, position, n % 2 == 0)
+        project_block(block, wq, wk, wv, small_ref, chip, stores, position, n % 2 == 0)
 
 
 def attend_kernel(
@@ -486,10 +541,7 @@
     wq_ref,
     wk_ref,
     wv_ref,
-    bq_ref,
-    bv_ref,
-    gain_ref,
-    shift_ref,
+    small_ref,
     q_half,
     k_half,
     kt_half,
@@ -530,10 +582,8 @@
             wq_ref,
             wk_ref,
             wv_ref,
-            bq_ref,
-            bv_ref,
-            gain_ref,
-            shift_ref,
+            small_ref,
+            chip,
             stores,
             position,
             n % 2 == 0,
@@ -720,11 +770,7 @@
     tokens_ref,
     cotangent_ref,
     live_ref,
-    bias_out_ref,
-    gain_ref,
-    shift_ref,
-    bias_fc_ref,
-    bias_proj_ref,
+    small_ref,
     bundle_own,
     bundle_other,
     block_ref,
@@ -778,14 +824,16 @@
         copy.wait()
 
     attended = [a0_ref, a1_ref, a2_ref, a3_ref]
-    middle = tokens_ref[...].astype(FP32) + bias_out_ref[...]
+    middle = tokens_ref[...].astype(FP32) + whole_vector(small_ref, 2)
     a_start = 2 * parts * half_columns + features
     for s in range(parts):
         span = pl.ds(pl.multiple_of((chip ^ s) * shard, 16), shard)
         middle = middle + dot_nn(attended[s][...], wo_ref[span, :])
         mine_ref[:, a_start + shard * s : a_start + shard * (s + 1)] = attended[s][...]
         send_ref[:, a_start + shard * s : a_start + shard * (s + 1)] = attended[s][...]
-    normed, unit, inverse = layer_norm(middle, gain_ref[...], shift_ref[...])
+    normed, unit, inverse = layer_norm(
+        middle, whole_vector(small_ref, 6), whole_vector(small_ref, 7)
+    )
     normed_low = normed.astype(BF16)
     h_start = 2 * parts * half_columns
     mine_ref[:, h_start : h_start + features] = normed_low
@@ -799,12 +847,13 @@
         copy.wait()
 
     sums_ref[...] = jnp.zeros_like(sums_ref)
-    output = middle + bias_proj_ref[...]
+    output = middle + whole_vector(small_ref, 3)
     grad_normed = jnp.zeros((rows, features), FP32)
     scale, cubic = 0.7978845608028654, 0.044715
     for j in range(parts):
         span = slice(columns * j, columns * (j + 1))
-        hidden = dot_nn(normed_low, wf_ref[j]) + bias_fc_ref[:, span]
+        bias_fc = jnp.concatenate([small_ref[j, 8 + n : 9 + n, :] for n in range(parts)], axis=1)
+        hidden = dot_nn(normed_low, wf_ref[j]) + bias_fc
         square = hidden * hidden
         bent = jnp.tanh(scale * hidden * (1.0 + cubic * square))
         active = 0.5 * hidden * (1.0 + bent)
@@ -832,7 +881,9 @@
             send_ref[:, first : first + columns] = grad_hidden
 
     block_ref[...] = output.astype(BF16)
-    inner, gain_sum, shift_sum = norm_back(grad_normed, unit, inverse, gain_ref[...])
+    inner, gain_sum, shift_sum = norm_back(
+        grad_normed, unit, inverse, whole_vector(small_ref, 6)
+    )
     grad_middle = grad_out + inner
     dx_ref[...] = grad_middle
     dz_ref[...] = grad_middle.astype(BF16)
@@ -917,8 +968,7 @@
     wq_ref,
     wk_ref,
     wv_ref,
-    gain_ref,
-    shift_ref,
+    small_ref,
     keep_ref,
     send_ref,
     total_ref,
@@ -947,11 +997,13 @@
         gain_grad = gain_grad + jnp.sum(
             wide * total_ref[:, width * n : width * (n + 1)], axis=1, keepdims=True
         )
-    gain_grad = (gain_grad - shift_ref[...] * shift_grad) / gain_ref[...]
     columns = jnp.concatenate(
         [gain_grad, shift_grad, jnp.zeros((features, 126), FP32)], axis=1
     )
     norm_rows = columns.T[0:8]
+    gain, shift = whole_vector(small_ref, 4), whole_vector(small_ref, 5)
+    gain_row = (norm_rows[0:1] - shift * norm_rows[1:2]) / gain
+    norm_rows = jnp.concatenate([gain_row, norm_rows[1:]], axis=0)
     order = [part, part ^ across, part ^ near, part ^ 3]
     other_order = [part, part ^ near, part ^ across, part ^ 3]
     for ref, which, owners in ((keep_ref, core, order), (send_ref, 1 - core, other_order)):
@@ -969,12 +1021,16 @@
             ref[slot, half : half + 16, :] = tail.astype(ref.dtype)
 
 
+def first_bit(core, chip):
+    return jnp.where(core == 0, chip % 2, chip // 2)
+
+
 def relay_kernel(where, keep_ref, theirs_ref, relay_ref):
     relay_ref[...] = (keep_ref[1].astype(FP32) + theirs_ref[1].astype(FP32)).astype(BF16)
 
 
 def pair_kernel(where, keep_ref, theirs_ref, last_ref, stay_ref, give_ref):
-    low = where[2] % 2
+    low = first_bit(where[1], where[2])
     count = stay_ref.shape[0]
     for ref, which in ((stay_ref, low), (give_ref, 1 - low)):
         span = pl.ds(pl.multiple_of(which * count, 16), count)
@@ -983,7 +1039,7 @@
 
 
 def quad_kernel(where, stay_ref, arrived_ref, keep_ref, give_ref):
-    high = where[2] // 2
+    high = first_bit(1 - where[1], where[2])
     count = keep_ref.shape[0]
     for ref, which in ((keep_ref, high), (give_ref, 1 - high)):
         span = pl.ds(pl.multiple_of(which * count, 16), count)
@@ -996,14 +1052,14 @@
 
 
 def join_kernel(where, mine_ref, arrived_ref, out_ref):
-    high = where[2] // 2
+    high = first_bit(1 - where[1], where[2])
     count = mine_ref.shape[0]
     out_ref[pl.ds(pl.multiple_of(high * count, 16), count), :] = mine_ref[...]
     out_ref[pl.ds(pl.multiple_of((1 - high) * count, 16), count), :] = arrived_ref[...]
 
 
 def input_grad_kernel(
-    where, p0, p1, p2, p3, w_ref, tokens_ref, dx_ref, gain_ref, shift_ref, out_ref, packed_ref
+    where, p0, p1, p2, p3, w_ref, tokens_ref, dx_ref, small_ref, out_ref, packed_ref
 ):
     chip = where[2]
     features = w_ref.shape[0]
@@ -1018,19 +1074,22 @@
                     packed_ref[:, first : first + width] = piece[:, width * n : width * (n + 1)]
 
     total = dot_nt(packed_ref[...], w_ref[...])
-    unit, inverse = layer_norm(tokens_ref[...].astype(FP32), gain_ref[...], shift_ref[...])[1:]
-    out_ref[...] = dx_ref[...] + norm_back(total, unit, inverse, gain_ref[...])[0]
+    unit, inverse = layer_norm(
+        tokens_ref[...].astype(FP32), whole_vector(small_ref, 4), whole_vector(small_ref, 5)
+    )[1:]
+    out_ref[...] = dx_ref[...] + norm_back(total, unit, inverse, whole_vector(small_ref, 4))[0]
 
 
 def output_kernel(
     where, m0, m1, t0, t1, proj_ref, fc_ref, out_ref, sums_ref, mine_ref, other_ref
 ):
-    core, low = where[1], where[2] % 2
+    core = where[1]
     count = m0.shape[0]
+    own_bit, other_bit = first_bit(core, where[2]), first_bit(1 - core, where[2])
     for n, (mine, other) in enumerate(((m0, t0), (m1, t1))):
-        span = pl.ds(pl.multiple_of((low if n == 0 else 1 - low) * count, 16), count)
-        mine_ref[span, :] = mine[...]
-        other_ref[span, :] = other[...]
+        for bit, source, target in ((own_bit, mine, mine_ref), (other_bit, other, other_ref)):
+            first = pl.multiple_of((bit if n == 0 else 1 - bit) * count, 16)
+            target[pl.ds(first, count), :] = source[...]
     half_columns = proj_ref.shape[0] // 2
     shard, features = out_ref.shape
     out_rows = half_columns + 2 * shard
@@ -1143,6 +1202,12 @@
     def to_chip(value, step):
         return exchange(value, lambda f, c: (f, c ^ (2 * step)))
 
+    def to_first(value):
+        return exchange(value, lambda f, c: (f, c ^ (2 + 2 * (c % 2))))
+
+    def to_second(value):
+        return exchange(value, lambda f, c: (f, c ^ (4 - 2 * (c % 2))))
+
     def pick(array, index, axis=0):
         return lax.dynamic_index_in_dim(array, index, axis, keepdims=False)
 
@@ -1166,9 +1231,7 @@
     )
 
     blocks = [tokens] + [to_chip(tokens, s) for s in (1, 2, 3)]
-    near_pair = to_core(jnp.stack(blocks[:2]))
-    far_pair = to_core(jnp.stack(blocks[2:]))
-    beside = [near_pair[0], near_pair[1], far_pair[0], far_pair[1]]
+    beside = [to_core(v) for v in blocks]
     bundles = lax.all_gather(bundle, "fsdp", axis=0)
 
     count_row = counts[0]
@@ -1195,54 +1258,24 @@
     far_rows = own_parity(fars)[:, None, :]
     live_rows = (within < pick(count_row, place)).astype(FP32)[:, None]
 
-    smalls = jnp.concatenate(
-        [b_query, b_value, b_out, b_proj, gain1, shift1, gain2, shift2, b_fc]
-    ).reshape(1, -1)
+    vectors = [b_query, b_value, b_out, b_proj, gain1, shift1, gain2, shift2]
+    vectors += [b_fc[shard * n : shard * (n + 1)] for n in range(fsdp)]
+    row = lax.broadcasted_iota(jnp.int32, (16, shard), 0)
+    smalls = jnp.zeros((16, shard), BF16)
+    for n, vector in enumerate(vectors):
+        smalls = jnp.where(row == n, vector[None, :], smalls)
     mine = jnp.concatenate(
         [
             lax.dynamic_slice_in_dim(w_qkv, core * half, half, 0),
-            jnp.pad(smalls, ((0, 15), (0, 0))),
+            jnp.pad(smalls, ((0, 0), (0, 3 * features - shard))),
         ],
         axis=0,
     )
     from_near, from_across = to_near(mine), to_across(mine)
     from_far = to_across(from_near)
-    swapped = to_core(jnp.stack([from_near, from_across, from_far])[:, :half])
-    qkv_full = place_all(
-        (fsdp, 2, half, 3 * features),
-        BF16,
-        [
-            ((part, 0), w_qkv.reshape(2, half, -1)),
-            ((part ^ near, core), from_near[:half]),
-            ((part ^ across, core), from_across[:half]),
-            ((part ^ 3, core), from_far[:half]),
-            ((part ^ across, 1 - core), swapped[0]),
-            ((part ^ near, 1 - core), swapped[1]),
-            ((part ^ 3, 1 - core), swapped[2]),
-        ],
-    ).reshape(features, 3 * features)
-    own_weights = tuple(
-        lax.dynamic_slice(qkv_full, (0, features * n + width * chip), (features, width))
-        for n in range(3)
-    )
-    small_all = place_all(
-        (fsdp, smalls.shape[1]),
-        BF16,
-        [
-            ((part,), smalls[0]),
-            ((part ^ near,), from_near[half]),
-            ((part ^ across,), from_across[half]),
-            ((part ^ 3,), from_far[half]),
-        ],
-    ).astype(FP32)
-    vectors = [small_all[:, n * shard : (n + 1) * shard].reshape(1, -1) for n in range(8)]
-    bias_q, bias_v, bias_out, bias_proj, gain_one, shift_one, gain_two, shift_two = vectors
-    bias_fc = small_all[:, 8 * shard :].reshape(1, -1)
-
-    own_bias_q = lax.dynamic_slice_in_dim(bias_q, chip * width, width, 1)
-    own_bias_v = lax.dynamic_slice_in_dim(bias_v, chip * width, width, 1)
-    normal = own_weights + (own_bias_q, own_bias_v, gain_one, shift_one)
-    half_stores = kernel_call(
+    gathered = (from_near, from_across, from_far)
+    gathered += tuple(to_core(v) for v in gathered)
+    *half_stores, qkv_full, weight_q, weight_k, weight_v, small_all = kernel_call(
         project_kernel,
         [
             jax.ShapeDtypeStruct((chips // 2, rows, width), BF16),
@@ -1251,10 +1284,15 @@
             jax.ShapeDtypeStruct((chips, rows, width), BF16),
             jax.ShapeDtypeStruct((chips, width, rows), BF16),
             jax.ShapeDtypeStruct((chips // 2, rows, features), BF16),
+            jax.ShapeDtypeStruct((features, 3 * features), BF16),
+            jax.ShapeDtypeStruct((features, width), BF16),
+            jax.ShapeDtypeStruct((features, width), BF16),
+            jax.ShapeDtypeStruct((features, width), BF16),
+            jax.ShapeDtypeStruct((fsdp, 16, width), FP32),
         ],
         [],
-        (where, blocks[0], beside[0], blocks[1], beside[1]) + normal,
-        5,
+        (where, blocks[0], beside[0], blocks[1], beside[1], w_qkv, smalls) + gathered,
+        9,
     )
     queries, keys, keys_t, values, normed_mine, *rest = kernel_call(
         attend_kernel,
@@ -1277,7 +1315,7 @@
             pltpu.VMEM((chips, rows, width), BF16),
         ],
         (where, blocks[2], beside[2], blocks[3], beside[3])
-        + normal
+        + (weight_q, weight_k, weight_v, small_all)
         + tuple(half_stores)
         + (key_tile, low_rows, high_rows, far_rows),
         30,
@@ -1317,16 +1355,12 @@
             tokens,
             cotangent,
             live_rows,
-            bias_out,
-            gain_two,
-            shift_two,
-            bias_fc,
-            bias_proj,
+            small_all,
             bundles,
             bundles_other,
         ),
         21,
-        special={13: hbm, 14: hbm},
+        special={9: hbm, 10: hbm},
     )
 
     grad_blocks = swap_chips([d0, d1, d2, d3])
@@ -1382,15 +1416,6 @@
         2,
     )
 
-    arrived = swap_chips(packed)
-    (grad_tokens,) = kernel_call(
-        input_grad_kernel,
-        [jax.ShapeDtypeStruct((rows, features), FP32)],
-        [pltpu.VMEM((rows, 3 * features), BF16)],
-        tuple([where] + arrived) + (qkv_full, tokens, grad_middle, gain_one, shift_one),
-        5,
-    )
-
     def add_up(left_side, right_side):
         return left_side.astype(FP32) + right_side.astype(FP32)
 
@@ -1399,6 +1424,7 @@
         last = to_across(add_up(keep[1], theirs[1]).astype(BF16))
         return (add_up(keep[0], theirs[0]) + last.astype(FP32)).astype(BF16)
 
+    arrived = swap_chips(packed)
     theirs = to_near(grads_send)
     block = jax.ShapeDtypeStruct((block_rows, features), BF16)
 
@@ -1406,7 +1432,7 @@
         return jax.ShapeDtypeStruct((count, features), dtype)
 
     (relay,) = kernel_call(
-        relay_kernel, [block], [], (where, grads_keep, theirs), 1, after=(grad_query,)
+        relay_kernel, [block], [], (where, grads_keep, theirs), 1, after=(packed[0],)
     )
     stay, give = kernel_call(
         pair_kernel,
@@ -1414,21 +1440,31 @@
         [],
         (where, grads_keep, theirs, to_across(relay)),
         2,
+        after=tuple(arrived[1:]),
     )
     stay, give = kernel_call(
         quad_kernel,
         [shaped(block_rows // 4, FP32), shaped(block_rows // 4, BF16)],
         [],
-        (where, stay, to_chip(give, 1)),
+        (where, stay, to_first(give)),
         2,
     )
+    (grad_tokens,) = kernel_call(
+        input_grad_kernel,
+        [jax.ShapeDtypeStruct((rows, features), FP32)],
+        [pltpu.VMEM((rows, 3 * features), BF16)],
+        tuple([where] + arrived) + (qkv_full, tokens, grad_middle, small_all),
+        5,
+        after=(give,),
+    )
+
     (quad,) = kernel_call(
-        total_kernel, [shaped(block_rows // 4, BF16)], [], (where, stay, to_chip(give, 2)), 1
+        total_kernel, [shaped(block_rows // 4, BF16)], [], (where, stay, to_second(give)), 1
     )
     (joined,) = kernel_call(
-        join_kernel, [shaped(block_rows // 2, BF16)], [], (where, quad, to_chip(quad, 2)), 1
-    )
-    joined_next = to_chip(joined, 1)
+        join_kernel, [shaped(block_rows // 2, BF16)], [], (where, quad, to_second(quad)), 1
+    )
+    joined_next = to_first(joined)
     d_proj, d_fc, d_out, small_sums = kernel_call(
         output_kernel,
         [
@@ -1455,12 +1491,13 @@
             where,
             normed_mine,
             *packed,
-            *own_weights,
-            gain_one.reshape(-1, 1),
-            shift_one.reshape(-1, 1),
+            weight_q,
+            weight_k,
+            weight_v,
+            small_all,
         ),
         8,
-        after=tuple(arrived[1:]),
+        after=tuple(arrived[1:]) + (give,),
     )
     qkv_blocks = add_up(qkv_keep, to_core(qkv_send)).astype(BF16)
     qkv_half = scatter_parts(qkv_blocks[:2], qkv_blocks[2:])

time: 452 us -> 423 us (0.936)
  local copies, waits for them, and re-layouts: 68.2 us -> 25 us
  starting transfers between devices: 65.1 us -> 78.8 us
  other arithmetic: 14.9 us -> 8.44 us
  waiting for transfers between devices: 136 us -> 141 us
    ppermute x36 -> x40, starting transfers between devices: 65.1 us -> 78.7 us  [exchange(): return lax.ppermute(value, ('fsdp', 'ctx'), pairs)]
    dynamic_update_slice x11 -> x0, local copies, waits for them, and re-layouts: 10.7 us -> none  [place_all(): buffer = lax.dynamic_update_slice(buffer, full.astype(dtype), starts)]
    reshape x9 -> x0, local copies, waits for them, and re-layouts: 7.43 us -> none  [the longest x8 7.42 us: fast_body(): small_all[:, n * shard:(n + 1) * shard].reshape(1, -1)]
    another operation x6 -> x3, other arithmetic: 8.18 us -> 1.03 us  [the longest x1 2.43 us: fast_body(): swapped = to_core(jnp.stack([from_near, from_across, from_far])[:, :half])]
    concatenate x1 -> x0, local copies, waits for them, and re-layouts: 6.18 us -> none  [fast_body(): jnp.concatenate([b_query, b_value, b_out, b_proj, gain1, shift1, gain2, s...]
    slice x4 -> x1, local copies, waits for them, and re-layouts: 5.57 us -> 0.08 us  [fast_body(): vectors += [b_fc[shard * n:shard * (n + 1)] for n in range(fsdp)]]
    ppermute x36 -> x40, waiting for transfers between devices: 136 us -> 141 us  [exchange(): return lax.ppermute(value, ('fsdp', 'ctx'), pairs)]
    squeeze x2 -> x0, local copies, waits for them, and re-layouts: 4.7 us -> none  [fast_body(): beside = [near_pair[0], near_pair[1], far_pair[0], far_pair[1]]]
  transfers between devices with their start and end apart: 37 -> 41, of which waited for: 13 -> 17; matrix products, arithmetic and copies ran while one was open for 13% -> 3% of each run, Pallas kernels for 27% -> 25%
where the time goes in v1:
time: 423 us; the launch traced here: 418 us
  Pallas kernels  149 us (35%)
  waiting for transfers between devices  141 us (33%)
  starting transfers between devices  78.8 us (19%)
  local copies, waits for them, and re-layouts  25 us (6%)
  between operations  14.9 us (4%)
  other arithmetic  8.44 us (2%)
    pallas_call x15, Pallas kernels, kernel_call(): pl.pallas_call(ordered, out_shape=outputs, in_specs=in_specs, out_specs=[...  149 us
    ppermute x40, waiting for transfers between devices, exchange(): return lax.ppermute(value, ('fsdp', 'ctx'), pairs)  141 us
    ppermute x40, starting transfers between devices, exchange(): return lax.ppermute(value, ('fsdp', 'ctx'), pairs)  78.7 us
    unnamed x112, local copies, waits for them, and re-layouts  17.8 us
  transfers between devices with their start and end apart: 41, of which 17 were waited for; matrix products, arithmetic and copies ran while one was open for 3% of the time, Pallas kernels for 25%

profile of v1, /device:TPU:0, one launch (start us, length us, event | category | flops | bytes accessed | tf_op | source)
XLA Modules:
  0.0 417.5 jit_solution(1685111212721439592)
XLA Ops:
  7.3 1.2 dynamic-slice_dynamic-update-slice_fusion
  9.0 1.0 copy-done
  10.6 3.0 collective-permute-start.8
  13.6 1.5 collective-permute-start.7
  15.1 1.6 collective-permute-start.5
  16.7 2.5 collective-permute-start.2
  21.6 8.3 %collective-permute-done.7.refs_7_ = bf16[112,2304]{1,0:T(8,128)(2,1)} collective-permute-done((bf16[112,2304]{1,0:T(8,128)(2,1)S(1)}, bf16[112,2304]{1,0:T(8,128)(2,1)}, u32[]{:S(2)}, u32[]{:S(2)}) %collective-permute-start.7) | collective-permute-done | bytes 516128 | tf_op jit(solution)/shard_map/ppermute | solution.py:1191
  30.4 3.0 collective-permute-start
  34.1 12.0 %collective-permute-done.2.refs_3_ = bf16[384,768]{1,0:T(8,128)(2,1)S(1)} collective-permute-done((bf16[384,768]{1,0:T(8,128)(2,1)S(1)}, bf16[384,768]{1,0:T(8,128)(2,1)S(1)}, u32[]{:S(2)}, u32[]{:S(2)}) %collective-permute-start.2) | collective-permute-done | bytes 589856 | tf_op jit(solution)/shard_map/ppermute | solution.py:1191
  48.0 23.3 %collective-permute-done.refs_1_ = bf16[384,768]{1,0:T(8,128)(2,1)} collective-permute-done((bf16[384,768]{1,0:T(8,128)(2,1)S(1)}, bf16[384,768]{1,0:T(8,128)(2,1)}, u32[]{:S(2)}, u32[]{:S(2)}) %collective-permute-start) | collective-permute-done | bytes 589856 | tf_op jit(solution)/shard_map/ppermute | solution.py:1191
  73.4 9.2 %shard_map.280 = (bf16[2,384,192]{2,1,0:T(8,128)(2,1)}, bf16[4,384,192]{2,1,0:T(8,128)(2,1)}, bf16[4,192,384]{2,1,0:T(8,128)(2,1)}, bf16[4,384,192]{2,1,0:T(8,12...) custom-call(s32[3]{0:T(128)} %pad_add_fusion.refs_0_, ...), custom_call_target="tpu_custom_call" | custom-call | flops 10376999936 | bytes 14653452 | tf_op jit(solution)/shard_map/pallas_call | solution.py:742
  82.7 1.5 broadcast_in_dim.126.refs_15_.refs_9_
  84.2 31.7 %shard_map.281 = (bf16[4,384,192]{2,1,0:T(8,128)(2,1)}, bf16[8,384,192]{2,1,0:T(8,128)(2,1)}, bf16[8,192,384]{2,1,0:T(8,128)(2,1)}, bf16[8,384,192]{2,1,0:T(8,12...) custom-call(s32[3]{0:T(128)} %pad_add_fusion.refs_0_, ...), custom_call_target="tpu_custom_call" | custom-call | flops 34589999104 | bytes 17029132 | tf_op jit(solution)/shard_map/pallas_call | solution.py:742
  116.0 1.3 fusion.8.refs_9_
  117.3 5.3 %collective-permute-start.16 = (bf16[4,864,768]{2,1,0:T(8,128)(2,1)}, bf16[4,864,768]{2,1,0:T(8,128)(2,1)}, u32[]{:S(2)}, u32[]{:S(2)}) collective-permute-start(bf16[4,864,768]{2,1,0:T(8,128)(2,1)} %fusion.8.refs_9_), channel_id=1, source_target_pairs={{0,1},{1,0},{2,3},{3,2},{4,5},{5,4},{6,7},{7,6},{8,9},{9,8},{10,11... | collective-permute-start | bytes 15925256 | tf_op jit(solution)/shard_map/ppermute | solution.py:1191
  122.6 3.5 collective-permute-start.14
  127.5 1.4 fusion.3.refs_7_
  128.9 4.3 %collective-permute-done.13.refs_2_ = bf16[384,192]{1,0:T(8,128)(2,1)S(1)} collective-permute-done((bf16[384,192]{1,0:T(8,128)(2,1)}, bf16[384,192]{1,0:T(8,128)(2,1)S(1)}, u32[]{:S(2)}, u32[]{:S(2)}) %collective-permute-start.13) | collective-permute-done | bytes 147488 | tf_op jit(solution)/shard_map/ppermute | solution.py:1191
  133.2 7.3 %collective-permute-done.14.refs_3_ = bf16[384,192]{1,0:T(8,128)(2,1)S(1)} collective-permute-done((bf16[384,192]{1,0:T(8,128)(2,1)}, bf16[384,192]{1,0:T(8,128)(2,1)S(1)}, u32[]{:S(2)}, u32[]{:S(2)}) %collective-permute-start.14) | collective-permute-done | bytes 147488 | tf_op jit(solution)/shard_map/ppermute | solution.py:1191
  141.2 21.8 %shard_map.282 = (bf16[384,768]{1,0:T(8,128)(2,1)}, f32[384,768]{1,0:T(8,128)}, bf16[384,192]{1,0:T(8,128)(2,1)}, bf16[384,192]{1,0:T(8,128)(2,1)}, bf16[384,192...) custom-call(s32[3]{0:T(128)} %pad_add_fusion.refs_0_, ...), custom_call_target="tpu_custom_call" | custom-call | flops 24213000192 | bytes 23840268 | tf_op jit(solution)/shard_map/pallas_call | solution.py:742
  163.1 3.8 collective-permute-start.17
  167.9 1.5 collective-permute-start.19
  169.4 7.0 %collective-permute-done.17.refs_6_.refs_4_ = bf16[384,192]{1,0:T(8,128)(2,1)S(1)} collective-permute-done((bf16[384,192]{1,0:T(8,128)(2,1)}, bf16[384,192]{1,0:T(8,128)(2,1)S(1)}, u32[]{:S(2)}, u32[]{:S(2)}) %collective-permute-start.17) | collective-permute-done | bytes 147488 | tf_op jit(solution)/shard_map/ppermute | solution.py:1191
  177.0 1.5 copy-done.17
  178.5 13.4 %shard_map.285 = (bf16[2,896,768]{2,1,0:T(8,128)(2,1)}, bf16[2,896,768]{2,1,0:T(8,128)(2,1)}) custom-call(s32[3]{0:T(128)} %pad_add_fusion.refs_0_, bf16[384,5760]{1,0:T(8,128)(2,1)} %get-tuple-element.103.refs_1_, bf16[384,5760]{1,0:T(8,128)(2,1)} %copy-done.17, f32[4,16,768]{2,1,0:T(8,128)} %get-tuple-element.105.refs_3_, bf16[384,192]{1,0:T(8,128)(2,1)} %copy-done.46), custom_call_target="tpu_custom_call" | custom-call | flops 16142000128 | bytes 14549004 | tf_op jit(solution)/shard_map/pallas_call | solution.py:742
  193.2 30.7 %shard_map.283 = (bf16[4,384,192]{2,1,0:T(8,128)(2,1)}, f32[4,384,384]{2,1,0:T(8,128)}, bf16[4,384,384]{2,1,0:T(8,128)(2,1)}) custom-call(s32[3]{0:T(128)} %pad_add_fusion.refs_0_, bf16[4,384,192]{2,1,0:T(8,128)(2,1)} %get-tuple-element.84.refs_1_, bf16[8,384,192]{2,1,0:T(8,128)(2,1)} %get-tuple-element.85.refs_2_, ...), custom_call_target="tpu_custom_call" | custom-call | flops 34589999104 | bytes 11667468 | tf_op jit(solution)/shard_map/pallas_call | solution.py:742
  223.9 4.9 %collective-permute-start.20 = (bf16[4,384,384]{2,1,0:T(8,128)(2,1)}, bf16[4,384,384]{2,1,0:T(8,128)(2,1)S(1)}, u32[]{:S(2)}, u32[]{:S(2)}) collective-permute-start(bf16[4,384,384]{2,1,0:T(8,128)(2,1)} %get-tuple-element.96), channel_id=1, source_target_pairs={{0,1},{1,0},{2,3},{3,2},{4,5},{5,4},{6,7},{7,6},{8,9},{9,8},{10,11... | collective-permute-start | bytes 3538952 | tf_op jit(solution)/shard_map/ppermute | solution.py:1191
  228.8 2.7 collective-permute-done.20.refs_3_
  232.5 3.8 shard_map.284
  236.3 1.5 copy-done.1
  237.8 4.1 shard_map.286
  242.0 1.5 collective-permute-start.26
  243.5 2.3 collective-permute-start.22
  245.8 2.1 collective-permute-start.23
  247.9 17.1 %collective-permute-done.21.refs_4_.refs_2_.refs_10_ = bf16[384,576]{1,0:T(8,128)(2,1)S(1)} collective-permute-done((bf16[384,576]{1,0:T(8,128)(2,1)S(1)}, bf16[384,576]{1,0:T(8,128)(2,1)S(1)}, u32[]{:S(2)}, u32[]{:S(2)}) %collective-permute-start.21) | collective-permute-done | bytes 442400 | tf_op jit(solution)/shard_map/ppermute | solution.py:1191
  265.0 14.7 %collective-permute-done.22.refs_5_.refs_3_.refs_11_ = bf16[384,576]{1,0:T(8,128)(2,1)S(1)} collective-permute-done((bf16[384,576]{1,0:T(8,128)(2,1)S(1)}, bf16[384,576]{1,0:T(8,128)(2,1)S(1)}, u32[]{:S(2)}, u32[]{:S(2)}) %collective-permute-start.22) | collective-permute-done | bytes 442400 | tf_op jit(solution)/shard_map/ppermute | solution.py:1191
  280.7 1.1 copy-done.18
  281.8 4.5 %shard_map.287 = (f32[448,768]{1,0:T(8,128)}, bf16[448,768]{1,0:T(8,128)(2,1)}) custom-call(s32[3]{0:T(128)} %pad_add_fusion.refs_0_, bf16[2,896,768]{2,1,0:T(8,128)(2,1)} %get-tuple-element.106.refs_1_, bf16[2,896,768]{2,1,0:T(8,128)(2,1)} %copy-done.1, bf16[896,768]{1,0:T(8,128)(2,1)} %copy-done.18, bf16[384,576]{1,0:T(8,128)(2,1)} %copy-done.34, ...), custom_call_target="tpu_custom_call" | custom-call | flops 2305999872 | bytes 8945676 | tf_op jit(solution)/shard_map/pallas_call | solution.py:742
  286.3 9.0 %collective-permute-start.27 = (bf16[448,768]{1,0:T(8,128)(2,1)}, bf16[448,768]{1,0:T(8,128)(2,1)S(1)}, u32[]{:S(2)}, u32[]{:S(2)}) collective-permute-start(bf16[448,768]{1,0:T(8,128)(2,1)} %get-tuple-element.109), channel_id=1, source_target_pairs={{0,2},{1,5},{2,0},{3,7},{4,6},{5,1},{6,4},{7,3},{8,10},{9,13},{10,... | collective-permute-start | bytes 2064392 | tf_op jit(solution)/shard_map/ppermute | solution.py:1191
  295.3 14.6 %collective-permute-done.27.refs_2_ = bf16[448,768]{1,0:T(8,128)(2,1)S(1)} collective-permute-done((bf16[448,768]{1,0:T(8,128)(2,1)}, bf16[448,768]{1,0:T(8,128)(2,1)S(1)}, u32[]{:S(2)}, u32[]{:S(2)}) %collective-permute-start.27) | collective-permute-done | bytes 688160 | tf_op jit(solution)/shard_map/ppermute | solution.py:1191
  310.8 2.6 shard_map.288
  313.4 8.9 %shard_map.290 = (f32[4,112,576]{2,1,0:T(8,128)}, bf16[4,112,576]{2,1,0:T(8,128)(2,1)}) custom-call(s32[3]{0:T(128)} %pad_add_fusion.refs_0_, bf16[4,384,768]{2,1,0:T(8,128)(2,1)} %get-tuple-element.111.refs_1_, bf16[384,576]{1,0:T(8,128)(2,1)} %get-tuple-element.97.refs_3_.refs_1_.refs_2_, bf16[384,576]{1,0:T(8,128)(2,1)} %get-tuple-element.98.refs_3_, ...), custom_call_target="tpu_custom_call" | custom-call | flops 9223999488 | bytes 6610956 | tf_op jit(solution)/shard_map/pallas_call | solution.py:742
  322.3 2.2 collective-permute-done.28
  324.5 1.4 add_convert_fusion
  326.0 2.2 collective-permute-start.29
  328.2 2.4 collective-permute-start.35
  330.6 2.2 collective-permute-done.29
  332.8 2.3 collective-permute-start.30
  335.1 3.7 collective-permute-done.35.refs_2_
  339.6 2.0 shard_map.292.refs_1_
  341.6 2.1 collective-permute-start.36
  343.9 9.8 %collective-permute-done.36.refs_2_ = bf16[224,768]{1,0:T(8,128)(2,1)S(1)} collective-permute-done((bf16[224,768]{1,0:T(8,128)(2,1)}, bf16[224,768]{1,0:T(8,128)(2,1)S(1)}, u32[]{:S(2)}, u32[]{:S(2)}) %collective-permute-start.36) | collective-permute-done | bytes 344096 | tf_op jit(solution)/shard_map/ppermute | solution.py:1191
  354.4 2.1 shard_map.293.refs_1_
  356.4 15.1 %collective-permute-start.37 = (bf16[448,768]{1,0:T(8,128)(2,1)}, bf16[448,768]{1,0:T(8,128)(2,1)S(1)}, u32[]{:S(2)}, u32[]{:S(2)}) collective-permute-start(bf16[448,768]{1,0:T(8,128)(2,1)} %shard_map.293.refs_1_), channel_id=1, source_target_pairs={{0,2},{1,5},{2,0},{3,7},{4,6},{5,1},{6,4},{7,3},{8,10},{9,13},{10,... | collective-permute-start | bytes 2064392 | tf_op jit(solution)/shard_map/ppermute | solution.py:1191
  371.7 2.8 collective-permute-start.34
  375.1 1.0 collective-permute-start.32
  376.1 6.9 %shard_map.289 = f32[384,768]{1,0:T(8,128)} custom-call(s32[3]{0:T(128)} %pad_add_fusion.refs_0_, bf16[384,576]{1,0:T(8,128)(2,1)} %get-tuple-element.97.refs_3_.refs_1_.refs_2_, bf16[384,576]{1,0:T(8,128)(2,1)} %copy-done.34, bf16[384,576]{1,0:T(8,128)(2,1)} %copy-done.35, bf16[384,576]{1,0:T(8,128)(2,1)} %copy-done.36, ...), custom_call_target="tpu_custom_call" | custom-call | flops 5765000192 | bytes 8306700 | tf_op jit(solution)/shard_map/pallas_call | solution.py:742
  383.1 4.7 %collective-permute-done.37.refs_2_ = bf16[448,768]{1,0:T(8,128)(2,1)S(1)} collective-permute-done((bf16[448,768]{1,0:T(8,128)(2,1)}, bf16[448,768]{1,0:T(8,128)(2,1)S(1)}, u32[]{:S(2)}, u32[]{:S(2)}) %collective-permute-start.37) | collective-permute-done | bytes 688160 | tf_op jit(solution)/shard_map/ppermute | solution.py:1191
  387.8 6.1 %collective-permute-done.33.refs_3_ = bf16[2,112,576]{2,1,0:T(8,128)(2,1)S(1)} collective-permute-done((bf16[2,112,576]{2,1,0:T(8,128)(2,1)S(1)}, bf16[2,112,576]{2,1,0:T(8,128)(2,1)S(1)}, u32[]{:S(2)}, u32[]{:S(2)}) %collective-permute-start.33) | collective-permute-done | bytes 258080 | tf_op jit(solution)/shard_map/ppermute | solution.py:1191
  393.9 1.0 collective-permute-done.32.refs_2_
  395.7 3.0 shard_map.291
  403.1 4.6 %shard_map.294 = (f32[768,768]{1,0:T(8,128)}, f32[192,3072]{1,0:T(8,128)}, f32[192,768]{1,0:T(8,128)}, f32[16,768]{1,0:T(8,128)}) custom-call(s32[3]{0:T(128)} %pad_add_fusion.refs_0_, bf16[448,768]{1,0:T(8,128)(2,1)} %shard_map.293.refs_1_, bf16[448,768]{1,0:T(8,128)(2,1)} %copy-done.21, bf16[448,768]{1,0:T(8,128)(2,1)} %copy-done.22, ...), custom_call_target="tpu_custom_call" | custom-call | flops 2305999872 | bytes 8110092 | tf_op jit(solution)/shard_map/pallas_call | solution.py:742
  407.7 1.3 slice_reduce_fusion.1
  409.0 1.4 fusion.9
  (190 shorter events, 24.0 us)
Async XLA Ops:
  7.2 1.5 copy-start.2
  7.2 108.8 %all-gather.3.cloned.1.call-start = ((), (), s32[]{:S(2)}) async-start(), calls=%async_computation | async-start | bytes 6635520 | tf_op jit(solution)/shard_map/all_gather | solution.py:1235
  8.8 1.7 copy-start.4
  9.0 10.2 %copy-start.16 = (s32[1,8]{1,0:T(1,128)S(1)}, s32[1,8]{1,0:T(1,128)}, u32[]{:S(2)}) copy-start(s32[1,8]{1,0:T(1,128)} %param.32) | copy-start | bytes 100
  9.0 12.3 %copy-start.52 = (s32[1,3]{1,0:T(1,128)S(1)}, s32[1,3]{1,0:T(1,128)}, u32[]{:S(2)}) copy-start(s32[1,3]{1,0:T(1,128)} %param.33) | copy-start | bytes 40
  10.0 5.1 %copy-start.25 = (bf16[384,768]{1,0:T(8,128)(2,1)S(1)}, bf16[384,768]{1,0:T(8,128)(2,1)}, u32[]{:S(2)}) copy-start(bf16[384,768]{1,0:T(8,128)(2,1)} %refs_6_.3) | copy-start | bytes 1769476
  10.5 61.3 %copy-start.6 = (bf16[16,192]{1,0:T(8,128)(2,1)}, bf16[16,192]{1,0:T(8,128)(2,1)S(1)}, u32[]{:S(2)}) copy-start(bf16[16,192]{1,0:T(8,128)(2,1)S(1)} %select_select_fusion.refs_6_) | copy-start | bytes 18436
  10.6 19.8 %collective-permute-start.8 = (bf16[112,2304]{1,0:T(8,128)(2,1)S(1)}, bf16[112,2304]{1,0:T(8,128)(2,1)}, u32[]{:S(2)}, u32[]{:S(2)}) collective-permute-start(bf16[112,2304]{1,0:T(8,128)(2,1)S(1)} %fusion.1), channel_id=1, source_target_pairs={{0,16},{1,9},{2,18},{3,11},{4,20},{5,13},{6,22},{7,15},{8,24},{9,1... | collective-permute-start | bytes 1548296 | tf_op jit(solution)/shard_map/ppermute | solution.py:1191
  13.6 16.4 %collective-permute-start.7 = (bf16[112,2304]{1,0:T(8,128)(2,1)S(1)}, bf16[112,2304]{1,0:T(8,128)(2,1)}, u32[]{:S(2)}, u32[]{:S(2)}) collective-permute-start(bf16[112,2304]{1,0:T(8,128)(2,1)S(1)} %fusion.1), channel_id=1, source_target_pairs={{0,8},{1,17},{2,10},{3,19},{4,12},{5,21},{6,14},{7,23},{8,0},{9,25... | collective-permute-start | bytes 1548296 | tf_op jit(solution)/shard_map/ppermute | solution.py:1191
  15.1 18.3 %collective-permute-start.5 = (bf16[384,768]{1,0:T(8,128)(2,1)S(1)}, bf16[384,768]{1,0:T(8,128)(2,1)S(1)}, u32[]{:S(2)}, u32[]{:S(2)}) collective-permute-start(bf16[384,768]{1,0:T(8,128)(2,1)S(1)} %copy-done.25), channel_id=1, source_target_pairs={{0,2},{1,3},{2,0},{3,1},{4,6},{5,7},{6,4},{7,5},{8,10},{9,11},{10,... | collective-permute-start | bytes 1769480 | tf_op jit(solution)/shard_map/ppermute | solution.py:1191
  16.7 16.8 %collective-permute-start.4 = (bf16[384,768]{1,0:T(8,128)(2,1)S(1)}, bf16[384,768]{1,0:T(8,128)(2,1)S(1)}, u32[]{:S(2)}, u32[]{:S(2)}) collective-permute-start(bf16[384,768]{1,0:T(8,128)(2,1)S(1)} %copy-done.25), channel_id=1, source_target_pairs={{0,1},{1,0},{2,3},{3,2},{4,5},{5,4},{6,7},{7,6},{8,9},{9,8},{10,11... | collective-permute-start | bytes 1769480 | tf_op jit(solution)/shard_map/ppermute | solution.py:1191
  16.7 29.5 %collective-permute-start.2 = (bf16[384,768]{1,0:T(8,128)(2,1)S(1)}, bf16[384,768]{1,0:T(8,128)(2,1)S(1)}, u32[]{:S(2)}, u32[]{:S(2)}) collective-permute-start(bf16[384,768]{1,0:T(8,128)(2,1)S(1)} %copy-done.25), channel_id=1, source_target_pairs={{0,6},{1,7},{2,4},{3,5},{4,2},{5,3},{6,0},{7,1},{8,14},{9,15},{10,... | collective-permute-start | bytes 1769480 | tf_op jit(solution)/shard_map/ppermute | solution.py:1191
  30.0 16.2 %collective-permute-start.9 = (bf16[112,2304]{1,0:T(8,128)(2,1)}, bf16[112,2304]{1,0:T(8,128)(2,1)}, u32[]{:S(2)}, u32[]{:S(2)}) collective-permute-start(bf16[112,2304]{1,0:T(8,128)(2,1)} %collective-permute-done.7.refs_7_), channel_id=1, source_target_pairs={{0,16},{1,9},{2,18},{3,11},{4,20},{5,13},{6,22},{7,15},{8,24},{9,1... | collective-permute-start | bytes 1548296 | tf_op jit(solution)/shard_map/ppermute | solution.py:1191
  30.4 40.9 %collective-permute-start = (bf16[384,768]{1,0:T(8,128)(2,1)S(1)}, bf16[384,768]{1,0:T(8,128)(2,1)}, u32[]{:S(2)}, u32[]{:S(2)}) collective-permute-start(bf16[384,768]{1,0:T(8,128)(2,1)S(1)} %copy-done.25), channel_id=1, source_target_pairs={{0,4},{1,5},{2,6},{3,7},{4,0},{5,1},{6,2},{7,3},{8,12},{9,13},{10,... | collective-permute-start | bytes 1769480 | tf_op jit(solution)/shard_map/ppermute | solution.py:1191
  33.4 38.4 %copy-start.27 = (bf16[384,768]{1,0:T(8,128)(2,1)}, bf16[384,768]{1,0:T(8,128)(2,1)S(1)}, u32[]{:S(2)}) copy-start(bf16[384,768]{1,0:T(8,128)(2,1)S(1)} %collective-permute-done.5.refs_3_) | copy-start | bytes 1769476
  33.4 38.4 %collective-permute-start.6 = (bf16[384,768]{1,0:T(8,128)(2,1)S(1)}, bf16[384,768]{1,0:T(8,128)(2,1)}, u32[]{:S(2)}, u32[]{:S(2)}) collective-permute-start(bf16[384,768]{1,0:T(8,128)(2,1)S(1)} %collective-permute-done.5.refs_3_), channel_id=1, source_target_pairs={{0,1},{1,0},{2,3},{3,2},{4,5},{5,4},{6,7},{7,6},{8,9},{9,8},{10,11... | collective-permute-start | bytes 1769480 | tf_op jit(solution)/shard_map/ppermute | solution.py:1191
  33.5 38.3 %copy-start.28 = (bf16[384,768]{1,0:T(8,128)(2,1)}, bf16[384,768]{1,0:T(8,128)(2,1)S(1)}, u32[]{:S(2)}) copy-start(bf16[384,768]{1,0:T(8,128)(2,1)S(1)} %collective-permute-done.4.refs_2_) | copy-start | bytes 1769476
  33.5 38.3 %collective-permute-start.10 = (bf16[112,2304]{1,0:T(8,128)(2,1)}, bf16[112,2304]{1,0:T(8,128)(2,1)S(1)}, u32[]{:S(2)}, u32[]{:S(2)}) collective-permute-start(bf16[112,2304]{1,0:T(8,128)(2,1)} %collective-permute-done.7.refs_7_), channel_id=1, source_target_pairs={{0,1},{1,0},{2,3},{3,2},{4,5},{5,4},{6,7},{7,6},{8,9},{9,8},{10,11... | collective-permute-start | bytes 1548296 | tf_op jit(solution)/shard_map/ppermute | solution.py:1191
  46.1 36.5 %copy-start.26 = (bf16[384,768]{1,0:T(8,128)(2,1)}, bf16[384,768]{1,0:T(8,128)(2,1)S(1)}, u32[]{:S(2)}) copy-start(bf16[384,768]{1,0:T(8,128)(2,1)S(1)} %collective-permute-done.2.refs_3_) | copy-start | bytes 1769476
  46.1 25.2 %collective-permute-start.11 = (bf16[112,2304]{1,0:T(8,128)(2,1)}, bf16[112,2304]{1,0:T(8,128)(2,1)S(1)}, u32[]{:S(2)}, u32[]{:S(2)}) collective-permute-start(bf16[112,2304]{1,0:T(8,128)(2,1)} %collective-permute-done.8.refs_8_), channel_id=1, source_target_pairs={{0,1},{1,0},{2,3},{3,2},{4,5},{5,4},{6,7},{7,6},{8,9},{9,8},{10,11... | collective-permute-start | bytes 1548296 | tf_op jit(solution)/shard_map/ppermute | solution.py:1191
  46.1 25.7 %collective-permute-start.12 = (bf16[112,2304]{1,0:T(8,128)(2,1)}, bf16[112,2304]{1,0:T(8,128)(2,1)S(1)}, u32[]{:S(2)}, u32[]{:S(2)}) collective-permute-start(bf16[112,2304]{1,0:T(8,128)(2,1)} %collective-permute-done.9.refs_9_), channel_id=1, source_target_pairs={{0,1},{1,0},{2,3},{3,2},{4,5},{5,4},{6,7},{7,6},{8,9},{9,8},{10,11... | collective-permute-start | bytes 1548296 | tf_op jit(solution)/shard_map/ppermute | solution.py:1191
  71.3 11.4 %collective-permute-start.3 = (bf16[384,768]{1,0:T(8,128)(2,1)S(1)}, bf16[384,768]{1,0:T(8,128)(2,1)S(1)}, u32[]{:S(2)}, u32[]{:S(2)}) collective-permute-start(bf16[384,768]{1,0:T(8,128)(2,1)S(1)} %collective-permute-done.2.refs_3_), channel_id=1, source_target_pairs={{0,1},{1,0},{2,3},{3,2},{4,5},{5,4},{6,7},{7,6},{8,9},{9,8},{10,11... | collective-permute-start | bytes 1769480 | tf_op jit(solution)/shard_map/ppermute | solution.py:1191
  71.3 11.4 %collective-permute-start.1 = (bf16[384,768]{1,0:T(8,128)(2,1)}, bf16[384,768]{1,0:T(8,128)(2,1)S(1)}, u32[]{:S(2)}, u32[]{:S(2)}) collective-permute-start(bf16[384,768]{1,0:T(8,128)(2,1)} %collective-permute-done.refs_1_), channel_id=1, source_target_pairs={{0,1},{1,0},{2,3},{3,2},{4,5},{5,4},{6,7},{7,6},{8,9},{9,8},{10,11... | collective-permute-start | bytes 1769480 | tf_op jit(solution)/shard_map/ppermute | solution.py:1191
  82.7 1.5 copy-start.29
  82.7 1.5 copy-start.30
  117.3 23.2 %collective-permute-start.16 = (bf16[4,864,768]{2,1,0:T(8,128)(2,1)}, bf16[4,864,768]{2,1,0:T(8,128)(2,1)}, u32[]{:S(2)}, u32[]{:S(2)}) collective-permute-start(bf16[4,864,768]{2,1,0:T(8,128)(2,1)} %fusion.8.refs_9_), channel_id=1, source_target_pairs={{0,1},{1,0},{2,3},{3,2},{4,5},{5,4},{6,7},{7,6},{8,9},{9,8},{10,11... | collective-permute-start | bytes 15925256 | tf_op jit(solution)/shard_map/ppermute | solution.py:1191
  122.6 10.6 %collective-permute-start.13 = (bf16[384,192]{1,0:T(8,128)(2,1)}, bf16[384,192]{1,0:T(8,128)(2,1)S(1)}, u32[]{:S(2)}, u32[]{:S(2)}) collective-permute-start(bf16[384,192]{1,0:T(8,128)(2,1)} %get-tuple-element.79), channel_id=1, source_target_pairs={{0,2},{1,3},{2,0},{3,1},{4,6},{5,7},{6,4},{7,5},{8,10},{9,11},{10,... | collective-permute-start | bytes 442376 | tf_op jit(solution)/shard_map/ppermute | solution.py:1191
  122.6 17.9 %collective-permute-start.14 = (bf16[384,192]{1,0:T(8,128)(2,1)}, bf16[384,192]{1,0:T(8,128)(2,1)S(1)}, u32[]{:S(2)}, u32[]{:S(2)}) collective-permute-start(bf16[384,192]{1,0:T(8,128)(2,1)} %get-tuple-element.80), channel_id=1, source_target_pairs={{0,4},{1,5},{2,6},{3,7},{4,0},{5,1},{6,2},{7,3},{8,12},{9,13},{10,... | collective-permute-start | bytes 442376 | tf_op jit(solution)/shard_map/ppermute | solution.py:1191
  126.1 14.4 %collective-permute-start.15 = (bf16[384,192]{1,0:T(8,128)(2,1)}, bf16[384,192]{1,0:T(8,128)(2,1)S(1)}, u32[]{:S(2)}, u32[]{:S(2)}) collective-permute-start(bf16[384,192]{1,0:T(8,128)(2,1)} %get-tuple-element.81), channel_id=1, source_target_pairs={{0,6},{1,7},{2,4},{3,5},{4,2},{5,3},{6,0},{7,1},{8,14},{9,15},{10,... | collective-permute-start | bytes 442376 | tf_op jit(solution)/shard_map/ppermute | solution.py:1191
  133.2 7.3 %copy-start.47 = (bf16[384,192]{1,0:T(8,128)(2,1)}, bf16[384,192]{1,0:T(8,128)(2,1)S(1)}, u32[]{:S(2)}) copy-start(bf16[384,192]{1,0:T(8,128)(2,1)S(1)} %collective-permute-done.13.refs_2_) | copy-start | bytes 442372
  163.0 13.3 %collective-permute-start.24 = (bf16[384,5760]{1,0:T(8,128)(2,1)}, bf16[384,5760]{1,0:T(8,128)(2,1)S(1)}, u32[]{:S(2)}, u32[]{:S(2)}) collective-permute-start(bf16[384,5760]{1,0:T(8,128)(2,1)} %get-tuple-element.104), channel_id=1, source_target_pairs={{0,1},{1,0},{2,3},{3,2},{4,5},{5,4},{6,7},{7,6},{8,9},{9,8},{10,11... | collective-permute-start | bytes 13271048 | tf_op jit(solution)/shard_map/ppermute | solution.py:1191
  163.1 13.2 %collective-permute-start.17 = (bf16[384,192]{1,0:T(8,128)(2,1)}, bf16[384,192]{1,0:T(8,128)(2,1)S(1)}, u32[]{:S(2)}, u32[]{:S(2)}) collective-permute-start(bf16[384,192]{1,0:T(8,128)(2,1)} %get-tuple-element.89), channel_id=1, source_target_pairs={{0,2},{1,3},{2,0},{3,1},{4,6},{5,7},{6,4},{7,5},{8,10},{9,11},{10,... | collective-permute-start | bytes 442376 | tf_op jit(solution)/shard_map/ppermute | solution.py:1191
  166.9 25.5 %collective-permute-start.18 = (bf16[384,192]{1,0:T(8,128)(2,1)}, bf16[384,192]{1,0:T(8,128)(2,1)S(1)}, u32[]{:S(2)}, u32[]{:S(2)}) collective-permute-start(bf16[384,192]{1,0:T(8,128)(2,1)} %get-tuple-element.90), channel_id=1, source_target_pairs={{0,4},{1,5},{2,6},{3,7},{4,0},{5,1},{6,2},{7,3},{8,12},{9,13},{10,... | collective-permute-start | bytes 442376 | tf_op jit(solution)/shard_map/ppermute | solution.py:1191
  167.9 24.6 %collective-permute-start.19 = (bf16[384,192]{1,0:T(8,128)(2,1)}, bf16[384,192]{1,0:T(8,128)(2,1)S(1)}, u32[]{:S(2)}, u32[]{:S(2)}) collective-permute-start(bf16[384,192]{1,0:T(8,128)(2,1)} %get-tuple-element.91), channel_id=1, source_target_pairs={{0,6},{1,7},{2,4},{3,5},{4,2},{5,3},{6,0},{7,1},{8,14},{9,15},{10,... | collective-permute-start | bytes 442376 | tf_op jit(solution)/shard_map/ppermute | solution.py:1191
  176.3 2.1 copy-start.17
  191.9 44.4 %collective-permute-start.25 = (bf16[2,896,768]{2,1,0:T(8,128)(2,1)}, bf16[2,896,768]{2,1,0:T(8,128)(2,1)S(1)}, u32[]{:S(2)}, u32[]{:S(2)}) collective-permute-start(bf16[2,896,768]{2,1,0:T(8,128)(2,1)} %get-tuple-element.107), channel_id=1, source_target_pairs={{0,8},{1,17},{2,10},{3,19},{4,12},{5,21},{6,14},{7,23},{8,0},{9,25... | collective-permute-start | bytes 8257544 | tf_op jit(solution)/shard_map/ppermute | solution.py:1191
  223.9 7.6 %collective-permute-start.20 = (bf16[4,384,384]{2,1,0:T(8,128)(2,1)}, bf16[4,384,384]{2,1,0:T(8,128)(2,1)S(1)}, u32[]{:S(2)}, u32[]{:S(2)}) collective-permute-start(bf16[4,384,384]{2,1,0:T(8,128)(2,1)} %get-tuple-element.96), channel_id=1, source_target_pairs={{0,1},{1,0},{2,3},{3,2},{4,5},{5,4},{6,7},{7,6},{8,9},{9,8},{10,11... | collective-permute-start | bytes 3538952 | tf_op jit(solution)/shard_map/ppermute | solution.py:1191
  236.3 1.5 copy-start.1
  237.8 5.7 %copy-start.37 = (bf16[384,576]{1,0:T(8,128)(2,1)S(1)}, bf16[384,576]{1,0:T(8,128)(2,1)}, u32[]{:S(2)}) copy-start(bf16[384,576]{1,0:T(8,128)(2,1)} %get-tuple-element.98.refs_3_) | copy-start | bytes 1327108
  237.8 5.7 %copy-start.38 = (bf16[384,576]{1,0:T(8,128)(2,1)S(1)}, bf16[384,576]{1,0:T(8,128)(2,1)}, u32[]{:S(2)}) copy-start(bf16[384,576]{1,0:T(8,128)(2,1)} %get-tuple-element.99.refs_4_) | copy-start | bytes 1327108
  237.8 8.0 %copy-start.39 = (bf16[384,576]{1,0:T(8,128)(2,1)S(1)}, bf16[384,576]{1,0:T(8,128)(2,1)}, u32[]{:S(2)}) copy-start(bf16[384,576]{1,0:T(8,128)(2,1)} %get-tuple-element.100.refs_5_) | copy-start | bytes 1327108
  242.0 37.8 %collective-permute-start.26 = (bf16[896,768]{1,0:T(8,128)(2,1)}, bf16[896,768]{1,0:T(8,128)(2,1)S(1)}, u32[]{:S(2)}, u32[]{:S(2)}) collective-permute-start(bf16[896,768]{1,0:T(8,128)(2,1)} %shard_map.286), channel_id=1, source_target_pairs={{0,16},{1,9},{2,18},{3,11},{4,20},{5,13},{6,22},{7,15},{8,24},{9,1... | collective-permute-start | bytes 4128776 | tf_op jit(solution)/shard_map/ppermute | solution.py:1191
  243.5 21.5 %collective-permute-start.21 = (bf16[384,576]{1,0:T(8,128)(2,1)S(1)}, bf16[384,576]{1,0:T(8,128)(2,1)S(1)}, u32[]{:S(2)}, u32[]{:S(2)}) collective-permute-start(bf16[384,576]{1,0:T(8,128)(2,1)S(1)} %copy-done.37), channel_id=1, source_target_pairs={{0,2},{1,3},{2,0},{3,1},{4,6},{5,7},{6,4},{7,5},{8,10},{9,11},{10,... | collective-permute-start | bytes 1327112 | tf_op jit(solution)/shard_map/ppermute | solution.py:1191
  243.5 36.2 %collective-permute-start.22 = (bf16[384,576]{1,0:T(8,128)(2,1)S(1)}, bf16[384,576]{1,0:T(8,128)(2,1)S(1)}, u32[]{:S(2)}, u32[]{:S(2)}) collective-permute-start(bf16[384,576]{1,0:T(8,128)(2,1)S(1)} %copy-done.38), channel_id=1, source_target_pairs={{0,4},{1,5},{2,6},{3,7},{4,0},{5,1},{6,2},{7,3},{8,12},{9,13},{10,... | collective-permute-start | bytes 1327112 | tf_op jit(solution)/shard_map/ppermute | solution.py:1191
  245.8 33.9 %collective-permute-start.23 = (bf16[384,576]{1,0:T(8,128)(2,1)S(1)}, bf16[384,576]{1,0:T(8,128)(2,1)S(1)}, u32[]{:S(2)}, u32[]{:S(2)}) collective-permute-start(bf16[384,576]{1,0:T(8,128)(2,1)S(1)} %copy-done.39), channel_id=1, source_target_pairs={{0,6},{1,7},{2,4},{3,5},{4,2},{5,3},{6,0},{7,1},{8,14},{9,15},{10,... | collective-permute-start | bytes 1327112 | tf_op jit(solution)/shard_map/ppermute | solution.py:1191
  265.0 14.7 %copy-start.34 = (bf16[384,576]{1,0:T(8,128)(2,1)}, bf16[384,576]{1,0:T(8,128)(2,1)S(1)}, u32[]{:S(2)}) copy-start(bf16[384,576]{1,0:T(8,128)(2,1)S(1)} %collective-permute-done.21.refs_4_.refs_2_.refs_10_) | copy-start | bytes 1327108
  286.3 23.6 %collective-permute-start.27 = (bf16[448,768]{1,0:T(8,128)(2,1)}, bf16[448,768]{1,0:T(8,128)(2,1)S(1)}, u32[]{:S(2)}, u32[]{:S(2)}) collective-permute-start(bf16[448,768]{1,0:T(8,128)(2,1)} %get-tuple-element.109), channel_id=1, source_target_pairs={{0,2},{1,5},{2,0},{3,7},{4,6},{5,1},{6,4},{7,3},{8,10},{9,13},{10,... | collective-permute-start | bytes 2064392 | tf_op jit(solution)/shard_map/ppermute | solution.py:1191
  322.3 2.2 collective-permute-start.28
  324.5 3.7 copy-start.40
  326.0 6.8 %collective-permute-start.29 = (bf16[2,112,576]{2,1,0:T(8,128)(2,1)S(1)}, bf16[2,112,576]{2,1,0:T(8,128)(2,1)S(1)}, u32[]{:S(2)}, u32[]{:S(2)}) collective-permute-start(bf16[2,112,576]{2,1,0:T(8,128)(2,1)S(1)} %slice.101), channel_id=1, source_target_pairs={{0,8},{1,17},{2,10},{3,19},{4,12},{5,21},{6,14},{7,23},{8,0},{9,25... | collective-permute-start | bytes 774152 | tf_op jit(solution)/shard_map/ppermute | solution.py:1191
  328.2 10.7 %collective-permute-start.35 = (bf16[224,768]{1,0:T(8,128)(2,1)S(1)}, bf16[224,768]{1,0:T(8,128)(2,1)S(1)}, u32[]{:S(2)}, u32[]{:S(2)}) collective-permute-start(bf16[224,768]{1,0:T(8,128)(2,1)S(1)} %copy-done.40), channel_id=1, source_target_pairs={{0,4},{1,3},{2,6},{3,1},{4,0},{5,7},{6,2},{7,5},{8,12},{9,11},{10,... | collective-permute-start | bytes 1032200 | tf_op jit(solution)/shard_map/ppermute | solution.py:1191
  332.8 10.9 %collective-permute-start.30 = (bf16[112,576]{1,0:T(8,128)(2,1)S(1)}, bf16[112,576]{1,0:T(8,128)(2,1)S(1)}, u32[]{:S(2)}, u32[]{:S(2)}) collective-permute-start(bf16[112,576]{1,0:T(8,128)(2,1)S(1)} %fusion.4), channel_id=1, source_target_pairs={{0,16},{1,9},{2,18},{3,11},{4,20},{5,13},{6,22},{7,15},{8,24},{9,1... | collective-permute-start | bytes 387080 | tf_op jit(solution)/shard_map/ppermute | solution.py:1191
  341.6 12.1 %collective-permute-start.36 = (bf16[224,768]{1,0:T(8,128)(2,1)}, bf16[224,768]{1,0:T(8,128)(2,1)S(1)}, u32[]{:S(2)}, u32[]{:S(2)}) collective-permute-start(bf16[224,768]{1,0:T(8,128)(2,1)} %shard_map.292.refs_1_), channel_id=1, source_target_pairs={{0,4},{1,3},{2,6},{3,1},{4,0},{5,7},{6,2},{7,5},{8,12},{9,11},{10,... | collective-permute-start | bytes 1032200 | tf_op jit(solution)/shard_map/ppermute | solution.py:1191
  343.8 27.8 %collective-permute-start.31 = (bf16[112,576]{1,0:T(8,128)(2,1)S(1)}, bf16[112,576]{1,0:T(8,128)(2,1)S(1)}, u32[]{:S(2)}, u32[]{:S(2)}) collective-permute-start(bf16[112,576]{1,0:T(8,128)(2,1)S(1)} %fusion.2), channel_id=1, source_target_pairs={{0,1},{1,0},{2,3},{3,2},{4,5},{5,4},{6,7},{7,6},{8,9},{9,8},{10,11... | collective-permute-start | bytes 387080 | tf_op jit(solution)/shard_map/ppermute | solution.py:1191
  356.4 31.3 %collective-permute-start.37 = (bf16[448,768]{1,0:T(8,128)(2,1)}, bf16[448,768]{1,0:T(8,128)(2,1)S(1)}, u32[]{:S(2)}, u32[]{:S(2)}) collective-permute-start(bf16[448,768]{1,0:T(8,128)(2,1)} %shard_map.293.refs_1_), channel_id=1, source_target_pairs={{0,2},{1,5},{2,0},{3,7},{4,6},{5,1},{6,4},{7,3},{8,10},{9,13},{10,... | collective-permute-start | bytes 2064392 | tf_op jit(solution)/shard_map/ppermute | solution.py:1191
  371.6 11.4 %copy-start.3 = (bf16[2,112,576]{2,1,0:T(8,128)(2,1)}, bf16[2,112,576]{2,1,0:T(8,128)(2,1)S(1)}, u32[]{:S(2)}) copy-start(bf16[2,112,576]{2,1,0:T(8,128)(2,1)S(1)} %pad_maximum_fusion.refs_1_) | copy-start | bytes 774148
  371.7 16.1 %collective-permute-start.34 = (bf16[2,112,576]{2,1,0:T(8,128)(2,1)S(1)}, bf16[2,112,576]{2,1,0:T(8,128)(2,1)S(1)}, u32[]{:S(2)}, u32[]{:S(2)}) collective-permute-start(bf16[2,112,576]{2,1,0:T(8,128)(2,1)S(1)} %pad_maximum_fusion.refs_1_), channel_id=1, source_target_pairs={{0,6},{1,7},{2,4},{3,5},{4,2},{5,3},{6,0},{7,1},{8,14},{9,15},{10,... | collective-permute-start | bytes 774152 | tf_op jit(solution)/shard_map/ppermute | solution.py:1191
  374.4 19.5 %collective-permute-start.33 = (bf16[2,112,576]{2,1,0:T(8,128)(2,1)S(1)}, bf16[2,112,576]{2,1,0:T(8,128)(2,1)S(1)}, u32[]{:S(2)}, u32[]{:S(2)}) collective-permute-start(bf16[2,112,576]{2,1,0:T(8,128)(2,1)S(1)} %pad_maximum_fusion.refs_1_), channel_id=1, source_target_pairs={{0,4},{1,5},{2,6},{3,7},{4,0},{5,1},{6,2},{7,3},{8,12},{9,13},{10,... | collective-permute-start | bytes 774152 | tf_op jit(solution)/shard_map/ppermute | solution.py:1191
  375.1 19.9 %collective-permute-start.32 = (bf16[2,112,576]{2,1,0:T(8,128)(2,1)S(1)}, bf16[2,112,576]{2,1,0:T(8,128)(2,1)S(1)}, u32[]{:S(2)}, u32[]{:S(2)}) collective-permute-start(bf16[2,112,576]{2,1,0:T(8,128)(2,1)S(1)} %pad_maximum_fusion.refs_1_), channel_id=1, source_target_pairs={{0,2},{1,3},{2,0},{3,1},{4,6},{5,7},{6,4},{7,5},{8,10},{9,11},{10,... | collective-permute-start | bytes 774152 | tf_op jit(solution)/shard_map/ppermute | solution.py:1191
  376.1 6.9 %copy-start.20 = (bf16[448,768]{1,0:T(8,128)(2,1)S(1)}, bf16[448,768]{1,0:T(8,128)(2,1)}, u32[]{:S(2)}) copy-start(bf16[448,768]{1,0:T(8,128)(2,1)} %shard_map.293.refs_1_) | copy-start | bytes 2064388
  383.0 18.3 %collective-permute-start.38 = (bf16[448,768]{1,0:T(8,128)(2,1)S(1)}, bf16[448,768]{1,0:T(8,128)(2,1)S(1)}, u32[]{:S(2)}, u32[]{:S(2)}) collective-permute-start(bf16[448,768]{1,0:T(8,128)(2,1)S(1)} %copy-done.20), channel_id=1, source_target_pairs={{0,1},{1,0},{2,3},{3,2},{4,5},{5,4},{6,7},{7,6},{8,9},{9,8},{10,11... | collective-permute-start | bytes 2064392 | tf_op jit(solution)/shard_map/ppermute | solution.py:1191
  387.8 10.9 %copy-start.21 = (bf16[448,768]{1,0:T(8,128)(2,1)}, bf16[448,768]{1,0:T(8,128)(2,1)S(1)}, u32[]{:S(2)}) copy-start(bf16[448,768]{1,0:T(8,128)(2,1)S(1)} %collective-permute-done.37.refs_2_) | copy-start | bytes 2064388
  387.8 13.6 %collective-permute-start.39 = (bf16[448,768]{1,0:T(8,128)(2,1)S(1)}, bf16[448,768]{1,0:T(8,128)(2,1)S(1)}, u32[]{:S(2)}, u32[]{:S(2)}) collective-permute-start(bf16[448,768]{1,0:T(8,128)(2,1)S(1)} %collective-permute-done.37.refs_2_), channel_id=1, source_target_pairs={{0,1},{1,0},{2,3},{3,2},{4,5},{5,4},{6,7},{7,6},{8,9},{9,8},{10,11... | collective-permute-start | bytes 2064392 | tf_op jit(solution)/shard_map/ppermute | solution.py:1191
  387.8 7.2 %copy-start.43 = (bf16[2,112,576]{2,1,0:T(8,128)(2,1)}, bf16[2,112,576]{2,1,0:T(8,128)(2,1)S(1)}, u32[]{:S(2)}) copy-start(bf16[2,112,576]{2,1,0:T(8,128)(2,1)S(1)} %collective-permute-done.34.refs_4_) | copy-start | bytes 774148
  (30 other events, 31.1 us)
Sparse Core Ops, SparseCore 0:
  10.4 71.1 all-gather.2

commit v2 on v1

--- a/solution.py
+++ b/solution.py
@@ -484,10 +484,8 @@
     smalls_ref,
     near_ref,
     across_ref,
-    far_ref,
     near_other,
     across_other,
-    far_other,
     q,
     k,
     kt,
@@ -506,17 +504,19 @@
     features, half, width = wide // 3, shard // 2, wq.shape[1]
     full_ref[pl.ds(pl.multiple_of(part * shard, 16), shard), :] = w_ref[...]
     small_ref[part] = smalls_ref[...].astype(FP32)
-    for ref, owner in ((near_ref, part ^ near), (across_ref, part ^ across), (far_ref, part ^ 3)):
-        first = pl.multiple_of(owner * shard + core * half, 16)
-        full_ref[pl.ds(first, half), :] = ref[0:half, :]
-        small_ref[owner] = ref[half:, 0:width].astype(FP32)
-    for ref, owner in (
-        (near_other, part ^ across),
-        (across_other, part ^ near),
-        (far_other, part ^ 3),
-    ):
-        first = pl.multiple_of(owner * shard + (1 - core) * half, 16)
-        full_ref[pl.ds(first, half), :] = ref[0:half, :]
+    step = half + 16
+    pieces = (
+        (near_ref, 0, part ^ near, core),
+        (across_ref, 0, part ^ across, core),
+        (across_ref, step, part ^ 3, core),
+        (near_other, 0, part ^ across, 1 - core),
+        (across_other, 0, part ^ near, 1 - core),
+        (across_other, step, part ^ 3, 1 - core),
+    )
+    for ref, at, owner, which in pieces:
+        first = pl.multiple_of(owner * shard + which * half, 16)
+        full_ref[pl.ds(first, half), :] = ref[at : at + half, :]
+        small_ref[owner] = ref[at + half : at + step, 0:width].astype(FP32)
     for z in range(features // width):
 
         @pl.when(chip == z)
@@ -1021,41 +1021,13 @@
             ref[slot, half : half + 16, :] = tail.astype(ref.dtype)
 
 
-def first_bit(core, chip):
-    return jnp.where(core == 0, chip % 2, chip // 2)
-
-
 def relay_kernel(where, keep_ref, theirs_ref, relay_ref):
     relay_ref[...] = (keep_ref[1].astype(FP32) + theirs_ref[1].astype(FP32)).astype(BF16)
 
 
-def pair_kernel(where, keep_ref, theirs_ref, last_ref, stay_ref, give_ref):
-    low = first_bit(where[1], where[2])
-    count = stay_ref.shape[0]
-    for ref, which in ((stay_ref, low), (give_ref, 1 - low)):
-        span = pl.ds(pl.multiple_of(which * count, 16), count)
-        total = keep_ref[0, span, :].astype(FP32) + theirs_ref[0, span, :].astype(FP32)
-        ref[...] = (total + last_ref[span, :].astype(FP32)).astype(ref.dtype)
-
-
-def quad_kernel(where, stay_ref, arrived_ref, keep_ref, give_ref):
-    high = first_bit(1 - where[1], where[2])
-    count = keep_ref.shape[0]
-    for ref, which in ((keep_ref, high), (give_ref, 1 - high)):
-        span = pl.ds(pl.multiple_of(which * count, 16), count)
-        total = stay_ref[span, :] + arrived_ref[span, :].astype(FP32)
-        ref[...] = total.astype(ref.dtype)
-
-
-def total_kernel(where, keep_ref, arrived_ref, out_ref):
-    out_ref[...] = (keep_ref[...] + arrived_ref[...].astype(FP32)).astype(BF16)
-
-
-def join_kernel(where, mine_ref, arrived_ref, out_ref):
-    high = first_bit(1 - where[1], where[2])
-    count = mine_ref.shape[0]
-    out_ref[pl.ds(pl.multiple_of(high * count, 16), count), :] = mine_ref[...]
-    out_ref[pl.ds(pl.multiple_of((1 - high) * count, 16), count), :] = arrived_ref[...]
+def block_kernel(where, keep_ref, theirs_ref, last_ref, out_ref):
+    total = keep_ref[0].astype(FP32) + theirs_ref[0].astype(FP32)
+    out_ref[...] = (total + last_ref[...].astype(FP32)).astype(BF16)
 
 
 def input_grad_kernel(
@@ -1081,15 +1053,9 @@
 
 
 def output_kernel(
-    where, m0, m1, t0, t1, proj_ref, fc_ref, out_ref, sums_ref, mine_ref, other_ref
+    where, mine_ref, other_ref, proj_ref, fc_ref, out_ref, sums_ref
 ):
     core = where[1]
-    count = m0.shape[0]
-    own_bit, other_bit = first_bit(core, where[2]), first_bit(1 - core, where[2])
-    for n, (mine, other) in enumerate(((m0, t0), (m1, t1))):
-        for bit, source, target in ((own_bit, mine, mine_ref), (other_bit, other, other_ref)):
-            first = pl.multiple_of((bit if n == 0 else 1 - bit) * count, 16)
-            target[pl.ds(first, count), :] = source[...]
     half_columns = proj_ref.shape[0] // 2
     shard, features = out_ref.shape
     out_rows = half_columns + 2 * shard
@@ -1122,7 +1088,8 @@
         place(other_ref, 0)
 
 
-def qkv_output_kernel(where, h0, h1, h2, h3, out_ref, extra_ref):
+def qkv_output_kernel(where, h0, h1, h2, h3, out_ref, extra_ref, zero_ref):
+    zero_ref[...] = jnp.zeros_like(zero_ref)
     core, chip = where[1], where[2]
     shard, wide = out_ref.shape
     features = wide // 3
@@ -1179,6 +1146,7 @@
     part = lax.axis_index("fsdp")
     near = 1 + core
     across = 2 - core
+    same_core = [[2 * z + k for z in range(chips)] for k in range(2)]
     where = jnp.stack([part, core, chip]).astype(jnp.int32)
 
     def exchange(value, partner):
@@ -1201,12 +1169,6 @@
 
     def to_chip(value, step):
         return exchange(value, lambda f, c: (f, c ^ (2 * step)))
-
-    def to_first(value):
-        return exchange(value, lambda f, c: (f, c ^ (2 + 2 * (c % 2))))
-
-    def to_second(value):
-        return exchange(value, lambda f, c: (f, c ^ (4 - 2 * (c % 2))))
 
     def pick(array, index, axis=0):
         return lax.dynamic_index_in_dim(array, index, axis, keepdims=False)
@@ -1231,7 +1193,6 @@
     )
 
     blocks = [tokens] + [to_chip(tokens, s) for s in (1, 2, 3)]
-    beside = [to_core(v) for v in blocks]
     bundles = lax.all_gather(bundle, "fsdp", axis=0)
 
     count_row = counts[0]
@@ -1271,10 +1232,12 @@
         ],
         axis=0,
     )
-    from_near, from_across = to_near(mine), to_across(mine)
-    from_far = to_across(from_near)
-    gathered = (from_near, from_across, from_far)
-    gathered += tuple(to_core(v) for v in gathered)
+    from_near = to_near(mine)
+    from_across = to_across(jnp.concatenate([mine, from_near], axis=0))
+    gathered = (from_near, from_across, to_core(from_near), to_core(from_across))
+    first_tile = tokens[:16, :128] + from_near[:16, :128] * jnp.asarray(0, BF16)
+    swap_tokens = lax.dynamic_update_slice(tokens, first_tile, (0, 0))
+    beside = [to_core(v) for v in [swap_tokens] + blocks[1:]]
     *half_stores, qkv_full, weight_q, weight_k, weight_v, small_all = kernel_call(
         project_kernel,
         [
@@ -1419,69 +1382,23 @@
     def add_up(left_side, right_side):
         return left_side.astype(FP32) + right_side.astype(FP32)
 
-    def scatter_parts(keep, send):
-        theirs = to_near(send)
-        last = to_across(add_up(keep[1], theirs[1]).astype(BF16))
-        return (add_up(keep[0], theirs[0]) + last.astype(FP32)).astype(BF16)
-
     arrived = swap_chips(packed)
     theirs = to_near(grads_send)
     block = jax.ShapeDtypeStruct((block_rows, features), BF16)
 
-    def shaped(count, dtype):
-        return jax.ShapeDtypeStruct((count, features), dtype)
-
     (relay,) = kernel_call(
         relay_kernel, [block], [], (where, grads_keep, theirs), 1, after=(packed[0],)
     )
-    stay, give = kernel_call(
-        pair_kernel,
-        [shaped(block_rows // 2, FP32), shaped(block_rows // 2, BF16)],
+    (grads_block,) = kernel_call(
+        block_kernel,
+        [block],
         [],
         (where, grads_keep, theirs, to_across(relay)),
         2,
         after=tuple(arrived[1:]),
     )
-    stay, give = kernel_call(
-        quad_kernel,
-        [shaped(block_rows // 4, FP32), shaped(block_rows // 4, BF16)],
-        [],
-        (where, stay, to_first(give)),
-        2,
-    )
-    (grad_tokens,) = kernel_call(
-        input_grad_kernel,
-        [jax.ShapeDtypeStruct((rows, features), FP32)],
-        [pltpu.VMEM((rows, 3 * features), BF16)],
-        tuple([where] + arrived) + (qkv_full, tokens, grad_middle, small_all),
-        5,
-        after=(give,),
-    )
-
-    (quad,) = kernel_call(
-        total_kernel, [shaped(block_rows // 4, BF16)], [], (where, stay, to_second(give)), 1
-    )
-    (joined,) = kernel_call(
-        join_kernel, [shaped(block_rows // 2, BF16)], [], (where, quad, to_second(quad)), 1
-    )
-    joined_next = to_first(joined)
-    d_proj, d_fc, d_out, small_sums = kernel_call(
-        output_kernel,
-        [
-            jax.ShapeDtypeStruct((columns, features), FP32),
-            jax.ShapeDtypeStruct((shard, hidden_width), FP32),
-            jax.ShapeDtypeStruct((shard, features), FP32),
-            jax.ShapeDtypeStruct((16, features), FP32),
-        ],
-        [pltpu.VMEM((block_rows, features), BF16), pltpu.VMEM((block_rows, features), BF16)],
-        (where, joined, joined_next, to_core(joined), to_core(joined_next)),
-        2,
-    )
-    d_bias_out, d_bias_proj, d_gain_two, d_shift_two = (
-        small_sums[0, n * shard : (n + 1) * shard] for n in range(4)
-    )
-    d_bias_fc = small_sums[1]
-
+
+    grads_half = lax.psum(grads_block, "ctx", axis_index_groups=same_core)
     block_shape = (fsdp, half + 16, 3 * width)
     qkv_keep, qkv_send = kernel_call(
         qkv_grad_kernel,
@@ -1497,21 +1414,52 @@
             small_all,
         ),
         8,
-        after=tuple(arrived[1:]) + (give,),
+        after=tuple(arrived[1:]) + (grads_block,),
     )
     qkv_blocks = add_up(qkv_keep, to_core(qkv_send)).astype(BF16)
-    qkv_half = scatter_parts(qkv_blocks[:2], qkv_blocks[2:])
+    theirs_qkv = to_near(qkv_blocks[2:])
+    last_qkv = to_across(add_up(qkv_blocks[1], theirs_qkv[1]).astype(BF16))
+    qkv_half = (add_up(qkv_blocks[0], theirs_qkv[0]) + last_qkv.astype(FP32)).astype(BF16)
+    (grad_tokens,) = kernel_call(
+        input_grad_kernel,
+        [jax.ShapeDtypeStruct((rows, features), FP32)],
+        [pltpu.VMEM((rows, 3 * features), BF16)],
+        tuple([where] + arrived) + (qkv_full, tokens, grad_middle, small_all),
+        5,
+        after=(theirs_qkv,),
+    )
+
     halves = swap_chips([jnp.stack([qkv_half, to_core(qkv_half)])] * 4)
-    d_qkv, extra = kernel_call(
+    d_qkv, extra, zeros = kernel_call(
         qkv_output_kernel,
         [
             jax.ShapeDtypeStruct((shard, 3 * features), FP32),
             jax.ShapeDtypeStruct((chips, 16, 3 * width), FP32),
+            jax.ShapeDtypeStruct((16, 128), BF16),
         ],
         [],
         tuple([where] + halves),
         2,
-    )
+        after=(grad_tokens,),
+    )
+    grads_half = lax.dynamic_update_slice(grads_half, grads_half[:16, :128] + zeros, (0, 0))
+    d_proj, d_fc, d_out, small_sums = kernel_call(
+        output_kernel,
+        [
+            jax.ShapeDtypeStruct((columns, features), FP32),
+            jax.ShapeDtypeStruct((shard, hidden_width), FP32),
+            jax.ShapeDtypeStruct((shard, features), FP32),
+            jax.ShapeDtypeStruct((16, features), FP32),
+        ],
+        [],
+        (where, grads_half, to_core(grads_half)),
+        2,
+    )
+    d_bias_out, d_bias_proj, d_gain_two, d_shift_two = (
+        small_sums[0, n * shard : (n + 1) * shard] for n in range(4)
+    )
+    d_bias_fc = small_sums[1]
+
     owner_extra = pick(extra, part)
     d_bias_q = owner_extra[2, :width]
     d_bias_v = owner_extra[2, 2 * width :]

time: 423 us -> 419 us (level)
  waiting for transfers between devices: 141 us -> 174 us
  starting transfers between devices: 78.8 us -> 52.1 us
  Pallas kernels: 149 us -> 142 us
    ppermute x40 -> x33, starting transfers between devices: 78.7 us -> 52 us  [exchange(): return lax.ppermute(value, ('fsdp', 'ctx'), pairs)]
    psum x0 -> x1, waiting for transfers between devices: none -> 23.7 us  [fast_body(): grads_half = lax.psum(grads_block, 'ctx', axis_index_groups=same_core)]
    ppermute x40 -> x33, waiting for transfers between devices: 141 us -> 150 us  [exchange(): return lax.ppermute(value, ('fsdp', 'ctx'), pairs)]
    pallas_call x15 -> x12, Pallas kernels: 149 us -> 142 us  [kernel_call(): pl.pallas_call(ordered, out_shape=outputs, in_specs=in_specs, out_specs=[...]
    unnamed x112 -> x97, local copies, waits for them, and re-layouts: 17.8 us -> 15.2 us
  transfers between devices with their start and end apart: 41 -> 35, of which waited for: 17 -> 17; matrix products, arithmetic and copies ran while one was open for 3% -> 3% of each run, Pallas kernels for 25% -> 24%
where the time goes in v2:
time: 419 us; the launch traced here: 415 us
  waiting for transfers between devices  174 us (42%)
  Pallas kernels  142 us (34%)
  starting transfers between devices  52.1 us (12%)
  local copies, waits for them, and re-layouts  22.4 us (5%)
  between operations  14.9 us (4%)
  other arithmetic  9.78 us (2%)
    ppermute x33, waiting for transfers between devices, exchange(): return lax.ppermute(value, ('fsdp', 'ctx'), pairs)  150 us
    pallas_call x12, Pallas kernels, kernel_call(): pl.pallas_call(ordered, out_shape=outputs, in_specs=in_specs, out_specs=[...  142 us
    ppermute x33, starting transfers between devices, exchange(): return lax.ppermute(value, ('fsdp', 'ctx'), pairs)  52 us
    psum x1, waiting for transfers between devices, fast_body(): grads_half = lax.psum(grads_block, 'ctx', axis_index_groups=same_core)  23.7 us
    unnamed x97, local copies, waits for them, and re-layouts  15.2 us
  transfers between devices with their start and end apart: 35, of which 17 were waited for; matrix products, arithmetic and copies ran while one was open for 3% of the time, Pallas kernels for 24%

profile of v2, /device:TPU:0, one launch (start us, length us, event | category | flops | bytes accessed | tf_op | source)
XLA Modules:
  0.0 415.0 jit_solution(11763918455649131644)
XLA Ops:
  7.3 1.2 dynamic-slice_dynamic-update-slice_fusion
  9.0 1.1 copy-done.1
  10.6 3.0 collective-permute-start.4
  13.6 7.1 %collective-permute-done.4.refs_7_ = bf16[112,2304]{1,0:T(8,128)(2,1)S(1)} collective-permute-done((bf16[112,2304]{1,0:T(8,128)(2,1)S(1)}, bf16[112,2304]{1,0:T(8,128)(2,1)S(1)}, u32[]{:S(2)}, u32[]{:S(2)}) %collective-permute-start.4) | collective-permute-done | bytes 516128 | tf_op jit(solution)/shard_map/ppermute | solution.py:1159
  20.8 2.1 collective-permute-start.8
  22.9 1.6 collective-permute-start.6
  24.5 2.5 collective-permute-start.2
  28.7 21.2 %collective-permute-done.8.refs_8_ = bf16[224,2304]{1,0:T(8,128)(2,1)} collective-permute-done((bf16[224,2304]{1,0:T(8,128)(2,1)S(1)}, bf16[224,2304]{1,0:T(8,128)(2,1)}, u32[]{:S(2)}, u32[]{:S(2)}) %collective-permute-start.8) | collective-permute-done | bytes 1032224 | tf_op jit(solution)/shard_map/ppermute | solution.py:1159
  51.6 2.3 collective-permute-done.2.refs_3_
  55.3 21.6 %collective-permute-done.refs_1_ = bf16[384,768]{1,0:T(8,128)(2,1)} collective-permute-done((bf16[384,768]{1,0:T(8,128)(2,1)S(1)}, bf16[384,768]{1,0:T(8,128)(2,1)}, u32[]{:S(2)}, u32[]{:S(2)}) %collective-permute-start) | collective-permute-done | bytes 589856 | tf_op jit(solution)/shard_map/ppermute | solution.py:1159
  77.8 1.0 copy-done.27
  78.7 9.4 %shard_map.280 = (bf16[2,384,192]{2,1,0:T(8,128)(2,1)}, bf16[4,384,192]{2,1,0:T(8,128)(2,1)}, bf16[4,192,384]{2,1,0:T(8,128)(2,1)}, bf16[4,384,192]{2,1,0:T(8,12...) custom-call(s32[3]{0:T(128)} %pad_add_fusion.refs_0_, ...), custom_call_target="tpu_custom_call" | custom-call | flops 10376999936 | bytes 14653452 | tf_op jit(solution)/shard_map/pallas_call | solution.py:742
  88.1 1.5 broadcast_in_dim.126.refs_15_.refs_9_
  89.6 31.7 %shard_map.281 = (bf16[4,384,192]{2,1,0:T(8,128)(2,1)}, bf16[8,384,192]{2,1,0:T(8,128)(2,1)}, bf16[8,192,384]{2,1,0:T(8,128)(2,1)}, bf16[8,384,192]{2,1,0:T(8,12...) custom-call(s32[3]{0:T(128)} %pad_add_fusion.refs_0_, ...), custom_call_target="tpu_custom_call" | custom-call | flops 34589999104 | bytes 17029132 | tf_op jit(solution)/shard_map/pallas_call | solution.py:742
  121.4 1.3 fusion.7.refs_9_
  122.6 5.7 %collective-permute-start.14 = (bf16[4,864,768]{2,1,0:T(8,128)(2,1)}, bf16[4,864,768]{2,1,0:T(8,128)(2,1)}, u32[]{:S(2)}, u32[]{:S(2)}) collective-permute-start(bf16[4,864,768]{2,1,0:T(8,128)(2,1)} %fusion.7.refs_9_), channel_id=1, source_target_pairs={{0,1},{1,0},{2,3},{3,2},{4,5},{5,4},{6,7},{7,6},{8,9},{9,8},{10,11... | collective-permute-start | bytes 15925256 | tf_op jit(solution)/shard_map/ppermute | solution.py:1159
  128.3 3.5 collective-permute-start.12
  131.8 0.9 collective-permute-start.13
  133.3 1.3 fusion.1.refs_7_
  134.6 4.3 %collective-permute-done.11.refs_2_ = bf16[384,192]{1,0:T(8,128)(2,1)S(1)} collective-permute-done((bf16[384,192]{1,0:T(8,128)(2,1)}, bf16[384,192]{1,0:T(8,128)(2,1)S(1)}, u32[]{:S(2)}, u32[]{:S(2)}) %collective-permute-start.11) | collective-permute-done | bytes 147488 | tf_op jit(solution)/shard_map/ppermute | solution.py:1159
  138.9 7.3 %collective-permute-done.12.refs_3_ = bf16[384,192]{1,0:T(8,128)(2,1)S(1)} collective-permute-done((bf16[384,192]{1,0:T(8,128)(2,1)}, bf16[384,192]{1,0:T(8,128)(2,1)S(1)}, u32[]{:S(2)}, u32[]{:S(2)}) %collective-permute-start.12) | collective-permute-done | bytes 147488 | tf_op jit(solution)/shard_map/ppermute | solution.py:1159
  146.9 21.7 %shard_map.282 = (bf16[384,768]{1,0:T(8,128)(2,1)}, f32[384,768]{1,0:T(8,128)}, bf16[384,192]{1,0:T(8,128)(2,1)}, bf16[384,192]{1,0:T(8,128)(2,1)}, bf16[384,192...) custom-call(s32[3]{0:T(128)} %pad_add_fusion.refs_0_, ...), custom_call_target="tpu_custom_call" | custom-call | flops 24213000192 | bytes 23840268 | tf_op jit(solution)/shard_map/pallas_call | solution.py:742
  168.8 3.8 collective-permute-start.15
  172.6 1.0 collective-permute-start.16
  173.6 1.5 collective-permute-start.17
  175.0 7.0 %collective-permute-done.15.refs_6_.refs_4_ = bf16[384,192]{1,0:T(8,128)(2,1)S(1)} collective-permute-done((bf16[384,192]{1,0:T(8,128)(2,1)}, bf16[384,192]{1,0:T(8,128)(2,1)S(1)}, u32[]{:S(2)}, u32[]{:S(2)}) %collective-permute-start.15) | collective-permute-done | bytes 147488 | tf_op jit(solution)/shard_map/ppermute | solution.py:1159
  182.7 1.5 copy-done.24
  184.1 13.4 %shard_map.285 = (bf16[2,896,768]{2,1,0:T(8,128)(2,1)}, bf16[2,896,768]{2,1,0:T(8,128)(2,1)}) custom-call(s32[3]{0:T(128)} %pad_add_fusion.refs_0_, bf16[384,5760]{1,0:T(8,128)(2,1)} %get-tuple-element.101.refs_1_, bf16[384,5760]{1,0:T(8,128)(2,1)} %copy-done.24, f32[4,16,768]{2,1,0:T(8,128)} %get-tuple-element.103.refs_3_, bf16[384,192]{1,0:T(8,128)(2,1)} %copy-done.38), custom_call_target="tpu_custom_call" | custom-call | flops 16142000128 | bytes 14549004 | tf_op jit(solution)/shard_map/pallas_call | solution.py:742
  198.9 30.3 %shard_map.283 = (bf16[4,384,192]{2,1,0:T(8,128)(2,1)}, f32[4,384,384]{2,1,0:T(8,128)}, bf16[4,384,384]{2,1,0:T(8,128)(2,1)}) custom-call(s32[3]{0:T(128)} %pad_add_fusion.refs_0_, bf16[4,384,192]{2,1,0:T(8,128)(2,1)} %get-tuple-element.81.refs_1_, bf16[8,384,192]{2,1,0:T(8,128)(2,1)} %get-tuple-element.82.refs_2_, ...), custom_call_target="tpu_custom_call" | custom-call | flops 34589999104 | bytes 11667468 | tf_op jit(solution)/shard_map/pallas_call | solution.py:742
  229.1 5.9 %collective-permute-start.18 = (bf16[4,384,384]{2,1,0:T(8,128)(2,1)}, bf16[4,384,384]{2,1,0:T(8,128)(2,1)S(1)}, u32[]{:S(2)}, u32[]{:S(2)}) collective-permute-start(bf16[4,384,384]{2,1,0:T(8,128)(2,1)} %get-tuple-element.93), channel_id=1, source_target_pairs={{0,1},{1,0},{2,3},{3,2},{4,5},{5,4},{6,7},{7,6},{8,9},{9,8},{10,11... | collective-permute-start | bytes 3538952 | tf_op jit(solution)/shard_map/ppermute | solution.py:1159
  235.0 2.7 collective-permute-done.18.refs_3_
  237.7 1.0 copy-done.26
  238.7 3.8 shard_map.284
  242.5 1.5 copy-done
  244.0 4.1 shard_map.286
  248.6 2.3 collective-permute-start.20
  250.9 2.1 collective-permute-start.21
  253.0 18.5 %collective-permute-done.19.refs_4_.refs_10_.refs_2_ = bf16[384,576]{1,0:T(8,128)(2,1)S(1)} collective-permute-done((bf16[384,576]{1,0:T(8,128)(2,1)S(1)}, bf16[384,576]{1,0:T(8,128)(2,1)S(1)}, u32[]{:S(2)}, u32[]{:S(2)}) %collective-permute-start.19) | collective-permute-done | bytes 442400 | tf_op jit(solution)/shard_map/ppermute | solution.py:1159
  271.5 13.3 %collective-permute-done.20.refs_5_.refs_11_.refs_3_ = bf16[384,576]{1,0:T(8,128)(2,1)S(1)} collective-permute-done((bf16[384,576]{1,0:T(8,128)(2,1)S(1)}, bf16[384,576]{1,0:T(8,128)(2,1)S(1)}, u32[]{:S(2)}, u32[]{:S(2)}) %collective-permute-start.20) | collective-permute-done | bytes 442400 | tf_op jit(solution)/shard_map/ppermute | solution.py:1159
  284.8 0.8 copy-done.6
  285.8 1.1 copy-done.2
  286.8 4.6 %shard_map.287.refs_13_ = bf16[896,768]{1,0:T(8,128)(2,1)} custom-call(s32[3]{0:T(128)} %pad_add_fusion.refs_0_, bf16[2,896,768]{2,1,0:T(8,128)(2,1)} %get-tuple-element.104.refs_1_, bf16[2,896,768]{2,1,0:T(8,128)(2,1)} %copy-done, bf16[896,768]{1,0:T(8,128)(2,1)} %copy-done.2, bf16[384,576]{1,0:T(8,128)(2,1)} %copy-done.5, bf16[384,576]{1,0:T(8,128)(2,1)} %copy-done.6, ...), custom_call_target="tpu_custom_call" | custom-call | flops 2305999872 | bytes 8257548 | tf_op jit(solution)/shard_map/pallas_call | solution.py:742
  291.4 8.8 %shard_map.288 = (f32[4,112,576]{2,1,0:T(8,128)}, bf16[4,112,576]{2,1,0:T(8,128)(2,1)}) custom-call(s32[3]{0:T(128)} %pad_add_fusion.refs_0_, bf16[4,384,768]{2,1,0:T(8,128)(2,1)} %get-tuple-element.100.refs_1_, bf16[384,576]{1,0:T(8,128)(2,1)} %get-tuple-element.94.refs_3_.refs_2_.refs_1_, bf16[384,576]{1,0:T(8,128)(2,1)} %get-tuple-element.95.refs_3_, ...), custom_call_target="tpu_custom_call" | custom-call | flops 9223999488 | bytes 6610956 | tf_op jit(solution)/shard_map/pallas_call | solution.py:742
  300.2 2.2 collective-permute-done.25
  302.4 1.4 add_convert_fusion
  304.3 6.2 %collective-permute-done.26.refs_9_ = bf16[2,112,576]{2,1,0:T(8,128)(2,1)S(1)} collective-permute-done((bf16[2,112,576]{2,1,0:T(8,128)(2,1)S(1)}, bf16[2,112,576]{2,1,0:T(8,128)(2,1)S(1)}, u32[]{:S(2)}, u32[]{:S(2)}) %collective-permute-start.26) | collective-permute-done | bytes 258080 | tf_op jit(solution)/shard_map/ppermute | solution.py:1159
  310.5 1.6 collective-permute-start.27
  312.2 3.5 collective-permute-done.27
  315.8 1.4 collective-permute-done.28
  317.3 1.8 collective-permute-start.31
  319.1 9.9 %collective-permute-start.30 = (bf16[2,112,576]{2,1,0:T(8,128)(2,1)S(1)}, bf16[2,112,576]{2,1,0:T(8,128)(2,1)S(1)}, u32[]{:S(2)}, u32[]{:S(2)}) collective-permute-start(bf16[2,112,576]{2,1,0:T(8,128)(2,1)S(1)} %pad_maximum_fusion.2.refs_1_), channel_id=1, source_target_pairs={{0,4},{1,5},{2,6},{3,7},{4,0},{5,1},{6,2},{7,3},{8,12},{9,13},{10,... | collective-permute-start | bytes 774152 | tf_op jit(solution)/shard_map/ppermute | solution.py:1159
  328.9 6.9 %shard_map.289.refs_5_ = f32[384,768]{1,0:T(8,128)} custom-call(s32[3]{0:T(128)} %pad_add_fusion.refs_0_, bf16[384,576]{1,0:T(8,128)(2,1)} %get-tuple-element.94.refs_3_.refs_2_.refs_1_, bf16[384,576]{1,0:T(8,128)(2,1)} %copy-done.5, bf16[384,576]{1,0:T(8,128)(2,1)} %copy-done.6, bf16[384,576]{1,0:T(8,128)(2,1)} %copy-done.7, ...), custom_call_target="tpu_custom_call" | custom-call | flops 5765000192 | bytes 8306700 | tf_op jit(solution)/shard_map/pallas_call | solution.py:742
  335.8 31.1 %collective-permute-done.30.refs_3_ = bf16[2,112,576]{2,1,0:T(8,128)(2,1)S(1)} collective-permute-done((bf16[2,112,576]{2,1,0:T(8,128)(2,1)S(1)}, bf16[2,112,576]{2,1,0:T(8,128)(2,1)S(1)}, u32[]{:S(2)}, u32[]{:S(2)}) %collective-permute-start.30) | collective-permute-done | bytes 258080 | tf_op jit(solution)/shard_map/ppermute | solution.py:1159
  366.9 0.7 copy-done.36
  367.6 0.7 copy-done.37
  368.3 3.0 shard_map.290
  371.3 23.7 %all-reduce.3.cloned.1.call-done = bf16[896,768]{1,0:T(8,128)(2,1)} async-done(((bf16[896,768]{1,0:T(8,128)(2,1)}), bf16[896,768]{1,0:T(8,128)(2,1)}) %all-reduce.3.cloned.1.call-update) | async-done | bytes 1376272 | tf_op jit(solution)/shard_map/psum | solution.py:1401
  395.0 1.3 fusion.4.refs_1_
  396.3 0.8 dynamic-slice_bitcast_fusion
  397.1 0.8 slice_reduce_fusion
  399.6 1.1 copy-done.25
  400.7 4.5 %shard_map.291 = (f32[768,768]{1,0:T(8,128)}, f32[192,3072]{1,0:T(8,128)}, f32[192,768]{1,0:T(8,128)}, f32[16,768]{1,0:T(8,128)}) custom-call(s32[3]{0:T(128)} %pad_add_fusion.refs_0_, bf16[896,768]{1,0:T(8,128)(2,1)} %fusion.4.refs_1_, bf16[896,768]{1,0:T(8,128)(2,1)} %copy-done.25), custom_call_target="tpu_custom_call" | custom-call | flops 2305999872 | bytes 8110092 | tf_op jit(solution)/shard_map/pallas_call | solution.py:742
  405.2 1.3 slice_reduce_fusion.1
  406.5 1.4 fusion.11
  (165 shorter events, 13.4 us)
Async XLA Ops:
  7.2 1.5 copy-start.8
  7.2 114.2 %all-gather.3.cloned.1.call-start = ((), (), s32[]{:S(2)}) async-start(), calls=%async_computation.1 | async-start | bytes 6635520 | tf_op jit(solution)/shard_map/all_gather | solution.py:1196
  8.7 1.4 copy-start.14
  8.7 1.5 copy-start.15
  8.7 1.5 copy-start.16
  8.7 1.5 copy-start.17
  8.7 1.5 copy-start.18
  8.8 1.5 copy-start.19
  8.8 1.5 copy-start.20
  8.8 1.5 copy-start.21
  8.8 1.5 copy-start.22
  8.8 1.7 copy-start.11
  10.4 10.4 %copy-start.13 = (bf16[16,192]{1,0:T(8,128)(2,1)}, bf16[16,192]{1,0:T(8,128)(2,1)S(1)}, u32[]{:S(2)}) copy-start(bf16[16,192]{1,0:T(8,128)(2,1)S(1)} %select_select_fusion.refs_6_) | copy-start | bytes 18436
  10.5 12.4 %copy-start.3 = (bf16[384,768]{1,0:T(8,128)(2,1)S(1)}, bf16[384,768]{1,0:T(8,128)(2,1)}, u32[]{:S(2)}) copy-start(bf16[384,768]{1,0:T(8,128)(2,1)} %refs_6_.3) | copy-start | bytes 1769476
  10.5 16.5 %copy-start.23 = (s32[1,8]{1,0:T(1,128)S(1)}, s32[1,8]{1,0:T(1,128)}, u32[]{:S(2)}) copy-start(s32[1,8]{1,0:T(1,128)} %param.32) | copy-start | bytes 100
  10.6 39.9 %copy-start.44 = (s32[1,3]{1,0:T(1,128)S(1)}, s32[1,3]{1,0:T(1,128)}, u32[]{:S(2)}) copy-start(s32[1,3]{1,0:T(1,128)} %param.33) | copy-start | bytes 40
  10.6 10.1 %collective-permute-start.4 = (bf16[112,2304]{1,0:T(8,128)(2,1)S(1)}, bf16[112,2304]{1,0:T(8,128)(2,1)S(1)}, u32[]{:S(2)}, u32[]{:S(2)}) collective-permute-start(bf16[112,2304]{1,0:T(8,128)(2,1)S(1)} %pad_maximum_fusion.1), channel_id=1, source_target_pairs={{0,8},{1,17},{2,10},{3,19},{4,12},{5,21},{6,14},{7,23},{8,0},{9,25... | collective-permute-start | bytes 1548296 | tf_op jit(solution)/shard_map/ppermute | solution.py:1159
  20.7 33.2 %copy-start.4 = (bf16[112,2304]{1,0:T(8,128)(2,1)}, bf16[112,2304]{1,0:T(8,128)(2,1)S(1)}, u32[]{:S(2)}) copy-start(bf16[112,2304]{1,0:T(8,128)(2,1)S(1)} %collective-permute-done.4.refs_7_) | copy-start | bytes 1548292
  20.8 29.0 %collective-permute-start.8 = (bf16[224,2304]{1,0:T(8,128)(2,1)S(1)}, bf16[224,2304]{1,0:T(8,128)(2,1)}, u32[]{:S(2)}, u32[]{:S(2)}) collective-permute-start(bf16[224,2304]{1,0:T(8,128)(2,1)S(1)} %pad_maximum_fusion), channel_id=1, source_target_pairs={{0,16},{1,9},{2,18},{3,11},{4,20},{5,13},{6,22},{7,15},{8,24},{9,1... | collective-permute-start | bytes 3096584 | tf_op jit(solution)/shard_map/ppermute | solution.py:1159
  22.9 28.6 %collective-permute-start.6 = (bf16[384,768]{1,0:T(8,128)(2,1)S(1)}, bf16[384,768]{1,0:T(8,128)(2,1)}, u32[]{:S(2)}, u32[]{:S(2)}) collective-permute-start(bf16[384,768]{1,0:T(8,128)(2,1)S(1)} %copy-done.3), channel_id=1, source_target_pairs={{0,2},{1,3},{2,0},{3,1},{4,6},{5,7},{6,4},{7,5},{8,10},{9,11},{10,... | collective-permute-start | bytes 1769480 | tf_op jit(solution)/shard_map/ppermute | solution.py:1159
  24.5 29.5 %collective-permute-start.2 = (bf16[384,768]{1,0:T(8,128)(2,1)S(1)}, bf16[384,768]{1,0:T(8,128)(2,1)S(1)}, u32[]{:S(2)}, u32[]{:S(2)}) collective-permute-start(bf16[384,768]{1,0:T(8,128)(2,1)S(1)} %copy-done.3), channel_id=1, source_target_pairs={{0,6},{1,7},{2,4},{3,5},{4,2},{5,3},{6,0},{7,1},{8,14},{9,15},{10,... | collective-permute-start | bytes 1769480 | tf_op jit(solution)/shard_map/ppermute | solution.py:1159
  26.9 50.0 %collective-permute-start = (bf16[384,768]{1,0:T(8,128)(2,1)S(1)}, bf16[384,768]{1,0:T(8,128)(2,1)}, u32[]{:S(2)}, u32[]{:S(2)}) collective-permute-start(bf16[384,768]{1,0:T(8,128)(2,1)S(1)} %copy-done.3), channel_id=1, source_target_pairs={{0,4},{1,5},{2,6},{3,7},{4,0},{5,1},{6,2},{7,3},{8,12},{9,13},{10,... | collective-permute-start | bytes 1769480 | tf_op jit(solution)/shard_map/ppermute | solution.py:1159
  49.8 27.7 %collective-permute-start.10 = (bf16[224,2304]{1,0:T(8,128)(2,1)}, bf16[224,2304]{1,0:T(8,128)(2,1)S(1)}, u32[]{:S(2)}, u32[]{:S(2)}) collective-permute-start(bf16[224,2304]{1,0:T(8,128)(2,1)} %collective-permute-done.8.refs_8_), channel_id=1, source_target_pairs={{0,1},{1,0},{2,3},{3,2},{4,5},{5,4},{6,7},{7,6},{8,9},{9,8},{10,11... | collective-permute-start | bytes 3096584 | tf_op jit(solution)/shard_map/ppermute | solution.py:1159
  50.9 26.6 %collective-permute-start.5 = (bf16[384,768]{1,0:T(8,128)(2,1)S(1)}, bf16[384,768]{1,0:T(8,128)(2,1)}, u32[]{:S(2)}, u32[]{:S(2)}) collective-permute-start(bf16[384,768]{1,0:T(8,128)(2,1)S(1)} %fusion.9), channel_id=1, source_target_pairs={{0,1},{1,0},{2,3},{3,2},{4,5},{5,4},{6,7},{7,6},{8,9},{9,8},{10,11... | collective-permute-start | bytes 1769480 | tf_op jit(solution)/shard_map/ppermute | solution.py:1159
  51.5 26.0 %collective-permute-start.7 = (bf16[384,768]{1,0:T(8,128)(2,1)}, bf16[384,768]{1,0:T(8,128)(2,1)}, u32[]{:S(2)}, u32[]{:S(2)}) collective-permute-start(bf16[384,768]{1,0:T(8,128)(2,1)} %collective-permute-done.6.refs_3_), channel_id=1, source_target_pairs={{0,1},{1,0},{2,3},{3,2},{4,5},{5,4},{6,7},{7,6},{8,9},{9,8},{10,11... | collective-permute-start | bytes 1769480 | tf_op jit(solution)/shard_map/ppermute | solution.py:1159
  53.9 34.2 %copy-start.28 = (bf16[384,768]{1,0:T(8,128)(2,1)}, bf16[384,768]{1,0:T(8,128)(2,1)S(1)}, u32[]{:S(2)}) copy-start(bf16[384,768]{1,0:T(8,128)(2,1)S(1)} %collective-permute-done.2.refs_3_) | copy-start | bytes 1769476
  53.9 23.0 %collective-permute-start.9 = (bf16[112,2304]{1,0:T(8,128)(2,1)S(1)}, bf16[112,2304]{1,0:T(8,128)(2,1)S(1)}, u32[]{:S(2)}, u32[]{:S(2)}) collective-permute-start(bf16[112,2304]{1,0:T(8,128)(2,1)S(1)} %collective-permute-done.4.refs_7_), channel_id=1, source_target_pairs={{0,1},{1,0},{2,3},{3,2},{4,5},{5,4},{6,7},{7,6},{8,9},{9,8},{10,11... | collective-permute-start | bytes 1548296 | tf_op jit(solution)/shard_map/ppermute | solution.py:1159
  77.0 11.1 %collective-permute-start.3 = (bf16[384,768]{1,0:T(8,128)(2,1)S(1)}, bf16[384,768]{1,0:T(8,128)(2,1)S(1)}, u32[]{:S(2)}, u32[]{:S(2)}) collective-permute-start(bf16[384,768]{1,0:T(8,128)(2,1)S(1)} %collective-permute-done.2.refs_3_), channel_id=1, source_target_pairs={{0,1},{1,0},{2,3},{3,2},{4,5},{5,4},{6,7},{7,6},{8,9},{9,8},{10,11... | collective-permute-start | bytes 1769480 | tf_op jit(solution)/shard_map/ppermute | solution.py:1159
  77.0 11.2 %collective-permute-start.1 = (bf16[384,768]{1,0:T(8,128)(2,1)}, bf16[384,768]{1,0:T(8,128)(2,1)S(1)}, u32[]{:S(2)}, u32[]{:S(2)}) collective-permute-start(bf16[384,768]{1,0:T(8,128)(2,1)} %collective-permute-done.refs_1_), channel_id=1, source_target_pairs={{0,1},{1,0},{2,3},{3,2},{4,5},{5,4},{6,7},{7,6},{8,9},{9,8},{10,11... | collective-permute-start | bytes 1769480 | tf_op jit(solution)/shard_map/ppermute | solution.py:1159
  88.1 1.5 copy-start.29
  88.1 1.5 copy-start.30
  122.6 23.6 %collective-permute-start.14 = (bf16[4,864,768]{2,1,0:T(8,128)(2,1)}, bf16[4,864,768]{2,1,0:T(8,128)(2,1)}, u32[]{:S(2)}, u32[]{:S(2)}) collective-permute-start(bf16[4,864,768]{2,1,0:T(8,128)(2,1)} %fusion.7.refs_9_), channel_id=1, source_target_pairs={{0,1},{1,0},{2,3},{3,2},{4,5},{5,4},{6,7},{7,6},{8,9},{9,8},{10,11... | collective-permute-start | bytes 15925256 | tf_op jit(solution)/shard_map/ppermute | solution.py:1159
  128.3 10.6 %collective-permute-start.11 = (bf16[384,192]{1,0:T(8,128)(2,1)}, bf16[384,192]{1,0:T(8,128)(2,1)S(1)}, u32[]{:S(2)}, u32[]{:S(2)}) collective-permute-start(bf16[384,192]{1,0:T(8,128)(2,1)} %get-tuple-element.76), channel_id=1, source_target_pairs={{0,2},{1,3},{2,0},{3,1},{4,6},{5,7},{6,4},{7,5},{8,10},{9,11},{10,... | collective-permute-start | bytes 442376 | tf_op jit(solution)/shard_map/ppermute | solution.py:1159
  128.3 17.9 %collective-permute-start.12 = (bf16[384,192]{1,0:T(8,128)(2,1)}, bf16[384,192]{1,0:T(8,128)(2,1)S(1)}, u32[]{:S(2)}, u32[]{:S(2)}) collective-permute-start(bf16[384,192]{1,0:T(8,128)(2,1)} %get-tuple-element.77), channel_id=1, source_target_pairs={{0,4},{1,5},{2,6},{3,7},{4,0},{5,1},{6,2},{7,3},{8,12},{9,13},{10,... | collective-permute-start | bytes 442376 | tf_op jit(solution)/shard_map/ppermute | solution.py:1159
  131.8 14.4 %collective-permute-start.13 = (bf16[384,192]{1,0:T(8,128)(2,1)}, bf16[384,192]{1,0:T(8,128)(2,1)S(1)}, u32[]{:S(2)}, u32[]{:S(2)}) collective-permute-start(bf16[384,192]{1,0:T(8,128)(2,1)} %get-tuple-element.78), channel_id=1, source_target_pairs={{0,6},{1,7},{2,4},{3,5},{4,2},{5,3},{6,0},{7,1},{8,14},{9,15},{10,... | collective-permute-start | bytes 442376 | tf_op jit(solution)/shard_map/ppermute | solution.py:1159
  138.9 7.3 %copy-start.39 = (bf16[384,192]{1,0:T(8,128)(2,1)}, bf16[384,192]{1,0:T(8,128)(2,1)S(1)}, u32[]{:S(2)}) copy-start(bf16[384,192]{1,0:T(8,128)(2,1)S(1)} %collective-permute-done.11.refs_2_) | copy-start | bytes 442372
  168.7 13.3 %collective-permute-start.22 = (bf16[384,5760]{1,0:T(8,128)(2,1)}, bf16[384,5760]{1,0:T(8,128)(2,1)S(1)}, u32[]{:S(2)}, u32[]{:S(2)}) collective-permute-start(bf16[384,5760]{1,0:T(8,128)(2,1)} %get-tuple-element.102), channel_id=1, source_target_pairs={{0,1},{1,0},{2,3},{3,2},{4,5},{5,4},{6,7},{7,6},{8,9},{9,8},{10,11... | collective-permute-start | bytes 13271048 | tf_op jit(solution)/shard_map/ppermute | solution.py:1159
  168.8 13.2 %collective-permute-start.15 = (bf16[384,192]{1,0:T(8,128)(2,1)}, bf16[384,192]{1,0:T(8,128)(2,1)S(1)}, u32[]{:S(2)}, u32[]{:S(2)}) collective-permute-start(bf16[384,192]{1,0:T(8,128)(2,1)} %get-tuple-element.86), channel_id=1, source_target_pairs={{0,2},{1,3},{2,0},{3,1},{4,6},{5,7},{6,4},{7,5},{8,10},{9,11},{10,... | collective-permute-start | bytes 442376 | tf_op jit(solution)/shard_map/ppermute | solution.py:1159
  172.6 25.5 %collective-permute-start.16 = (bf16[384,192]{1,0:T(8,128)(2,1)}, bf16[384,192]{1,0:T(8,128)(2,1)S(1)}, u32[]{:S(2)}, u32[]{:S(2)}) collective-permute-start(bf16[384,192]{1,0:T(8,128)(2,1)} %get-tuple-element.87), channel_id=1, source_target_pairs={{0,4},{1,5},{2,6},{3,7},{4,0},{5,1},{6,2},{7,3},{8,12},{9,13},{10,... | collective-permute-start | bytes 442376 | tf_op jit(solution)/shard_map/ppermute | solution.py:1159
  173.6 24.5 %collective-permute-start.17 = (bf16[384,192]{1,0:T(8,128)(2,1)}, bf16[384,192]{1,0:T(8,128)(2,1)S(1)}, u32[]{:S(2)}, u32[]{:S(2)}) collective-permute-start(bf16[384,192]{1,0:T(8,128)(2,1)} %get-tuple-element.88), channel_id=1, source_target_pairs={{0,6},{1,7},{2,4},{3,5},{4,2},{5,3},{6,0},{7,1},{8,14},{9,15},{10,... | collective-permute-start | bytes 442376 | tf_op jit(solution)/shard_map/ppermute | solution.py:1159
  182.0 2.1 copy-start.24
  197.6 44.9 %collective-permute-start.23 = (bf16[2,896,768]{2,1,0:T(8,128)(2,1)}, bf16[2,896,768]{2,1,0:T(8,128)(2,1)S(1)}, u32[]{:S(2)}, u32[]{:S(2)}) collective-permute-start(bf16[2,896,768]{2,1,0:T(8,128)(2,1)} %get-tuple-element.105), channel_id=1, source_target_pairs={{0,8},{1,17},{2,10},{3,19},{4,12},{5,21},{6,14},{7,23},{8,0},{9,25... | collective-permute-start | bytes 8257544 | tf_op jit(solution)/shard_map/ppermute | solution.py:1159
  229.1 8.6 %collective-permute-start.18 = (bf16[4,384,384]{2,1,0:T(8,128)(2,1)}, bf16[4,384,384]{2,1,0:T(8,128)(2,1)S(1)}, u32[]{:S(2)}, u32[]{:S(2)}) collective-permute-start(bf16[4,384,384]{2,1,0:T(8,128)(2,1)} %get-tuple-element.93), channel_id=1, source_target_pairs={{0,1},{1,0},{2,3},{3,2},{4,5},{5,4},{6,7},{7,6},{8,9},{9,8},{10,11... | collective-permute-start | bytes 3538952 | tf_op jit(solution)/shard_map/ppermute | solution.py:1159
  242.5 1.5 copy-start
  244.0 4.6 %copy-start.32 = (bf16[384,576]{1,0:T(8,128)(2,1)S(1)}, bf16[384,576]{1,0:T(8,128)(2,1)}, u32[]{:S(2)}) copy-start(bf16[384,576]{1,0:T(8,128)(2,1)} %get-tuple-element.95.refs_3_) | copy-start | bytes 1327108
  244.0 4.6 %copy-start.33 = (bf16[384,576]{1,0:T(8,128)(2,1)S(1)}, bf16[384,576]{1,0:T(8,128)(2,1)}, u32[]{:S(2)}) copy-start(bf16[384,576]{1,0:T(8,128)(2,1)} %get-tuple-element.96.refs_4_) | copy-start | bytes 1327108
  244.0 6.9 %copy-start.34 = (bf16[384,576]{1,0:T(8,128)(2,1)S(1)}, bf16[384,576]{1,0:T(8,128)(2,1)}, u32[]{:S(2)}) copy-start(bf16[384,576]{1,0:T(8,128)(2,1)} %get-tuple-element.97.refs_5_) | copy-start | bytes 1327108
  248.1 36.7 %collective-permute-start.24 = (bf16[896,768]{1,0:T(8,128)(2,1)}, bf16[896,768]{1,0:T(8,128)(2,1)S(1)}, u32[]{:S(2)}, u32[]{:S(2)}) collective-permute-start(bf16[896,768]{1,0:T(8,128)(2,1)} %shard_map.286), channel_id=1, source_target_pairs={{0,16},{1,9},{2,18},{3,11},{4,20},{5,13},{6,22},{7,15},{8,24},{9,1... | collective-permute-start | bytes 4128776 | tf_op jit(solution)/shard_map/ppermute | solution.py:1159
  248.6 22.8 %collective-permute-start.19 = (bf16[384,576]{1,0:T(8,128)(2,1)S(1)}, bf16[384,576]{1,0:T(8,128)(2,1)S(1)}, u32[]{:S(2)}, u32[]{:S(2)}) collective-permute-start(bf16[384,576]{1,0:T(8,128)(2,1)S(1)} %copy-done.32), channel_id=1, source_target_pairs={{0,2},{1,3},{2,0},{3,1},{4,6},{5,7},{6,4},{7,5},{8,10},{9,11},{10,... | collective-permute-start | bytes 1327112 | tf_op jit(solution)/shard_map/ppermute | solution.py:1159
  248.6 36.1 %collective-permute-start.20 = (bf16[384,576]{1,0:T(8,128)(2,1)S(1)}, bf16[384,576]{1,0:T(8,128)(2,1)S(1)}, u32[]{:S(2)}, u32[]{:S(2)}) collective-permute-start(bf16[384,576]{1,0:T(8,128)(2,1)S(1)} %copy-done.33), channel_id=1, source_target_pairs={{0,4},{1,5},{2,6},{3,7},{4,0},{5,1},{6,2},{7,3},{8,12},{9,13},{10,... | collective-permute-start | bytes 1327112 | tf_op jit(solution)/shard_map/ppermute | solution.py:1159
  250.9 33.9 %collective-permute-start.21 = (bf16[384,576]{1,0:T(8,128)(2,1)S(1)}, bf16[384,576]{1,0:T(8,128)(2,1)S(1)}, u32[]{:S(2)}, u32[]{:S(2)}) collective-permute-start(bf16[384,576]{1,0:T(8,128)(2,1)S(1)} %copy-done.34), channel_id=1, source_target_pairs={{0,6},{1,7},{2,4},{3,5},{4,2},{5,3},{6,0},{7,1},{8,14},{9,15},{10,... | collective-permute-start | bytes 1327112 | tf_op jit(solution)/shard_map/ppermute | solution.py:1159
  271.5 13.3 %copy-start.5 = (bf16[384,576]{1,0:T(8,128)(2,1)}, bf16[384,576]{1,0:T(8,128)(2,1)S(1)}, u32[]{:S(2)}) copy-start(bf16[384,576]{1,0:T(8,128)(2,1)S(1)} %collective-permute-done.19.refs_4_.refs_10_.refs_2_) | copy-start | bytes 1327108
  300.2 94.8 %all-reduce.3.cloned.1.call-start = ((), (), s32[]{:S(2)}) async-start(), calls=%async_computation | async-start | bytes 2752512 | tf_op jit(solution)/shard_map/psum | solution.py:1401
  300.2 2.2 collective-permute-start.25
  303.8 6.7 %collective-permute-start.26 = (bf16[2,112,576]{2,1,0:T(8,128)(2,1)S(1)}, bf16[2,112,576]{2,1,0:T(8,128)(2,1)S(1)}, u32[]{:S(2)}, u32[]{:S(2)}) collective-permute-start(bf16[2,112,576]{2,1,0:T(8,128)(2,1)S(1)} %slice.110), channel_id=1, source_target_pairs={{0,8},{1,17},{2,10},{3,19},{4,12},{5,21},{6,14},{7,23},{8,0},{9,25... | collective-permute-start | bytes 774152 | tf_op jit(solution)/shard_map/ppermute | solution.py:1159
  310.5 18.4 %copy-start.9 = (bf16[2,112,576]{2,1,0:T(8,128)(2,1)}, bf16[2,112,576]{2,1,0:T(8,128)(2,1)S(1)}, u32[]{:S(2)}) copy-start(bf16[2,112,576]{2,1,0:T(8,128)(2,1)S(1)} %collective-permute-done.26.refs_9_) | copy-start | bytes 774148
  310.5 5.2 %collective-permute-start.27 = (bf16[112,576]{1,0:T(8,128)(2,1)S(1)}, bf16[112,576]{1,0:T(8,128)(2,1)S(1)}, u32[]{:S(2)}, u32[]{:S(2)}) collective-permute-start(bf16[112,576]{1,0:T(8,128)(2,1)S(1)} %fusion.2), channel_id=1, source_target_pairs={{0,16},{1,9},{2,18},{3,11},{4,20},{5,13},{6,22},{7,15},{8,24},{9,1... | collective-permute-start | bytes 387080 | tf_op jit(solution)/shard_map/ppermute | solution.py:1159
  315.8 1.4 collective-permute-start.28
  317.2 18.6 %copy-start.10 = (bf16[2,112,576]{2,1,0:T(8,128)(2,1)}, bf16[2,112,576]{2,1,0:T(8,128)(2,1)S(1)}, u32[]{:S(2)}) copy-start(bf16[2,112,576]{2,1,0:T(8,128)(2,1)S(1)} %pad_maximum_fusion.2.refs_1_) | copy-start | bytes 774148
  317.3 18.6 %collective-permute-start.31 = (bf16[2,112,576]{2,1,0:T(8,128)(2,1)S(1)}, bf16[2,112,576]{2,1,0:T(8,128)(2,1)S(1)}, u32[]{:S(2)}, u32[]{:S(2)}) collective-permute-start(bf16[2,112,576]{2,1,0:T(8,128)(2,1)S(1)} %pad_maximum_fusion.2.refs_1_), channel_id=1, source_target_pairs={{0,6},{1,7},{2,4},{3,5},{4,2},{5,3},{6,0},{7,1},{8,14},{9,15},{10,... | collective-permute-start | bytes 774152 | tf_op jit(solution)/shard_map/ppermute | solution.py:1159
  319.1 47.8 %collective-permute-start.30 = (bf16[2,112,576]{2,1,0:T(8,128)(2,1)S(1)}, bf16[2,112,576]{2,1,0:T(8,128)(2,1)S(1)}, u32[]{:S(2)}, u32[]{:S(2)}) collective-permute-start(bf16[2,112,576]{2,1,0:T(8,128)(2,1)S(1)} %pad_maximum_fusion.2.refs_1_), channel_id=1, source_target_pairs={{0,4},{1,5},{2,6},{3,7},{4,0},{5,1},{6,2},{7,3},{8,12},{9,13},{10,... | collective-permute-start | bytes 774152 | tf_op jit(solution)/shard_map/ppermute | solution.py:1159
  328.9 38.0 %collective-permute-start.29 = (bf16[2,112,576]{2,1,0:T(8,128)(2,1)S(1)}, bf16[2,112,576]{2,1,0:T(8,128)(2,1)S(1)}, u32[]{:S(2)}, u32[]{:S(2)}) collective-permute-start(bf16[2,112,576]{2,1,0:T(8,128)(2,1)S(1)} %pad_maximum_fusion.2.refs_1_), channel_id=1, source_target_pairs={{0,2},{1,3},{2,0},{3,1},{4,6},{5,7},{6,4},{7,5},{8,10},{9,11},{10,... | collective-permute-start | bytes 774152 | tf_op jit(solution)/shard_map/ppermute | solution.py:1159
  335.8 31.1 %copy-start.35 = (bf16[2,112,576]{2,1,0:T(8,128)(2,1)}, bf16[2,112,576]{2,1,0:T(8,128)(2,1)S(1)}, u32[]{:S(2)}) copy-start(bf16[2,112,576]{2,1,0:T(8,128)(2,1)S(1)} %collective-permute-done.31.refs_4_) | copy-start | bytes 774148
  396.3 3.3 collective-permute-start.32
  (16 other events, 14.0 us)
Sparse Core Ops, SparseCore 0:
  10.4 71.7 all-gather.2
  304.4 90.5 all-reduce.2

commit v3 on v1

--- a/solution.py
+++ b/solution.py
@@ -481,13 +481,8 @@
     t2,
     t3,
     w_ref,
-    smalls_ref,
-    near_ref,
-    across_ref,
-    far_ref,
-    near_other,
-    across_other,
-    far_other,
+    halves_ref,
+    others_ref,
     q,
     k,
     kt,
@@ -500,23 +495,14 @@
     wv,
     small_ref,
 ):
-    part, core, chip = where[0], where[1], where[2]
-    near, across = 1 + core, 2 - core
+    core, chip = where[1], where[2]
     shard, wide = w_ref.shape
     features, half, width = wide // 3, shard // 2, wq.shape[1]
-    full_ref[pl.ds(pl.multiple_of(part * shard, 16), shard), :] = w_ref[...]
-    small_ref[part] = smalls_ref[...].astype(FP32)
-    for ref, owner in ((near_ref, part ^ near), (across_ref, part ^ across), (far_ref, part ^ 3)):
-        first = pl.multiple_of(owner * shard + core * half, 16)
-        full_ref[pl.ds(first, half), :] = ref[0:half, :]
-        small_ref[owner] = ref[half:, 0:width].astype(FP32)
-    for ref, owner in (
-        (near_other, part ^ across),
-        (across_other, part ^ near),
-        (far_other, part ^ 3),
-    ):
-        first = pl.multiple_of(owner * shard + (1 - core) * half, 16)
-        full_ref[pl.ds(first, half), :] = ref[0:half, :]
+    for f in range(halves_ref.shape[0]):
+        for ref, which in ((halves_ref, core), (others_ref, 1 - core)):
+            first = pl.multiple_of(f * shard + which * half, 16)
+            full_ref[pl.ds(first, half), :] = ref[f, 0:half, :]
+        small_ref[f] = halves_ref[f, half:, 0:width].astype(FP32)
     for z in range(features // width):
 
         @pl.when(chip == z)
@@ -728,7 +714,7 @@
     lax.fori_loop(0, blocks, write_block, 0)
 
 
-def kernel_call(kernel, outputs, scratch, operands, cost, special={}, after=()):
+def kernel_call(kernel, outputs, scratch, operands, cost, special={}, after=(), grid=()):
     whole = pl.BlockSpec(memory_space=pltpu.VMEM)
     in_specs = [pl.BlockSpec(memory_space=pltpu.SMEM)]
     in_specs += [special.get(n, whole) for n in range(1, len(operands))]
@@ -741,6 +727,7 @@
     moved = sum(v.size * v.dtype.itemsize for v in list(operands) + list(outputs))
     return pl.pallas_call(
         ordered,
+        grid=grid,
         out_shape=outputs,
         in_specs=in_specs,
         out_specs=[pl.BlockSpec(memory_space=pltpu.VMEM) for unused in outputs],
@@ -1026,7 +1013,7 @@
 
 
 def relay_kernel(where, keep_ref, theirs_ref, relay_ref):
-    relay_ref[...] = (keep_ref[1].astype(FP32) + theirs_ref[1].astype(FP32)).astype(BF16)
+    relay_ref[...] = (keep_ref[0].astype(FP32) + theirs_ref[0].astype(FP32)).astype(BF16)
 
 
 def pair_kernel(where, keep_ref, theirs_ref, last_ref, stay_ref, give_ref):
@@ -1179,6 +1166,7 @@
     part = lax.axis_index("fsdp")
     near = 1 + core
     across = 2 - core
+    same_core = [[2 * z + k for z in range(chips)] for k in range(2)]
     where = jnp.stack([part, core, chip]).astype(jnp.int32)
 
     def exchange(value, partner):
@@ -1271,10 +1259,8 @@
         ],
         axis=0,
     )
-    from_near, from_across = to_near(mine), to_across(mine)
-    from_far = to_across(from_near)
-    gathered = (from_near, from_across, from_far)
-    gathered += tuple(to_core(v) for v in gathered)
+    gathered = lax.all_gather(mine, "fsdp", axis=0)
+    gathered = (gathered, to_core(gathered))
     *half_stores, qkv_full, weight_q, weight_k, weight_v, small_all = kernel_call(
         project_kernel,
         [
@@ -1291,7 +1277,7 @@
             jax.ShapeDtypeStruct((fsdp, 16, width), FP32),
         ],
         [],
-        (where, blocks[0], beside[0], blocks[1], beside[1], w_qkv, smalls) + gathered,
+        (where, blocks[0], beside[0], blocks[1], beside[1], w_qkv) + gathered,
         9,
     )
     queries, keys, keys_t, values, normed_mine, *rest = kernel_call(
@@ -1419,69 +1405,39 @@
     def add_up(left_side, right_side):
         return left_side.astype(FP32) + right_side.astype(FP32)
 
-    def scatter_parts(keep, send):
-        theirs = to_near(send)
-        last = to_across(add_up(keep[1], theirs[1]).astype(BF16))
-        return (add_up(keep[0], theirs[0]) + last.astype(FP32)).astype(BF16)
-
     arrived = swap_chips(packed)
     theirs = to_near(grads_send)
     block = jax.ShapeDtypeStruct((block_rows, features), BF16)
 
+    def one_of(slot):
+        spec = pl.BlockSpec((1, block_rows, features), lambda step: (slot, 0, 0))
+        return {1: spec, 2: spec}
+
+    (relay,) = kernel_call(
+        relay_kernel,
+        [block],
+        [],
+        (where, grads_keep, theirs),
+        1,
+        special=one_of(1),
+        grid=(1,),
+        after=(packed[0],),
+    )
+
     def shaped(count, dtype):
         return jax.ShapeDtypeStruct((count, features), dtype)
 
-    (relay,) = kernel_call(
-        relay_kernel, [block], [], (where, grads_keep, theirs), 1, after=(packed[0],)
-    )
     stay, give = kernel_call(
         pair_kernel,
         [shaped(block_rows // 2, FP32), shaped(block_rows // 2, BF16)],
         [],
         (where, grads_keep, theirs, to_across(relay)),
         2,
+        special=one_of(0),
+        grid=(1,),
         after=tuple(arrived[1:]),
     )
-    stay, give = kernel_call(
-        quad_kernel,
-        [shaped(block_rows // 4, FP32), shaped(block_rows // 4, BF16)],
-        [],
-        (where, stay, to_first(give)),
-        2,
-    )
-    (grad_tokens,) = kernel_call(
-        input_grad_kernel,
-        [jax.ShapeDtypeStruct((rows, features), FP32)],
-        [pltpu.VMEM((rows, 3 * features), BF16)],
-        tuple([where] + arrived) + (qkv_full, tokens, grad_middle, small_all),
-        5,
-        after=(give,),
-    )
-
-    (quad,) = kernel_call(
-        total_kernel, [shaped(block_rows // 4, BF16)], [], (where, stay, to_second(give)), 1
-    )
-    (joined,) = kernel_call(
-        join_kernel, [shaped(block_rows // 2, BF16)], [], (where, quad, to_second(quad)), 1
-    )
-    joined_next = to_first(joined)
-    d_proj, d_fc, d_out, small_sums = kernel_call(
-        output_kernel,
-        [
-            jax.ShapeDtypeStruct((columns, features), FP32),
-            jax.ShapeDtypeStruct((shard, hidden_width), FP32),
-            jax.ShapeDtypeStruct((shard, features), FP32),
-            jax.ShapeDtypeStruct((16, features), FP32),
-        ],
-        [pltpu.VMEM((block_rows, features), BF16), pltpu.VMEM((block_rows, features), BF16)],
-        (where, joined, joined_next, to_core(joined), to_core(joined_next)),
-        2,
-    )
-    d_bias_out, d_bias_proj, d_gain_two, d_shift_two = (
-        small_sums[0, n * shard : (n + 1) * shard] for n in range(4)
-    )
-    d_bias_fc = small_sums[1]
-
+    given = give
     block_shape = (fsdp, half + 16, 3 * width)
     qkv_keep, qkv_send = kernel_call(
         qkv_grad_kernel,
@@ -1497,10 +1453,30 @@
             small_all,
         ),
         8,
-        after=tuple(arrived[1:]) + (give,),
-    )
+        after=tuple(arrived[1:]) + (given,),
+    )
+    stay, give = kernel_call(
+        quad_kernel,
+        [shaped(block_rows // 4, FP32), shaped(block_rows // 4, BF16)],
+        [],
+        (where, stay, to_first(give)),
+        1,
+        after=(qkv_keep,),
+    )
+    given = give
     qkv_blocks = add_up(qkv_keep, to_core(qkv_send)).astype(BF16)
-    qkv_half = scatter_parts(qkv_blocks[:2], qkv_blocks[2:])
+    theirs_qkv = to_near(qkv_blocks[2:])
+    last_qkv = to_across(add_up(qkv_blocks[1], theirs_qkv[1]).astype(BF16))
+    qkv_half = (add_up(qkv_blocks[0], theirs_qkv[0]) + last_qkv.astype(FP32)).astype(BF16)
+    (grad_tokens,) = kernel_call(
+        input_grad_kernel,
+        [jax.ShapeDtypeStruct((rows, features), FP32)],
+        [pltpu.VMEM((rows, 3 * features), BF16)],
+        tuple([where] + arrived) + (qkv_full, tokens, grad_middle, small_all),
+        5,
+        after=(given,),
+    )
+
     halves = swap_chips([jnp.stack([qkv_half, to_core(qkv_half)])] * 4)
     d_qkv, extra = kernel_call(
         qkv_output_kernel,
@@ -1512,6 +1488,30 @@
         tuple([where] + halves),
         2,
     )
+    (quad,) = kernel_call(
+        total_kernel, [shaped(block_rows // 4, BF16)], [], (where, stay, to_second(give)), 1
+    )
+    (joined,) = kernel_call(
+        join_kernel, [shaped(block_rows // 2, BF16)], [], (where, quad, to_second(quad)), 1
+    )
+    joined_next = to_first(joined)
+    d_proj, d_fc, d_out, small_sums = kernel_call(
+        output_kernel,
+        [
+            jax.ShapeDtypeStruct((columns, features), FP32),
+            jax.ShapeDtypeStruct((shard, hidden_width), FP32),
+            jax.ShapeDtypeStruct((shard, features), FP32),
+            jax.ShapeDtypeStruct((16, features), FP32),
+        ],
+        [pltpu.VMEM((block_rows, features), BF16), pltpu.VMEM((block_rows, features), BF16)],
+        (where, joined, joined_next, to_core(joined), to_core(joined_next)),
+        2,
+    )
+    d_bias_out, d_bias_proj, d_gain_two, d_shift_two = (
+        small_sums[0, n * shard : (n + 1) * shard] for n in range(4)
+    )
+    d_bias_fc = small_sums[1]
+
     owner_extra = pick(extra, part)
     d_bias_q = owner_extra[2, :width]
     d_bias_v = owner_extra[2, 2 * width :]

time: 423 us -> 448 us (1.059)
  waiting for transfers between devices: 141 us -> 189 us
  starting transfers between devices: 78.8 us -> 52.9 us
    all_gather x0 -> x1, waiting for transfers between devices: none -> 32.8 us  [fast_body(): gathered = lax.all_gather(mine, 'fsdp', axis=0)]
    ppermute x40 -> x35, starting transfers between devices: 78.7 us -> 52.8 us  [exchange(): return lax.ppermute(value, ('fsdp', 'ctx'), pairs)]
    ppermute x40 -> x35, waiting for transfers between devices: 141 us -> 156 us  [exchange(): return lax.ppermute(value, ('fsdp', 'ctx'), pairs)]
    unnamed x112 -> x82, local copies, waits for them, and re-layouts: 17.8 us -> 19.5 us
  transfers between devices with their start and end apart: 41 -> 37, of which waited for: 17 -> 15; matrix products, arithmetic and copies ran while one was open for 3% -> 3% of each run, Pallas kernels for 25% -> 24%
where the time goes in v3:
time: 448 us; the launch traced here: 443 us
  waiting for transfers between devices  189 us (42%)
  Pallas kernels  147 us (33%)
  starting transfers between devices  52.9 us (12%)
  local copies, waits for them, and re-layouts  29.4 us (7%)
  between operations  14.8 us (3%)
  other arithmetic  9.89 us (2%)
    ppermute x35, waiting for transfers between devices, exchange(): return lax.ppermute(value, ('fsdp', 'ctx'), pairs)  156 us
    pallas_call x15, Pallas kernels, kernel_call(): pl.pallas_call(ordered, grid=grid, out_shape=outputs, in_specs=in_specs,...  147 us
    ppermute x35, starting transfers between devices, exchange(): return lax.ppermute(value, ('fsdp', 'ctx'), pairs)  52.8 us
    all_gather x1, waiting for transfers between devices, fast_body(): gathered = lax.all_gather(mine, 'fsdp', axis=0)  32.8 us
    unnamed x82, local copies, waits for them, and re-layouts  19.5 us
  transfers between devices with their start and end apart: 37, of which 15 were waited for; matrix products, arithmetic and copies ran while one was open for 3% of the time, Pallas kernels for 24%

profile of v3, /device:TPU:0, one launch (start us, length us, event | category | flops | bytes accessed | tf_op | source)
XLA Modules:
  0.0 443.2 jit_solution(8309415694709161768)
XLA Ops:
  8.2 1.0 constant_dynamic-slice_fusion.3
  11.2 1.0 dynamic-slice_dynamic-update-slice_fusion.4
  12.2 0.9 dynamic-slice_dynamic-update-slice_fusion.3
  13.2 0.9 dynamic-slice_dynamic-update-slice_fusion.2
  14.1 0.9 dynamic-slice_dynamic-update-slice_fusion.1
  15.0 1.1 copy-done
  16.1 32.8 %all-gather.5.cloned.1.call-done = bf16[448,2304]{1,0:T(8,128)(2,1)} async-done(((bf16[112,2304]{1,0:T(8,128)(2,1)}), bf16[448,2304]{1,0:T(8,128)(2,1)}) %all-gather.5.cloned.1.call-update) | async-done | bytes 2064400 | tf_op jit(solution)/shard_map/all_gather | solution.py:1262
  48.9 1.5 collective-permute-start.5
  50.6 2.4 collective-permute-start.2
  54.9 9.8 %collective-permute-done.5.refs_3_ = bf16[384,768]{1,0:T(8,128)(2,1)} collective-permute-done((bf16[384,768]{1,0:T(8,128)(2,1)S(1)}, bf16[384,768]{1,0:T(8,128)(2,1)}, u32[]{:S(2)}, u32[]{:S(2)}) %collective-permute-start.5) | collective-permute-done | bytes 589856 | tf_op jit(solution)/shard_map/ppermute | solution.py:1179
  67.0 12.7 %collective-permute-done.2.refs_3_ = bf16[384,768]{1,0:T(8,128)(2,1)S(1)} collective-permute-done((bf16[384,768]{1,0:T(8,128)(2,1)S(1)}, bf16[384,768]{1,0:T(8,128)(2,1)S(1)}, u32[]{:S(2)}, u32[]{:S(2)}) %collective-permute-start.2) | collective-permute-done | bytes 589856 | tf_op jit(solution)/shard_map/ppermute | solution.py:1179
  79.6 25.2 %collective-permute-done.refs_1_ = bf16[384,768]{1,0:T(8,128)(2,1)} collective-permute-done((bf16[384,768]{1,0:T(8,128)(2,1)S(1)}, bf16[384,768]{1,0:T(8,128)(2,1)}, u32[]{:S(2)}, u32[]{:S(2)}) %collective-permute-start) | collective-permute-done | bytes 589856 | tf_op jit(solution)/shard_map/ppermute | solution.py:1179
  104.9 1.3 copy-done.7
  106.2 9.7 %shard_map.280 = (bf16[2,384,192]{2,1,0:T(8,128)(2,1)}, bf16[4,384,192]{2,1,0:T(8,128)(2,1)}, bf16[4,192,384]{2,1,0:T(8,128)(2,1)}, bf16[4,384,192]{2,1,0:T(8,12...) custom-call(s32[3]{0:T(128)} %pad_add_fusion.refs_0_, ...), custom_call_target="tpu_custom_call" | custom-call | flops 10376999936 | bytes 15679500 | tf_op jit(solution)/shard_map/pallas_call | solution.py:728
  115.9 1.5 broadcast_in_dim.126.refs_15_.refs_9_
  117.4 31.7 %shard_map.281 = (bf16[4,384,192]{2,1,0:T(8,128)(2,1)}, bf16[8,384,192]{2,1,0:T(8,128)(2,1)}, bf16[8,192,384]{2,1,0:T(8,128)(2,1)}, bf16[8,384,192]{2,1,0:T(8,12...) custom-call(s32[3]{0:T(128)} %pad_add_fusion.refs_0_, ...), custom_call_target="tpu_custom_call" | custom-call | flops 34589999104 | bytes 17029132 | tf_op jit(solution)/shard_map/pallas_call | solution.py:728
  149.2 1.3 fusion.8.refs_9_
  150.4 5.6 %collective-permute-start.11 = (bf16[4,864,768]{2,1,0:T(8,128)(2,1)}, bf16[4,864,768]{2,1,0:T(8,128)(2,1)}, u32[]{:S(2)}, u32[]{:S(2)}) collective-permute-start(bf16[4,864,768]{2,1,0:T(8,128)(2,1)} %fusion.8.refs_9_), channel_id=1, source_target_pairs={{0,1},{1,0},{2,3},{3,2},{4,5},{5,4},{6,7},{7,6},{8,9},{9,8},{10,11... | collective-permute-start | bytes 15925256 | tf_op jit(solution)/shard_map/ppermute | solution.py:1179
  156.1 3.5 collective-permute-start.9
  161.0 1.3 fusion.3.refs_7_
  162.4 4.3 collective-permute-done.8.refs_2_
  166.7 7.3 %collective-permute-done.9.refs_3_ = bf16[384,192]{1,0:T(8,128)(2,1)S(1)} collective-permute-done((bf16[384,192]{1,0:T(8,128)(2,1)}, bf16[384,192]{1,0:T(8,128)(2,1)S(1)}, u32[]{:S(2)}, u32[]{:S(2)}) %collective-permute-start.9) | collective-permute-done | bytes 147488 | tf_op jit(solution)/shard_map/ppermute | solution.py:1179
  174.7 21.7 %shard_map.282 = (bf16[384,768]{1,0:T(8,128)(2,1)}, f32[384,768]{1,0:T(8,128)}, bf16[384,192]{1,0:T(8,128)(2,1)}, bf16[384,192]{1,0:T(8,128)(2,1)}, bf16[384,192...) custom-call(s32[3]{0:T(128)} %pad_add_fusion.refs_0_, ...), custom_call_target="tpu_custom_call" | custom-call | flops 24213000192 | bytes 23840268 | tf_op jit(solution)/shard_map/pallas_call | solution.py:728
  196.5 3.8 collective-permute-start.12
  200.4 1.0 collective-permute-start.13
  201.3 1.5 collective-permute-start.14
  202.8 7.0 %collective-permute-done.12.refs_6_.refs_4_ = bf16[384,192]{1,0:T(8,128)(2,1)S(1)} collective-permute-done((bf16[384,192]{1,0:T(8,128)(2,1)}, bf16[384,192]{1,0:T(8,128)(2,1)S(1)}, u32[]{:S(2)}, u32[]{:S(2)}) %collective-permute-start.12) | collective-permute-done | bytes 147488 | tf_op jit(solution)/shard_map/ppermute | solution.py:1179
  210.4 1.5 copy-done.6
  211.9 13.4 %shard_map.285 = (bf16[2,896,768]{2,1,0:T(8,128)(2,1)}, bf16[2,896,768]{2,1,0:T(8,128)(2,1)}) custom-call(s32[3]{0:T(128)} %pad_add_fusion.refs_0_, bf16[384,5760]{1,0:T(8,128)(2,1)} %get-tuple-element.103.refs_1_, bf16[384,5760]{1,0:T(8,128)(2,1)} %copy-done.6, f32[4,16,768]{2,1,0:T(8,128)} %get-tuple-element.105.refs_3_, bf16[384,192]{1,0:T(8,128)(2,1)} %copy-done.31), custom_call_target="tpu_custom_call" | custom-call | flops 16142000128 | bytes 14549004 | tf_op jit(solution)/shard_map/pallas_call | solution.py:728
  225.3 1.5 collective-permute-start.20
  227.6 30.3 %shard_map.283 = (bf16[4,384,192]{2,1,0:T(8,128)(2,1)}, f32[4,384,384]{2,1,0:T(8,128)}, bf16[4,384,384]{2,1,0:T(8,128)(2,1)}) custom-call(s32[3]{0:T(128)} %pad_add_fusion.refs_0_, bf16[4,384,192]{2,1,0:T(8,128)(2,1)} %get-tuple-element.84.refs_1_, bf16[8,384,192]{2,1,0:T(8,128)(2,1)} %get-tuple-element.85.refs_2_, ...), custom_call_target="tpu_custom_call" | custom-call | flops 34589999104 | bytes 11667468 | tf_op jit(solution)/shard_map/pallas_call | solution.py:728
  257.8 4.9 %collective-permute-start.15 = (bf16[4,384,384]{2,1,0:T(8,128)(2,1)}, bf16[4,384,384]{2,1,0:T(8,128)(2,1)S(1)}, u32[]{:S(2)}, u32[]{:S(2)}) collective-permute-start(bf16[4,384,384]{2,1,0:T(8,128)(2,1)} %get-tuple-element.96), channel_id=1, source_target_pairs={{0,1},{1,0},{2,3},{3,2},{4,5},{5,4},{6,7},{7,6},{8,9},{9,8},{10,11... | collective-permute-start | bytes 3538952 | tf_op jit(solution)/shard_map/ppermute | solution.py:1179
  262.7 2.7 collective-permute-done.15.refs_3_
  265.4 1.0 copy-done.9
  266.4 3.8 shard_map.284
  270.2 1.5 copy-done.1
  271.7 3.3 shard_map.286
  275.5 2.3 collective-permute-start.17
  277.8 2.1 collective-permute-start.18
  279.9 18.4 %collective-permute-done.16.refs_4_.refs_10_.refs_2_ = bf16[384,576]{1,0:T(8,128)(2,1)S(1)} collective-permute-done((bf16[384,576]{1,0:T(8,128)(2,1)S(1)}, bf16[384,576]{1,0:T(8,128)(2,1)S(1)}, u32[]{:S(2)}, u32[]{:S(2)}) %collective-permute-start.16) | collective-permute-done | bytes 442400 | tf_op jit(solution)/shard_map/ppermute | solution.py:1179
  298.3 13.3 %collective-permute-done.17.refs_5_.refs_11_.refs_3_ = bf16[384,576]{1,0:T(8,128)(2,1)S(1)} collective-permute-done((bf16[384,576]{1,0:T(8,128)(2,1)S(1)}, bf16[384,576]{1,0:T(8,128)(2,1)S(1)}, u32[]{:S(2)}, u32[]{:S(2)}) %collective-permute-start.17) | collective-permute-done | bytes 442400 | tf_op jit(solution)/shard_map/ppermute | solution.py:1179
  312.7 1.1 copy-done.8
  313.8 3.7 shard_map.287
  317.5 8.8 %shard_map.288 = (f32[4,112,576]{2,1,0:T(8,128)}, bf16[4,112,576]{2,1,0:T(8,128)(2,1)}) custom-call(s32[3]{0:T(128)} %pad_add_fusion.refs_0_, bf16[4,384,768]{2,1,0:T(8,128)(2,1)} %get-tuple-element.110.refs_1_, bf16[384,576]{1,0:T(8,128)(2,1)} %get-tuple-element.97.refs_3_.refs_2_.refs_1_, bf16[384,576]{1,0:T(8,128)(2,1)} %get-tuple-element.98.refs_3_, ...), custom_call_target="tpu_custom_call" | custom-call | flops 9223999488 | bytes 6610956 | tf_op jit(solution)/shard_map/pallas_call | solution.py:728
  326.3 10.1 %collective-permute-start.22 = (bf16[448,768]{1,0:T(8,128)(2,1)S(1)}, bf16[448,768]{1,0:T(8,128)(2,1)S(1)}, u32[]{:S(2)}, u32[]{:S(2)}) collective-permute-start(bf16[448,768]{1,0:T(8,128)(2,1)S(1)} %copy-done.14), channel_id=1, source_target_pairs={{0,2},{1,5},{2,0},{3,7},{4,6},{5,1},{6,4},{7,3},{8,10},{9,13},{10,... | collective-permute-start | bytes 2064392 | tf_op jit(solution)/shard_map/ppermute | solution.py:1179
  336.4 1.4 add_convert_fusion
  337.8 1.5 collective-permute-start.24
  339.4 13.4 %collective-permute-done.22.refs_2_ = bf16[448,768]{1,0:T(8,128)(2,1)S(1)} collective-permute-done((bf16[448,768]{1,0:T(8,128)(2,1)S(1)}, bf16[448,768]{1,0:T(8,128)(2,1)S(1)}, u32[]{:S(2)}, u32[]{:S(2)}) %collective-permute-start.22) | collective-permute-done | bytes 688160 | tf_op jit(solution)/shard_map/ppermute | solution.py:1179
  353.6 2.6 shard_map.289
  356.2 2.2 collective-permute-start.30
  358.4 1.5 collective-permute-start.25
  359.9 8.3 %collective-permute-done.30.refs_2_ = bf16[224,768]{1,0:T(8,128)(2,1)S(1)} collective-permute-done((bf16[224,768]{1,0:T(8,128)(2,1)}, bf16[224,768]{1,0:T(8,128)(2,1)S(1)}, u32[]{:S(2)}, u32[]{:S(2)}) %collective-permute-start.30) | collective-permute-done | bytes 344096 | tf_op jit(solution)/shard_map/ppermute | solution.py:1179
  369.0 2.0 shard_map.292.refs_1_
  371.0 1.1 collective-permute-start.31
  372.2 17.9 %collective-permute-done.31.refs_2_ = bf16[224,768]{1,0:T(8,128)(2,1)S(1)} collective-permute-done((bf16[224,768]{1,0:T(8,128)(2,1)}, bf16[224,768]{1,0:T(8,128)(2,1)S(1)}, u32[]{:S(2)}, u32[]{:S(2)}) %collective-permute-start.31) | collective-permute-done | bytes 344096 | tf_op jit(solution)/shard_map/ppermute | solution.py:1179
  390.9 2.0 shard_map.293.refs_1_
  393.0 3.5 collective-permute-start.28
  397.4 6.9 %shard_map.290 = f32[384,768]{1,0:T(8,128)} custom-call(s32[3]{0:T(128)} %pad_add_fusion.refs_0_, bf16[384,576]{1,0:T(8,128)(2,1)} %get-tuple-element.97.refs_3_.refs_2_.refs_1_, bf16[384,576]{1,0:T(8,128)(2,1)} %copy-done.20, bf16[384,576]{1,0:T(8,128)(2,1)} %copy-done.21, bf16[384,576]{1,0:T(8,128)(2,1)} %copy-done.22, ...), custom_call_target="tpu_custom_call" | custom-call | flops 5765000192 | bytes 8306700 | tf_op jit(solution)/shard_map/pallas_call | solution.py:728
  404.4 6.8 %collective-permute-done.32.refs_2_ = bf16[448,768]{1,0:T(8,128)(2,1)S(1)} collective-permute-done((bf16[448,768]{1,0:T(8,128)(2,1)}, bf16[448,768]{1,0:T(8,128)(2,1)S(1)}, u32[]{:S(2)}, u32[]{:S(2)}) %collective-permute-start.32) | collective-permute-done | bytes 688160 | tf_op jit(solution)/shard_map/ppermute | solution.py:1179
  411.2 8.7 %collective-permute-done.28.refs_3_ = bf16[2,112,576]{2,1,0:T(8,128)(2,1)S(1)} collective-permute-done((bf16[2,112,576]{2,1,0:T(8,128)(2,1)S(1)}, bf16[2,112,576]{2,1,0:T(8,128)(2,1)S(1)}, u32[]{:S(2)}, u32[]{:S(2)}) %collective-permute-start.28) | collective-permute-done | bytes 258080 | tf_op jit(solution)/shard_map/ppermute | solution.py:1179
  421.3 3.0 shard_map.291
  428.7 4.6 %shard_map.294 = (f32[768,768]{1,0:T(8,128)}, f32[192,3072]{1,0:T(8,128)}, f32[192,768]{1,0:T(8,128)}, f32[16,768]{1,0:T(8,128)}) custom-call(s32[3]{0:T(128)} %pad_add_fusion.refs_0_, bf16[448,768]{1,0:T(8,128)(2,1)} %shard_map.293.refs_1_, bf16[448,768]{1,0:T(8,128)(2,1)} %copy-done.11, bf16[448,768]{1,0:T(8,128)(2,1)} %copy-done.12, ...), custom_call_target="tpu_custom_call" | custom-call | flops 2305999872 | bytes 8110092 | tf_op jit(solution)/shard_map/pallas_call | solution.py:728
  433.3 1.3 slice_reduce_fusion.1
  434.7 1.4 fusion.9
  (153 shorter events, 22.0 us)
Async XLA Ops:
  7.2 3.9 copy-start.2
  7.2 41.7 %all-gather.5.cloned.1.call-start = ((), (), s32[]{:S(2)}) async-start(), calls=%async_computation | async-start | bytes 2580480 | tf_op jit(solution)/shard_map/all_gather | solution.py:1262
  10.2 1.0 copy-start.4
  11.0 138.1 %all-gather.7.cloned.1.call-start = ((), (), s32[]{:S(2)}) async-start(), calls=%async_computation.1 | async-start | bytes 6635520 | tf_op jit(solution)/shard_map/all_gather | solution.py:1223
  11.2 37.7 %copy-start.16 = (bf16[384,768]{1,0:T(8,128)(2,1)S(1)}, bf16[384,768]{1,0:T(8,128)(2,1)}, u32[]{:S(2)}) copy-start(bf16[384,768]{1,0:T(8,128)(2,1)} %refs_6_.3) | copy-start | bytes 1769476
  11.2 41.8 %copy-start.5 = (s32[1,8]{1,0:T(1,128)S(1)}, s32[1,8]{1,0:T(1,128)}, u32[]{:S(2)}) copy-start(s32[1,8]{1,0:T(1,128)} %param.32) | copy-start | bytes 100
  11.2 43.2 %copy-start.37 = (s32[1,3]{1,0:T(1,128)S(1)}, s32[1,3]{1,0:T(1,128)}, u32[]{:S(2)}) copy-start(s32[1,3]{1,0:T(1,128)} %param.33) | copy-start | bytes 40
  15.0 1.1 copy-start
  48.9 55.9 %collective-permute-start.7 = (bf16[4,112,2304]{2,1,0:T(8,128)(2,1)}, bf16[4,112,2304]{2,1,0:T(8,128)(2,1)S(1)}, u32[]{:S(2)}, u32[]{:S(2)}) collective-permute-start(bf16[4,112,2304]{2,1,0:T(8,128)(2,1)} %bitcast.58), channel_id=1, source_target_pairs={{0,1},{1,0},{2,3},{3,2},{4,5},{5,4},{6,7},{7,6},{8,9},{9,8},{10,11... | collective-permute-start | bytes 6193160 | tf_op jit(solution)/shard_map/ppermute | solution.py:1179
  48.9 15.8 %collective-permute-start.5 = (bf16[384,768]{1,0:T(8,128)(2,1)S(1)}, bf16[384,768]{1,0:T(8,128)(2,1)}, u32[]{:S(2)}, u32[]{:S(2)}) collective-permute-start(bf16[384,768]{1,0:T(8,128)(2,1)S(1)} %copy-done.16), channel_id=1, source_target_pairs={{0,2},{1,3},{2,0},{3,1},{4,6},{5,7},{6,4},{7,5},{8,10},{9,11},{10,... | collective-permute-start | bytes 1769480 | tf_op jit(solution)/shard_map/ppermute | solution.py:1179
  50.4 54.4 %collective-permute-start.4 = (bf16[384,768]{1,0:T(8,128)(2,1)S(1)}, bf16[384,768]{1,0:T(8,128)(2,1)}, u32[]{:S(2)}, u32[]{:S(2)}) collective-permute-start(bf16[384,768]{1,0:T(8,128)(2,1)S(1)} %copy-done.16), channel_id=1, source_target_pairs={{0,1},{1,0},{2,3},{3,2},{4,5},{5,4},{6,7},{7,6},{8,9},{9,8},{10,11... | collective-permute-start | bytes 1769480 | tf_op jit(solution)/shard_map/ppermute | solution.py:1179
  50.6 29.0 %collective-permute-start.2 = (bf16[384,768]{1,0:T(8,128)(2,1)S(1)}, bf16[384,768]{1,0:T(8,128)(2,1)S(1)}, u32[]{:S(2)}, u32[]{:S(2)}) collective-permute-start(bf16[384,768]{1,0:T(8,128)(2,1)S(1)} %copy-done.16), channel_id=1, source_target_pairs={{0,6},{1,7},{2,4},{3,5},{4,2},{5,3},{6,0},{7,1},{8,14},{9,15},{10,... | collective-permute-start | bytes 1769480 | tf_op jit(solution)/shard_map/ppermute | solution.py:1179
  53.0 51.8 %collective-permute-start = (bf16[384,768]{1,0:T(8,128)(2,1)S(1)}, bf16[384,768]{1,0:T(8,128)(2,1)}, u32[]{:S(2)}, u32[]{:S(2)}) collective-permute-start(bf16[384,768]{1,0:T(8,128)(2,1)S(1)} %copy-done.16), channel_id=1, source_target_pairs={{0,4},{1,5},{2,6},{3,7},{4,0},{5,1},{6,2},{7,3},{8,12},{9,13},{10,... | collective-permute-start | bytes 1769480 | tf_op jit(solution)/shard_map/ppermute | solution.py:1179
  64.8 40.1 %collective-permute-start.6 = (bf16[384,768]{1,0:T(8,128)(2,1)}, bf16[384,768]{1,0:T(8,128)(2,1)}, u32[]{:S(2)}, u32[]{:S(2)}) collective-permute-start(bf16[384,768]{1,0:T(8,128)(2,1)} %collective-permute-done.5.refs_3_), channel_id=1, source_target_pairs={{0,1},{1,0},{2,3},{3,2},{4,5},{5,4},{6,7},{7,6},{8,9},{9,8},{10,11... | collective-permute-start | bytes 1769480 | tf_op jit(solution)/shard_map/ppermute | solution.py:1179
  79.6 36.2 %copy-start.17 = (bf16[384,768]{1,0:T(8,128)(2,1)}, bf16[384,768]{1,0:T(8,128)(2,1)S(1)}, u32[]{:S(2)}) copy-start(bf16[384,768]{1,0:T(8,128)(2,1)S(1)} %collective-permute-done.2.refs_3_) | copy-start | bytes 1769476
  79.6 36.3 %collective-permute-start.3 = (bf16[384,768]{1,0:T(8,128)(2,1)S(1)}, bf16[384,768]{1,0:T(8,128)(2,1)S(1)}, u32[]{:S(2)}, u32[]{:S(2)}) collective-permute-start(bf16[384,768]{1,0:T(8,128)(2,1)S(1)} %collective-permute-done.2.refs_3_), channel_id=1, source_target_pairs={{0,1},{1,0},{2,3},{3,2},{4,5},{5,4},{6,7},{7,6},{8,9},{9,8},{10,11... | collective-permute-start | bytes 1769480 | tf_op jit(solution)/shard_map/ppermute | solution.py:1179
  104.8 11.1 %collective-permute-start.1 = (bf16[384,768]{1,0:T(8,128)(2,1)}, bf16[384,768]{1,0:T(8,128)(2,1)S(1)}, u32[]{:S(2)}, u32[]{:S(2)}) collective-permute-start(bf16[384,768]{1,0:T(8,128)(2,1)} %collective-permute-done.refs_1_), channel_id=1, source_target_pairs={{0,1},{1,0},{2,3},{3,2},{4,5},{5,4},{6,7},{7,6},{8,9},{9,8},{10,11... | collective-permute-start | bytes 1769480 | tf_op jit(solution)/shard_map/ppermute | solution.py:1179
  104.9 1.3 copy-start.7
  115.9 1.5 copy-start.18
  115.9 1.5 copy-start.19
  150.4 23.6 %collective-permute-start.11 = (bf16[4,864,768]{2,1,0:T(8,128)(2,1)}, bf16[4,864,768]{2,1,0:T(8,128)(2,1)}, u32[]{:S(2)}, u32[]{:S(2)}) collective-permute-start(bf16[4,864,768]{2,1,0:T(8,128)(2,1)} %fusion.8.refs_9_), channel_id=1, source_target_pairs={{0,1},{1,0},{2,3},{3,2},{4,5},{5,4},{6,7},{7,6},{8,9},{9,8},{10,11... | collective-permute-start | bytes 15925256 | tf_op jit(solution)/shard_map/ppermute | solution.py:1179
  156.1 10.6 %collective-permute-start.8 = (bf16[384,192]{1,0:T(8,128)(2,1)}, bf16[384,192]{1,0:T(8,128)(2,1)S(1)}, u32[]{:S(2)}, u32[]{:S(2)}) collective-permute-start(bf16[384,192]{1,0:T(8,128)(2,1)} %get-tuple-element.79), channel_id=1, source_target_pairs={{0,2},{1,3},{2,0},{3,1},{4,6},{5,7},{6,4},{7,5},{8,10},{9,11},{10,... | collective-permute-start | bytes 442376 | tf_op jit(solution)/shard_map/ppermute | solution.py:1179
  156.1 17.9 %collective-permute-start.9 = (bf16[384,192]{1,0:T(8,128)(2,1)}, bf16[384,192]{1,0:T(8,128)(2,1)S(1)}, u32[]{:S(2)}, u32[]{:S(2)}) collective-permute-start(bf16[384,192]{1,0:T(8,128)(2,1)} %get-tuple-element.80), channel_id=1, source_target_pairs={{0,4},{1,5},{2,6},{3,7},{4,0},{5,1},{6,2},{7,3},{8,12},{9,13},{10,... | collective-permute-start | bytes 442376 | tf_op jit(solution)/shard_map/ppermute | solution.py:1179
  159.6 14.4 %collective-permute-start.10 = (bf16[384,192]{1,0:T(8,128)(2,1)}, bf16[384,192]{1,0:T(8,128)(2,1)S(1)}, u32[]{:S(2)}, u32[]{:S(2)}) collective-permute-start(bf16[384,192]{1,0:T(8,128)(2,1)} %get-tuple-element.81), channel_id=1, source_target_pairs={{0,6},{1,7},{2,4},{3,5},{4,2},{5,3},{6,0},{7,1},{8,14},{9,15},{10,... | collective-permute-start | bytes 442376 | tf_op jit(solution)/shard_map/ppermute | solution.py:1179
  166.7 7.3 %copy-start.32 = (bf16[384,192]{1,0:T(8,128)(2,1)}, bf16[384,192]{1,0:T(8,128)(2,1)S(1)}, u32[]{:S(2)}) copy-start(bf16[384,192]{1,0:T(8,128)(2,1)S(1)} %collective-permute-done.8.refs_2_) | copy-start | bytes 442372
  196.5 13.3 %collective-permute-start.19 = (bf16[384,5760]{1,0:T(8,128)(2,1)}, bf16[384,5760]{1,0:T(8,128)(2,1)S(1)}, u32[]{:S(2)}, u32[]{:S(2)}) collective-permute-start(bf16[384,5760]{1,0:T(8,128)(2,1)} %get-tuple-element.104), channel_id=1, source_target_pairs={{0,1},{1,0},{2,3},{3,2},{4,5},{5,4},{6,7},{7,6},{8,9},{9,8},{10,11... | collective-permute-start | bytes 13271048 | tf_op jit(solution)/shard_map/ppermute | solution.py:1179
  196.5 13.2 %collective-permute-start.12 = (bf16[384,192]{1,0:T(8,128)(2,1)}, bf16[384,192]{1,0:T(8,128)(2,1)S(1)}, u32[]{:S(2)}, u32[]{:S(2)}) collective-permute-start(bf16[384,192]{1,0:T(8,128)(2,1)} %get-tuple-element.89), channel_id=1, source_target_pairs={{0,2},{1,3},{2,0},{3,1},{4,6},{5,7},{6,4},{7,5},{8,10},{9,11},{10,... | collective-permute-start | bytes 442376 | tf_op jit(solution)/shard_map/ppermute | solution.py:1179
  200.4 26.4 %collective-permute-start.13 = (bf16[384,192]{1,0:T(8,128)(2,1)}, bf16[384,192]{1,0:T(8,128)(2,1)S(1)}, u32[]{:S(2)}, u32[]{:S(2)}) collective-permute-start(bf16[384,192]{1,0:T(8,128)(2,1)} %get-tuple-element.90), channel_id=1, source_target_pairs={{0,4},{1,5},{2,6},{3,7},{4,0},{5,1},{6,2},{7,3},{8,12},{9,13},{10,... | collective-permute-start | bytes 442376 | tf_op jit(solution)/shard_map/ppermute | solution.py:1179
  201.3 25.5 %collective-permute-start.14 = (bf16[384,192]{1,0:T(8,128)(2,1)}, bf16[384,192]{1,0:T(8,128)(2,1)S(1)}, u32[]{:S(2)}, u32[]{:S(2)}) collective-permute-start(bf16[384,192]{1,0:T(8,128)(2,1)} %get-tuple-element.91), channel_id=1, source_target_pairs={{0,6},{1,7},{2,4},{3,5},{4,2},{5,3},{6,0},{7,1},{8,14},{9,15},{10,... | collective-permute-start | bytes 442376 | tf_op jit(solution)/shard_map/ppermute | solution.py:1179
  209.8 2.1 copy-start.6
  225.3 44.8 %collective-permute-start.20 = (bf16[2,896,768]{2,1,0:T(8,128)(2,1)}, bf16[2,896,768]{2,1,0:T(8,128)(2,1)S(1)}, u32[]{:S(2)}, u32[]{:S(2)}) collective-permute-start(bf16[2,896,768]{2,1,0:T(8,128)(2,1)} %get-tuple-element.107), channel_id=1, source_target_pairs={{0,8},{1,17},{2,10},{3,19},{4,12},{5,21},{6,14},{7,23},{8,0},{9,25... | collective-permute-start | bytes 8257544 | tf_op jit(solution)/shard_map/ppermute | solution.py:1179
  257.8 7.6 %collective-permute-start.15 = (bf16[4,384,384]{2,1,0:T(8,128)(2,1)}, bf16[4,384,384]{2,1,0:T(8,128)(2,1)S(1)}, u32[]{:S(2)}, u32[]{:S(2)}) collective-permute-start(bf16[4,384,384]{2,1,0:T(8,128)(2,1)} %get-tuple-element.96), channel_id=1, source_target_pairs={{0,1},{1,0},{2,3},{3,2},{4,5},{5,4},{6,7},{7,6},{8,9},{9,8},{10,11... | collective-permute-start | bytes 3538952 | tf_op jit(solution)/shard_map/ppermute | solution.py:1179
  265.4 1.0 copy-start.9
  270.2 1.5 copy-start.1
  271.7 3.8 copy-start.23
  271.7 3.8 copy-start.24
  271.7 6.1 %copy-start.25 = (bf16[384,576]{1,0:T(8,128)(2,1)S(1)}, bf16[384,576]{1,0:T(8,128)(2,1)}, u32[]{:S(2)}) copy-start(bf16[384,576]{1,0:T(8,128)(2,1)} %get-tuple-element.100.refs_5_) | copy-start | bytes 1327108
  275.0 36.7 %collective-permute-start.21 = (bf16[896,768]{1,0:T(8,128)(2,1)}, bf16[896,768]{1,0:T(8,128)(2,1)S(1)}, u32[]{:S(2)}, u32[]{:S(2)}) collective-permute-start(bf16[896,768]{1,0:T(8,128)(2,1)} %shard_map.286), channel_id=1, source_target_pairs={{0,16},{1,9},{2,18},{3,11},{4,20},{5,13},{6,22},{7,15},{8,24},{9,1... | collective-permute-start | bytes 4128776 | tf_op jit(solution)/shard_map/ppermute | solution.py:1179
  275.5 22.8 %collective-permute-start.16 = (bf16[384,576]{1,0:T(8,128)(2,1)S(1)}, bf16[384,576]{1,0:T(8,128)(2,1)S(1)}, u32[]{:S(2)}, u32[]{:S(2)}) collective-permute-start(bf16[384,576]{1,0:T(8,128)(2,1)S(1)} %copy-done.23), channel_id=1, source_target_pairs={{0,2},{1,3},{2,0},{3,1},{4,6},{5,7},{6,4},{7,5},{8,10},{9,11},{10,... | collective-permute-start | bytes 1327112 | tf_op jit(solution)/shard_map/ppermute | solution.py:1179
  275.5 36.2 %collective-permute-start.17 = (bf16[384,576]{1,0:T(8,128)(2,1)S(1)}, bf16[384,576]{1,0:T(8,128)(2,1)S(1)}, u32[]{:S(2)}, u32[]{:S(2)}) collective-permute-start(bf16[384,576]{1,0:T(8,128)(2,1)S(1)} %copy-done.24), channel_id=1, source_target_pairs={{0,4},{1,5},{2,6},{3,7},{4,0},{5,1},{6,2},{7,3},{8,12},{9,13},{10,... | collective-permute-start | bytes 1327112 | tf_op jit(solution)/shard_map/ppermute | solution.py:1179
  277.8 33.9 %collective-permute-start.18 = (bf16[384,576]{1,0:T(8,128)(2,1)S(1)}, bf16[384,576]{1,0:T(8,128)(2,1)S(1)}, u32[]{:S(2)}, u32[]{:S(2)}) collective-permute-start(bf16[384,576]{1,0:T(8,128)(2,1)S(1)} %copy-done.25), channel_id=1, source_target_pairs={{0,6},{1,7},{2,4},{3,5},{4,2},{5,3},{6,0},{7,1},{8,14},{9,15},{10,... | collective-permute-start | bytes 1327112 | tf_op jit(solution)/shard_map/ppermute | solution.py:1179
  298.3 13.4 %copy-start.20 = (bf16[384,576]{1,0:T(8,128)(2,1)}, bf16[384,576]{1,0:T(8,128)(2,1)S(1)}, u32[]{:S(2)}) copy-start(bf16[384,576]{1,0:T(8,128)(2,1)S(1)} %collective-permute-done.16.refs_4_.refs_10_.refs_2_) | copy-start | bytes 1327108
  311.7 1.0 copy-start.22
  312.7 1.1 copy-start.8
  317.5 8.8 %copy-start.14 = (bf16[448,768]{1,0:T(8,128)(2,1)S(1)}, bf16[448,768]{1,0:T(8,128)(2,1)}, u32[]{:S(2)}) copy-start(bf16[448,768]{1,0:T(8,128)(2,1)} %get-tuple-element.109.refs_13_) | copy-start | bytes 2064388
  326.3 10.1 %collective-permute-start.23 = (bf16[4,112,576]{2,1,0:T(8,128)(2,1)}, bf16[4,112,576]{2,1,0:T(8,128)(2,1)S(1)}, u32[]{:S(2)}, u32[]{:S(2)}) collective-permute-start(bf16[4,112,576]{2,1,0:T(8,128)(2,1)} %get-tuple-element.113), channel_id=1, source_target_pairs={{0,1},{1,0},{2,3},{3,2},{4,5},{5,4},{6,7},{7,6},{8,9},{9,8},{10,11... | collective-permute-start | bytes 1548296 | tf_op jit(solution)/shard_map/ppermute | solution.py:1179
  326.3 26.4 %collective-permute-start.22 = (bf16[448,768]{1,0:T(8,128)(2,1)S(1)}, bf16[448,768]{1,0:T(8,128)(2,1)S(1)}, u32[]{:S(2)}, u32[]{:S(2)}) collective-permute-start(bf16[448,768]{1,0:T(8,128)(2,1)S(1)} %copy-done.14), channel_id=1, source_target_pairs={{0,2},{1,5},{2,0},{3,7},{4,6},{5,1},{6,4},{7,3},{8,10},{9,13},{10,... | collective-permute-start | bytes 2064392 | tf_op jit(solution)/shard_map/ppermute | solution.py:1179
  337.8 20.5 %collective-permute-start.24 = (bf16[2,112,576]{2,1,0:T(8,128)(2,1)S(1)}, bf16[2,112,576]{2,1,0:T(8,128)(2,1)S(1)}, u32[]{:S(2)}, u32[]{:S(2)}) collective-permute-start(bf16[2,112,576]{2,1,0:T(8,128)(2,1)S(1)} %slice.98), channel_id=1, source_target_pairs={{0,8},{1,17},{2,10},{3,19},{4,12},{5,21},{6,14},{7,23},{8,0},{9,25... | collective-permute-start | bytes 774152 | tf_op jit(solution)/shard_map/ppermute | solution.py:1179
  352.7 0.8 copy-start.15
  356.2 12.1 %collective-permute-start.30 = (bf16[224,768]{1,0:T(8,128)(2,1)}, bf16[224,768]{1,0:T(8,128)(2,1)S(1)}, u32[]{:S(2)}, u32[]{:S(2)}) collective-permute-start(bf16[224,768]{1,0:T(8,128)(2,1)} %get-tuple-element.112.refs_9_), channel_id=1, source_target_pairs={{0,4},{1,3},{2,6},{3,1},{4,0},{5,7},{6,2},{7,5},{8,12},{9,11},{10,... | collective-permute-start | bytes 1032200 | tf_op jit(solution)/shard_map/ppermute | solution.py:1179
  358.4 13.7 %collective-permute-start.25 = (bf16[112,576]{1,0:T(8,128)(2,1)S(1)}, bf16[112,576]{1,0:T(8,128)(2,1)S(1)}, u32[]{:S(2)}, u32[]{:S(2)}) collective-permute-start(bf16[112,576]{1,0:T(8,128)(2,1)S(1)} %fusion.4), channel_id=1, source_target_pairs={{0,16},{1,9},{2,18},{3,11},{4,20},{5,13},{6,22},{7,15},{8,24},{9,1... | collective-permute-start | bytes 387080 | tf_op jit(solution)/shard_map/ppermute | solution.py:1179
  371.0 19.1 %collective-permute-start.31 = (bf16[224,768]{1,0:T(8,128)(2,1)}, bf16[224,768]{1,0:T(8,128)(2,1)S(1)}, u32[]{:S(2)}, u32[]{:S(2)}) collective-permute-start(bf16[224,768]{1,0:T(8,128)(2,1)} %shard_map.292.refs_1_), channel_id=1, source_target_pairs={{0,4},{1,3},{2,6},{3,1},{4,0},{5,7},{6,2},{7,5},{8,12},{9,11},{10,... | collective-permute-start | bytes 1032200 | tf_op jit(solution)/shard_map/ppermute | solution.py:1179
  372.1 20.7 %collective-permute-start.26 = (bf16[112,576]{1,0:T(8,128)(2,1)S(1)}, bf16[112,576]{1,0:T(8,128)(2,1)S(1)}, u32[]{:S(2)}, u32[]{:S(2)}) collective-permute-start(bf16[112,576]{1,0:T(8,128)(2,1)S(1)} %fusion.2), channel_id=1, source_target_pairs={{0,1},{1,0},{2,3},{3,2},{4,5},{5,4},{6,7},{7,6},{8,9},{9,8},{10,11... | collective-permute-start | bytes 387080 | tf_op jit(solution)/shard_map/ppermute | solution.py:1179
  392.9 18.4 %collective-permute-start.32 = (bf16[448,768]{1,0:T(8,128)(2,1)}, bf16[448,768]{1,0:T(8,128)(2,1)S(1)}, u32[]{:S(2)}, u32[]{:S(2)}) collective-permute-start(bf16[448,768]{1,0:T(8,128)(2,1)} %shard_map.293.refs_1_), channel_id=1, source_target_pairs={{0,2},{1,5},{2,0},{3,7},{4,6},{5,1},{6,4},{7,3},{8,10},{9,13},{10,... | collective-permute-start | bytes 2064392 | tf_op jit(solution)/shard_map/ppermute | solution.py:1179
  392.9 11.4 %copy-start.3 = (bf16[2,112,576]{2,1,0:T(8,128)(2,1)}, bf16[2,112,576]{2,1,0:T(8,128)(2,1)S(1)}, u32[]{:S(2)}) copy-start(bf16[2,112,576]{2,1,0:T(8,128)(2,1)S(1)} %pad_maximum_fusion.refs_1_) | copy-start | bytes 774148
  392.9 18.3 %collective-permute-start.29 = (bf16[2,112,576]{2,1,0:T(8,128)(2,1)S(1)}, bf16[2,112,576]{2,1,0:T(8,128)(2,1)S(1)}, u32[]{:S(2)}, u32[]{:S(2)}) collective-permute-start(bf16[2,112,576]{2,1,0:T(8,128)(2,1)S(1)} %pad_maximum_fusion.refs_1_), channel_id=1, source_target_pairs={{0,6},{1,7},{2,4},{3,5},{4,2},{5,3},{6,0},{7,1},{8,14},{9,15},{10,... | collective-permute-start | bytes 774152 | tf_op jit(solution)/shard_map/ppermute | solution.py:1179
  393.0 26.9 %collective-permute-start.28 = (bf16[2,112,576]{2,1,0:T(8,128)(2,1)S(1)}, bf16[2,112,576]{2,1,0:T(8,128)(2,1)S(1)}, u32[]{:S(2)}, u32[]{:S(2)}) collective-permute-start(bf16[2,112,576]{2,1,0:T(8,128)(2,1)S(1)} %pad_maximum_fusion.refs_1_), channel_id=1, source_target_pairs={{0,4},{1,5},{2,6},{3,7},{4,0},{5,1},{6,2},{7,3},{8,12},{9,13},{10,... | collective-permute-start | bytes 774152 | tf_op jit(solution)/shard_map/ppermute | solution.py:1179
  396.5 23.4 %collective-permute-start.27 = (bf16[2,112,576]{2,1,0:T(8,128)(2,1)S(1)}, bf16[2,112,576]{2,1,0:T(8,128)(2,1)S(1)}, u32[]{:S(2)}, u32[]{:S(2)}) collective-permute-start(bf16[2,112,576]{2,1,0:T(8,128)(2,1)S(1)} %pad_maximum_fusion.refs_1_), channel_id=1, source_target_pairs={{0,2},{1,3},{2,0},{3,1},{4,6},{5,7},{6,4},{7,5},{8,10},{9,11},{10,... | collective-permute-start | bytes 774152 | tf_op jit(solution)/shard_map/ppermute | solution.py:1179
  397.4 7.0 %copy-start.10 = (bf16[448,768]{1,0:T(8,128)(2,1)S(1)}, bf16[448,768]{1,0:T(8,128)(2,1)}, u32[]{:S(2)}) copy-start(bf16[448,768]{1,0:T(8,128)(2,1)} %shard_map.293.refs_1_) | copy-start | bytes 2064388
  404.3 22.7 %collective-permute-start.33 = (bf16[448,768]{1,0:T(8,128)(2,1)S(1)}, bf16[448,768]{1,0:T(8,128)(2,1)S(1)}, u32[]{:S(2)}, u32[]{:S(2)}) collective-permute-start(bf16[448,768]{1,0:T(8,128)(2,1)S(1)} %copy-done.10), channel_id=1, source_target_pairs={{0,1},{1,0},{2,3},{3,2},{4,5},{5,4},{6,7},{7,6},{8,9},{9,8},{10,11... | collective-permute-start | bytes 2064392 | tf_op jit(solution)/shard_map/ppermute | solution.py:1179
  411.2 13.1 %copy-start.11 = (bf16[448,768]{1,0:T(8,128)(2,1)}, bf16[448,768]{1,0:T(8,128)(2,1)S(1)}, u32[]{:S(2)}) copy-start(bf16[448,768]{1,0:T(8,128)(2,1)S(1)} %collective-permute-done.32.refs_2_) | copy-start | bytes 2064388
  411.2 15.8 %collective-permute-start.34 = (bf16[448,768]{1,0:T(8,128)(2,1)S(1)}, bf16[448,768]{1,0:T(8,128)(2,1)S(1)}, u32[]{:S(2)}, u32[]{:S(2)}) collective-permute-start(bf16[448,768]{1,0:T(8,128)(2,1)S(1)} %collective-permute-done.32.refs_2_), channel_id=1, source_target_pairs={{0,1},{1,0},{2,3},{3,2},{4,5},{5,4},{6,7},{7,6},{8,9},{9,8},{10,11... | collective-permute-start | bytes 2064392 | tf_op jit(solution)/shard_map/ppermute | solution.py:1179
  411.2 8.7 %copy-start.28 = (bf16[2,112,576]{2,1,0:T(8,128)(2,1)}, bf16[2,112,576]{2,1,0:T(8,128)(2,1)S(1)}, u32[]{:S(2)}) copy-start(bf16[2,112,576]{2,1,0:T(8,128)(2,1)S(1)} %collective-permute-done.29.refs_4_) | copy-start | bytes 774148
  427.8 0.9 copy-start.13
  (11 other events, 8.1 us)
Sparse Core Ops, SparseCore 0:
  11.1 37.7 all-gather.4
  51.3 61.9 all-gather.6

commit v4 on v2

--- a/solution.py
+++ b/solution.py
@@ -455,12 +455,24 @@
     return jnp.concatenate(parts, axis=1)
 
 
+def stats_kernel(where, *refs):
+    out_ref = refs[-1]
+    for n, ref in enumerate(refs[:-1]):
+        wide = ref[...].astype(FP32)
+        mean = jnp.mean(wide, axis=1, keepdims=True)
+        centre = wide - mean
+        inverse = lax.rsqrt(jnp.mean(centre * centre, axis=1, keepdims=True) + EPS)
+        out_ref[n, :, 0:1] = mean
+        out_ref[n, :, 1:2] = inverse
+
+
 def project_block(
-    tokens_ref, wq_ref, wk_ref, wv_ref, small_ref, chip, stores, position, wanted
+    tokens_ref, row_stats, wq_ref, wk_ref, wv_ref, small_ref, chip, stores, position, wanted
 ):
     q_ref, k_ref, kt_ref, v_ref, vt_ref, normed_ref = stores
     gain, shift = whole_vector(small_ref, 4), whole_vector(small_ref, 5)
-    normed = layer_norm(tokens_ref[...].astype(FP32), gain, shift)[0]
+    centre = tokens_ref[...].astype(FP32) - row_stats[:, 0:1]
+    normed = centre * row_stats[:, 1:2] * gain + shift
     normed = normed.astype(BF16)
     keys = dot_nn(normed, wk_ref[...])
     values = dot_nn(normed, wv_ref[...]) + small_ref[chip, 1:2, :]
@@ -480,12 +492,10 @@
     t1,
     t2,
     t3,
+    stats_ref,
     w_ref,
-    smalls_ref,
-    near_ref,
-    across_ref,
-    near_other,
-    across_other,
+    halves_ref,
+    others_ref,
     q,
     k,
     kt,
@@ -498,25 +508,14 @@
     wv,
     small_ref,
 ):
-    part, core, chip = where[0], where[1], where[2]
-    near, across = 1 + core, 2 - core
+    core, chip = where[1], where[2]
     shard, wide = w_ref.shape
     features, half, width = wide // 3, shard // 2, wq.shape[1]
-    full_ref[pl.ds(pl.multiple_of(part * shard, 16), shard), :] = w_ref[...]
-    small_ref[part] = smalls_ref[...].astype(FP32)
-    step = half + 16
-    pieces = (
-        (near_ref, 0, part ^ near, core),
-        (across_ref, 0, part ^ across, core),
-        (across_ref, step, part ^ 3, core),
-        (near_other, 0, part ^ across, 1 - core),
-        (across_other, 0, part ^ near, 1 - core),
-        (across_other, step, part ^ 3, 1 - core),
-    )
-    for ref, at, owner, which in pieces:
-        first = pl.multiple_of(owner * shard + which * half, 16)
-        full_ref[pl.ds(first, half), :] = ref[at : at + half, :]
-        small_ref[owner] = ref[at + half : at + step, 0:width].astype(FP32)
+    for f in range(halves_ref.shape[0]):
+        for ref, which in ((halves_ref, core), (others_ref, 1 - core)):
+            first = pl.multiple_of(f * shard + which * half, 16)
+            full_ref[pl.ds(first, half), :] = ref[f, 0:half, :]
+        small_ref[f] = halves_ref[f, half:, 0:width].astype(FP32)
     for z in range(features // width):
 
         @pl.when(chip == z)
@@ -529,7 +528,7 @@
     for n, block in enumerate((t0, t1, t2, t3)):
         owner = (chip ^ (n // 2)) % 2
         position = 2 * owner + (core if n % 2 == 0 else 1 - core)
-        project_block(block, wq, wk, wv, small_ref, chip, stores, position, n % 2 == 0)
+        project_block(block, stats_ref[n], wq, wk, wv, small_ref, chip, stores, position, n % 2 == 0)
 
 
 def attend_kernel(
@@ -538,6 +537,7 @@
     t1,
     t2,
     t3,
+    stats_ref,
     wq_ref,
     wk_ref,
     wv_ref,
@@ -579,6 +579,7 @@
         position = 2 * owner + (core if n % 2 == 0 else 1 - core)
         project_block(
             block,
+            stats_ref[4 + n],
             wq_ref,
             wk_ref,
             wv_ref,
@@ -1232,12 +1233,17 @@
         ],
         axis=0,
     )
-    from_near = to_near(mine)
-    from_across = to_across(jnp.concatenate([mine, from_near], axis=0))
-    gathered = (from_near, from_across, to_core(from_near), to_core(from_across))
-    first_tile = tokens[:16, :128] + from_near[:16, :128] * jnp.asarray(0, BF16)
-    swap_tokens = lax.dynamic_update_slice(tokens, first_tile, (0, 0))
-    beside = [to_core(v) for v in [swap_tokens] + blocks[1:]]
+    gathered = lax.all_gather(mine, "fsdp", axis=0)
+    gathered = (gathered, to_core(gathered))
+    beside = [to_core(v) for v in blocks]
+    order = [v for pair in zip(blocks, beside) for v in pair]
+    (stats,) = kernel_call(
+        stats_kernel,
+        [jax.ShapeDtypeStruct((ctx, rows, 2), FP32)],
+        [],
+        (where, *order),
+        40,
+    )
     *half_stores, qkv_full, weight_q, weight_k, weight_v, small_all = kernel_call(
         project_kernel,
         [
@@ -1254,7 +1260,7 @@
             jax.ShapeDtypeStruct((fsdp, 16, width), FP32),
         ],
         [],
-        (where, blocks[0], beside[0], blocks[1], beside[1], w_qkv, smalls) + gathered,
+        (where, blocks[0], beside[0], blocks[1], beside[1], stats, w_qkv) + gathered,
         9,
     )
     queries, keys, keys_t, values, normed_mine, *rest = kernel_call(
@@ -1278,7 +1284,7 @@
             pltpu.VMEM((chips, rows, width), BF16),
         ],
         (where, blocks[2], beside[2], blocks[3], beside[3])
-        + (weight_q, weight_k, weight_v, small_all)
+        + (stats, weight_q, weight_k, weight_v, small_all)
         + tuple(half_stores)
         + (key_tile, low_rows, high_rows, far_rows),
         30,
@@ -1395,7 +1401,7 @@
         [],
         (where, grads_keep, theirs, to_across(relay)),
         2,
-        after=tuple(arrived[1:]),
+        after=(arrived[1],),
     )
 
     grads_half = lax.psum(grads_block, "ctx", axis_index_groups=same_core)

time: 419 us -> 415 us (level)
  waiting for transfers between devices: 174 us -> 159 us
  local copies, waits for them, and re-layouts: 22.4 us -> 29 us
  Pallas kernels: 142 us -> 148 us
    ppermute x33 -> x30, waiting for transfers between devices: 150 us -> 135 us  [exchange(): return lax.ppermute(value, ('fsdp', 'ctx'), pairs)]
    pallas_call x12 -> x13, Pallas kernels: 142 us -> 148 us  [kernel_call(): pl.pallas_call(ordered, out_shape=outputs, in_specs=in_specs, out_specs=[...]
    unnamed x97 -> x70, local copies, waits for them, and re-layouts: 15.2 us -> 19 us
    ppermute x33 -> x30, starting transfers between devices: 52 us -> 48.9 us  [exchange(): return lax.ppermute(value, ('fsdp', 'ctx'), pairs)]
  transfers between devices with their start and end apart: 35 -> 33, of which waited for: 17 -> 16; matrix products, arithmetic and copies ran while one was open for 3% -> 3% of each run, Pallas kernels for 24% -> 27%
where the time goes in v4:
time: 415 us; the launch traced here: 411 us
  waiting for transfers between devices  159 us (38%)
  Pallas kernels  148 us (36%)
  starting transfers between devices  49 us (12%)
  local copies, waits for them, and re-layouts  29 us (7%)
  between operations  14.4 us (3%)
  other arithmetic  11.2 us (3%)
    pallas_call x13, Pallas kernels, kernel_call(): pl.pallas_call(ordered, out_shape=outputs, in_specs=in_specs, out_specs=[...  148 us
    ppermute x30, waiting for transfers between devices, exchange(): return lax.ppermute(value, ('fsdp', 'ctx'), pairs)  135 us
    ppermute x30, starting transfers between devices, exchange(): return lax.ppermute(value, ('fsdp', 'ctx'), pairs)  48.9 us
    psum x1, waiting for transfers between devices, fast_body(): grads_half = lax.psum(grads_block, 'ctx', axis_index_groups=same_core)  23.7 us
    unnamed x70, local copies, waits for them, and re-layouts  19 us
  transfers between devices with their start and end apart: 33, of which 16 were waited for; matrix products, arithmetic and copies ran while one was open for 3% of the time, Pallas kernels for 27%

profile of v4, /device:TPU:0, one launch (start us, length us, event | category | flops | bytes accessed | tf_op | source)
XLA Modules:
  0.0 410.6 jit_solution(16752240081721156118)
XLA Ops:
  7.3 0.9 fusion.14
  8.3 1.0 constant_dynamic-slice_fusion.5
  9.3 0.9 select_select_fusion
  11.1 3.1 collective-permute-start.5
  14.2 2.5 collective-permute-start.2
  16.9 0.9 dynamic-slice_dynamic-update-slice_fusion.4
  17.8 0.9 dynamic-slice_dynamic-update-slice_fusion.3
  18.8 0.9 dynamic-slice_dynamic-update-slice_fusion.2
  19.7 0.9 dynamic-slice_dynamic-update-slice_fusion.1
  20.6 1.1 copy-done.1
  23.6 4.3 %collective-permute-done.5.refs_3_ = bf16[384,768]{1,0:T(8,128)(2,1)} collective-permute-done((bf16[384,768]{1,0:T(8,128)(2,1)S(1)}, bf16[384,768]{1,0:T(8,128)(2,1)}, u32[]{:S(2)}, u32[]{:S(2)}) %collective-permute-start.5) | collective-permute-done | bytes 589856 | tf_op jit(solution)/shard_map/ppermute | solution.py:1160
  27.9 15.8 %collective-permute-done.2.refs_7_.refs_3_ = bf16[384,768]{1,0:T(8,128)(2,1)} collective-permute-done((bf16[384,768]{1,0:T(8,128)(2,1)S(1)}, bf16[384,768]{1,0:T(8,128)(2,1)}, u32[]{:S(2)}, u32[]{:S(2)}) %collective-permute-start.2) | collective-permute-done | bytes 589856 | tf_op jit(solution)/shard_map/ppermute | solution.py:1160
  43.7 25.1 %collective-permute-done.refs_5_.refs_1_ = bf16[384,768]{1,0:T(8,128)(2,1)} collective-permute-done((bf16[384,768]{1,0:T(8,128)(2,1)S(1)}, bf16[384,768]{1,0:T(8,128)(2,1)}, u32[]{:S(2)}, u32[]{:S(2)}) %collective-permute-start) | collective-permute-done | bytes 589856 | tf_op jit(solution)/shard_map/ppermute | solution.py:1160
  73.3 5.5 %shard_map.280.refs_5_ = f32[8,384,2]{2,1,0:T(8,128)} custom-call(s32[3]{0:T(128)} %pad_add_fusion.refs_0_, bf16[384,768]{1,0:T(8,128)(2,1)} %refs_6_.5, bf16[384,768]{1,0:T(8,128)(2,1)} %collective-permute-done.4.refs_2_, bf16[384,768]{1,0:T(8,128)(2,1)} %collective-permute-done.5.refs_3_, bf16[384,768]{1,0:T(8,128)(2,1)} %copy-done.16, ...), custom_call_target="tpu_custom_call" | custom-call | flops 46120001536 | bytes 4743180 | tf_op jit(solution)/shard_map/pallas_call | solution.py:743
  78.8 1.3 copy-done.10
  80.1 10.4 %shard_map.281 = (bf16[2,384,192]{2,1,0:T(8,128)(2,1)}, bf16[4,384,192]{2,1,0:T(8,128)(2,1)}, bf16[4,192,384]{2,1,0:T(8,128)(2,1)}, bf16[4,384,192]{2,1,0:T(8,12...) custom-call(s32[3]{0:T(128)} %pad_add_fusion.refs_0_, ...), custom_call_target="tpu_custom_call" | custom-call | flops 10376999936 | bytes 15704076 | tf_op jit(solution)/shard_map/pallas_call | solution.py:743
  90.5 1.5 broadcast_in_dim.126.refs_16_.refs_9_
  92.0 31.5 %shard_map.282 = (bf16[4,384,192]{2,1,0:T(8,128)(2,1)}, bf16[8,384,192]{2,1,0:T(8,128)(2,1)}, bf16[8,192,384]{2,1,0:T(8,128)(2,1)}, bf16[8,384,192]{2,1,0:T(8,12...) custom-call(s32[3]{0:T(128)} %pad_add_fusion.refs_0_, ...), custom_call_target="tpu_custom_call" | custom-call | flops 34589999104 | bytes 17053708 | tf_op jit(solution)/shard_map/pallas_call | solution.py:743
  123.5 1.3 fusion.9.refs_9_
  124.8 5.0 %collective-permute-start.11 = (bf16[4,864,768]{2,1,0:T(8,128)(2,1)}, bf16[4,864,768]{2,1,0:T(8,128)(2,1)}, u32[]{:S(2)}, u32[]{:S(2)}) collective-permute-start(bf16[4,864,768]{2,1,0:T(8,128)(2,1)} %fusion.9.refs_9_), channel_id=1, source_target_pairs={{0,1},{1,0},{2,3},{3,2},{4,5},{5,4},{6,7},{7,6},{8,9},{9,8},{10,11... | collective-permute-start | bytes 15925256 | tf_op jit(solution)/shard_map/ppermute | solution.py:1160
  129.8 2.8 collective-permute-start.9
  132.6 1.6 collective-permute-start.10
  134.7 1.3 fusion.3.refs_7_
  136.1 4.3 %collective-permute-done.8.refs_2_ = bf16[384,192]{1,0:T(8,128)(2,1)S(1)} collective-permute-done((bf16[384,192]{1,0:T(8,128)(2,1)}, bf16[384,192]{1,0:T(8,128)(2,1)S(1)}, u32[]{:S(2)}, u32[]{:S(2)}) %collective-permute-start.8) | collective-permute-done | bytes 147488 | tf_op jit(solution)/shard_map/ppermute | solution.py:1160
  140.3 6.8 %collective-permute-done.9.refs_3_ = bf16[384,192]{1,0:T(8,128)(2,1)S(1)} collective-permute-done((bf16[384,192]{1,0:T(8,128)(2,1)}, bf16[384,192]{1,0:T(8,128)(2,1)S(1)}, u32[]{:S(2)}, u32[]{:S(2)}) %collective-permute-start.9) | collective-permute-done | bytes 147488 | tf_op jit(solution)/shard_map/ppermute | solution.py:1160
  147.8 21.7 %shard_map.283 = (bf16[384,768]{1,0:T(8,128)(2,1)}, f32[384,768]{1,0:T(8,128)}, bf16[384,192]{1,0:T(8,128)(2,1)}, bf16[384,192]{1,0:T(8,128)(2,1)}, bf16[384,192...) custom-call(s32[3]{0:T(128)} %pad_add_fusion.refs_0_, ...), custom_call_target="tpu_custom_call" | custom-call | flops 24213000192 | bytes 23840268 | tf_op jit(solution)/shard_map/pallas_call | solution.py:743
  169.7 3.8 collective-permute-start.12
  174.4 1.6 collective-permute-start.14
  175.9 6.9 %collective-permute-done.12.refs_6_.refs_4_ = bf16[384,192]{1,0:T(8,128)(2,1)S(1)} collective-permute-done((bf16[384,192]{1,0:T(8,128)(2,1)}, bf16[384,192]{1,0:T(8,128)(2,1)S(1)}, u32[]{:S(2)}, u32[]{:S(2)}) %collective-permute-start.12) | collective-permute-done | bytes 147488 | tf_op jit(solution)/shard_map/ppermute | solution.py:1160
  183.5 1.5 copy-done.9
  185.0 13.4 %shard_map.286 = (bf16[2,896,768]{2,1,0:T(8,128)(2,1)}, bf16[2,896,768]{2,1,0:T(8,128)(2,1)}) custom-call(s32[3]{0:T(128)} %pad_add_fusion.refs_0_, bf16[384,5760]{1,0:T(8,128)(2,1)} %get-tuple-element.101.refs_1_, bf16[384,5760]{1,0:T(8,128)(2,1)} %copy-done.9, f32[4,16,768]{2,1,0:T(8,128)} %get-tuple-element.103.refs_3_, bf16[384,192]{1,0:T(8,128)(2,1)} %copy-done.25), custom_call_target="tpu_custom_call" | custom-call | flops 16142000128 | bytes 14549004 | tf_op jit(solution)/shard_map/pallas_call | solution.py:743
  198.4 1.4 collective-permute-start.20
  200.6 30.3 %shard_map.284 = (bf16[4,384,192]{2,1,0:T(8,128)(2,1)}, f32[4,384,384]{2,1,0:T(8,128)}, bf16[4,384,384]{2,1,0:T(8,128)(2,1)}) custom-call(s32[3]{0:T(128)} %pad_add_fusion.refs_0_, bf16[4,384,192]{2,1,0:T(8,128)(2,1)} %get-tuple-element.81.refs_1_, bf16[8,384,192]{2,1,0:T(8,128)(2,1)} %get-tuple-element.82.refs_2_, ...), custom_call_target="tpu_custom_call" | custom-call | flops 34589999104 | bytes 11667468 | tf_op jit(solution)/shard_map/pallas_call | solution.py:743
  230.9 4.9 %collective-permute-start.15 = (bf16[4,384,384]{2,1,0:T(8,128)(2,1)}, bf16[4,384,384]{2,1,0:T(8,128)(2,1)S(1)}, u32[]{:S(2)}, u32[]{:S(2)}) collective-permute-start(bf16[4,384,384]{2,1,0:T(8,128)(2,1)} %get-tuple-element.93), channel_id=1, source_target_pairs={{0,1},{1,0},{2,3},{3,2},{4,5},{5,4},{6,7},{7,6},{8,9},{9,8},{10,11... | collective-permute-start | bytes 3538952 | tf_op jit(solution)/shard_map/ppermute | solution.py:1160
  235.8 2.7 collective-permute-done.15.refs_3_
  238.5 1.0 copy-done.12
  239.5 3.8 shard_map.285
  243.2 1.5 copy-done
  244.8 4.1 %shard_map.287 = bf16[896,768]{1,0:T(8,128)(2,1)} custom-call(s32[3]{0:T(128)} %pad_add_fusion.refs_0_, bf16[2,896,768]{2,1,0:T(8,128)(2,1)} %get-tuple-element.104.refs_1_, bf16[2,896,768]{2,1,0:T(8,128)(2,1)} %copy-done, bf16[384,576]{1,0:T(8,128)(2,1)} %get-tuple-element.94.refs_3_.refs_2_.refs_1_), custom_call_target="tpu_custom_call" | custom-call | flops 1152999936 | bytes 6881292 | tf_op jit(solution)/shard_map/pallas_call | solution.py:743
  249.5 2.4 collective-permute-start.17
  251.8 2.0 collective-permute-start.18
  253.8 19.0 %collective-permute-done.16.refs_4_.refs_10_.refs_2_ = bf16[384,576]{1,0:T(8,128)(2,1)S(1)} collective-permute-done((bf16[384,576]{1,0:T(8,128)(2,1)S(1)}, bf16[384,576]{1,0:T(8,128)(2,1)S(1)}, u32[]{:S(2)}, u32[]{:S(2)}) %collective-permute-start.16) | collective-permute-done | bytes 442400 | tf_op jit(solution)/shard_map/ppermute | solution.py:1160
  273.7 1.1 copy-done.2
  274.7 4.6 %shard_map.288.refs_13_ = bf16[896,768]{1,0:T(8,128)(2,1)} custom-call(s32[3]{0:T(128)} %pad_add_fusion.refs_0_, bf16[2,896,768]{2,1,0:T(8,128)(2,1)} %get-tuple-element.104.refs_1_, bf16[2,896,768]{2,1,0:T(8,128)(2,1)} %copy-done, bf16[896,768]{1,0:T(8,128)(2,1)} %copy-done.2, bf16[384,576]{1,0:T(8,128)(2,1)} %copy-done.3), custom_call_target="tpu_custom_call" | custom-call | flops 2305999872 | bytes 8257548 | tf_op jit(solution)/shard_map/pallas_call | solution.py:743
  279.3 6.3 %collective-permute-done.17.refs_11_.refs_3_ = bf16[384,576]{1,0:T(8,128)(2,1)S(1)} collective-permute-done((bf16[384,576]{1,0:T(8,128)(2,1)S(1)}, bf16[384,576]{1,0:T(8,128)(2,1)S(1)}, u32[]{:S(2)}, u32[]{:S(2)}) %collective-permute-start.17) | collective-permute-done | bytes 442400 | tf_op jit(solution)/shard_map/ppermute | solution.py:1160
  286.5 8.8 %shard_map.289 = (f32[4,112,576]{2,1,0:T(8,128)}, bf16[4,112,576]{2,1,0:T(8,128)(2,1)}) custom-call(s32[3]{0:T(128)} %pad_add_fusion.refs_0_, bf16[4,384,768]{2,1,0:T(8,128)(2,1)} %get-tuple-element.100.refs_1_, bf16[384,576]{1,0:T(8,128)(2,1)} %get-tuple-element.94.refs_3_.refs_2_.refs_1_, bf16[384,576]{1,0:T(8,128)(2,1)} %get-tuple-element.95.refs_3_, ...), custom_call_target="tpu_custom_call" | custom-call | flops 9223999488 | bytes 6610956 | tf_op jit(solution)/shard_map/pallas_call | solution.py:743
  295.4 2.1 collective-permute-done.22
  297.5 1.4 add_convert_fusion
  298.9 1.5 collective-permute-start.23
  300.4 5.1 %collective-permute-done.23.refs_9_ = bf16[2,112,576]{2,1,0:T(8,128)(2,1)S(1)} collective-permute-done((bf16[2,112,576]{2,1,0:T(8,128)(2,1)S(1)}, bf16[2,112,576]{2,1,0:T(8,128)(2,1)S(1)}, u32[]{:S(2)}, u32[]{:S(2)}) %collective-permute-start.23) | collective-permute-done | bytes 258080 | tf_op jit(solution)/shard_map/ppermute | solution.py:1160
  305.6 1.6 collective-permute-start.24
  307.2 3.6 collective-permute-done.24
  310.9 1.4 collective-permute-done.25
  312.4 1.9 collective-permute-start.28
  314.3 10.5 %collective-permute-start.27 = (bf16[2,112,576]{2,1,0:T(8,128)(2,1)S(1)}, bf16[2,112,576]{2,1,0:T(8,128)(2,1)S(1)}, u32[]{:S(2)}, u32[]{:S(2)}) collective-permute-start(bf16[2,112,576]{2,1,0:T(8,128)(2,1)S(1)} %pad_maximum_fusion.refs_1_), channel_id=1, source_target_pairs={{0,4},{1,5},{2,6},{3,7},{4,0},{5,1},{6,2},{7,3},{8,12},{9,13},{10,... | collective-permute-start | bytes 774152 | tf_op jit(solution)/shard_map/ppermute | solution.py:1160
  324.8 6.9 %shard_map.290.refs_5_ = f32[384,768]{1,0:T(8,128)} custom-call(s32[3]{0:T(128)} %pad_add_fusion.refs_0_, bf16[384,576]{1,0:T(8,128)(2,1)} %get-tuple-element.94.refs_3_.refs_2_.refs_1_, bf16[384,576]{1,0:T(8,128)(2,1)} %copy-done.3, bf16[384,576]{1,0:T(8,128)(2,1)} %copy-done.17, bf16[384,576]{1,0:T(8,128)(2,1)} %copy-done.18, ...), custom_call_target="tpu_custom_call" | custom-call | flops 5765000192 | bytes 8306700 | tf_op jit(solution)/shard_map/pallas_call | solution.py:743
  331.7 31.0 %collective-permute-done.27.refs_3_ = bf16[2,112,576]{2,1,0:T(8,128)(2,1)S(1)} collective-permute-done((bf16[2,112,576]{2,1,0:T(8,128)(2,1)S(1)}, bf16[2,112,576]{2,1,0:T(8,128)(2,1)S(1)}, u32[]{:S(2)}, u32[]{:S(2)}) %collective-permute-start.27) | collective-permute-done | bytes 258080 | tf_op jit(solution)/shard_map/ppermute | solution.py:1160
  364.1 3.0 shard_map.291
  367.1 23.7 %all-reduce.3.cloned.1.call-done = bf16[896,768]{1,0:T(8,128)(2,1)} async-done(((bf16[896,768]{1,0:T(8,128)(2,1)}), bf16[896,768]{1,0:T(8,128)(2,1)}) %all-reduce.3.cloned.1.call-update) | async-done | bytes 1376272 | tf_op jit(solution)/shard_map/psum | solution.py:1407
  390.9 1.3 fusion.6.refs_1_
  395.5 1.1 copy-done.11
  396.6 4.5 %shard_map.292 = (f32[768,768]{1,0:T(8,128)}, f32[192,3072]{1,0:T(8,128)}, f32[192,768]{1,0:T(8,128)}, f32[16,768]{1,0:T(8,128)}) custom-call(s32[3]{0:T(128)} %pad_add_fusion.refs_0_, bf16[896,768]{1,0:T(8,128)(2,1)} %fusion.6.refs_1_, bf16[896,768]{1,0:T(8,128)(2,1)} %copy-done.11), custom_call_target="tpu_custom_call" | custom-call | flops 2305999872 | bytes 8110092 | tf_op jit(solution)/shard_map/pallas_call | solution.py:743
  401.1 1.3 slice_reduce_fusion.1
  402.4 1.4 fusion.11
  (133 shorter events, 18.7 us)
Async XLA Ops:
  7.2 3.9 copy-start.13
  7.2 9.6 %copy-start.4 = (bf16[768,768]{1,0:T(8,128)(2,1)S(1)}, bf16[768,768]{1,0:T(8,128)(2,1)}, u32[]{:S(2)}) copy-start(bf16[768,768]{1,0:T(8,128)(2,1)} %param.26) | copy-start | bytes 3538948
  7.2 63.8 %all-gather.5.cloned.1.call-start = ((), (), s32[]{:S(2)}) async-start(), calls=%async_computation.1 | async-start | bytes 2580480 | tf_op jit(solution)/shard_map/all_gather | solution.py:1236
  10.2 6.7 %copy-start.7 = (bf16[192,768]{1,0:T(8,128)(2,1)S(1)}, bf16[192,768]{1,0:T(8,128)(2,1)}, u32[]{:S(2)}) copy-start(bf16[192,768]{1,0:T(8,128)(2,1)} %param.22) | copy-start | bytes 884740
  11.0 112.5 %all-gather.7.cloned.1.call-start = ((), (), s32[]{:S(2)}) async-start(), calls=%async_computation.2 | async-start | bytes 6635520 | tf_op jit(solution)/shard_map/all_gather | solution.py:1197
  11.1 16.8 %collective-permute-start.5 = (bf16[384,768]{1,0:T(8,128)(2,1)S(1)}, bf16[384,768]{1,0:T(8,128)(2,1)}, u32[]{:S(2)}, u32[]{:S(2)}) collective-permute-start(bf16[384,768]{1,0:T(8,128)(2,1)S(1)} %copy-done.13), channel_id=1, source_target_pairs={{0,2},{1,3},{2,0},{3,1},{4,6},{5,7},{6,4},{7,5},{8,10},{9,11},{10,... | collective-permute-start | bytes 1769480 | tf_op jit(solution)/shard_map/ppermute | solution.py:1160
  14.2 57.3 %collective-permute-start.4 = (bf16[384,768]{1,0:T(8,128)(2,1)S(1)}, bf16[384,768]{1,0:T(8,128)(2,1)}, u32[]{:S(2)}, u32[]{:S(2)}) collective-permute-start(bf16[384,768]{1,0:T(8,128)(2,1)S(1)} %copy-done.13), channel_id=1, source_target_pairs={{0,1},{1,0},{2,3},{3,2},{4,5},{5,4},{6,7},{7,6},{8,9},{9,8},{10,11... | collective-permute-start | bytes 1769480 | tf_op jit(solution)/shard_map/ppermute | solution.py:1160
  14.2 29.5 %collective-permute-start.2 = (bf16[384,768]{1,0:T(8,128)(2,1)S(1)}, bf16[384,768]{1,0:T(8,128)(2,1)}, u32[]{:S(2)}, u32[]{:S(2)}) collective-permute-start(bf16[384,768]{1,0:T(8,128)(2,1)S(1)} %copy-done.13), channel_id=1, source_target_pairs={{0,6},{1,7},{2,4},{3,5},{4,2},{5,3},{6,0},{7,1},{8,14},{9,15},{10,... | collective-permute-start | bytes 1769480 | tf_op jit(solution)/shard_map/ppermute | solution.py:1160
  16.7 52.1 %collective-permute-start = (bf16[384,768]{1,0:T(8,128)(2,1)S(1)}, bf16[384,768]{1,0:T(8,128)(2,1)}, u32[]{:S(2)}, u32[]{:S(2)}) collective-permute-start(bf16[384,768]{1,0:T(8,128)(2,1)S(1)} %copy-done.13), channel_id=1, source_target_pairs={{0,4},{1,5},{2,6},{3,7},{4,0},{5,1},{6,2},{7,3},{8,12},{9,13},{10,... | collective-permute-start | bytes 1769480 | tf_op jit(solution)/shard_map/ppermute | solution.py:1160
  16.9 4.9 %copy-start.8 = (s32[1,8]{1,0:T(1,128)S(1)}, s32[1,8]{1,0:T(1,128)}, u32[]{:S(2)}) copy-start(s32[1,8]{1,0:T(1,128)} %param.32) | copy-start | bytes 100
  16.9 6.2 %copy-start.31 = (s32[1,3]{1,0:T(1,128)S(1)}, s32[1,3]{1,0:T(1,128)}, u32[]{:S(2)}) copy-start(s32[1,3]{1,0:T(1,128)} %param.33) | copy-start | bytes 40
  20.6 1.1 copy-start.1
  27.9 43.6 %collective-permute-start.6 = (bf16[384,768]{1,0:T(8,128)(2,1)}, bf16[384,768]{1,0:T(8,128)(2,1)S(1)}, u32[]{:S(2)}, u32[]{:S(2)}) collective-permute-start(bf16[384,768]{1,0:T(8,128)(2,1)} %collective-permute-done.5.refs_3_), channel_id=1, source_target_pairs={{0,1},{1,0},{2,3},{3,2},{4,5},{5,4},{6,7},{7,6},{8,9},{9,8},{10,11... | collective-permute-start | bytes 1769480 | tf_op jit(solution)/shard_map/ppermute | solution.py:1160
  43.7 27.8 %collective-permute-start.3 = (bf16[384,768]{1,0:T(8,128)(2,1)}, bf16[384,768]{1,0:T(8,128)(2,1)S(1)}, u32[]{:S(2)}, u32[]{:S(2)}) collective-permute-start(bf16[384,768]{1,0:T(8,128)(2,1)} %collective-permute-done.2.refs_7_.refs_3_), channel_id=1, source_target_pairs={{0,1},{1,0},{2,3},{3,2},{4,5},{5,4},{6,7},{7,6},{8,9},{9,8},{10,11... | collective-permute-start | bytes 1769480 | tf_op jit(solution)/shard_map/ppermute | solution.py:1160
  68.8 2.7 collective-permute-start.1
  71.0 7.8 %collective-permute-start.7 = (bf16[4,112,2304]{2,1,0:T(8,128)(2,1)}, bf16[4,112,2304]{2,1,0:T(8,128)(2,1)S(1)}, u32[]{:S(2)}, u32[]{:S(2)}) collective-permute-start(bf16[4,112,2304]{2,1,0:T(8,128)(2,1)} %bitcast.58), channel_id=1, source_target_pairs={{0,1},{1,0},{2,3},{3,2},{4,5},{5,4},{6,7},{7,6},{8,9},{9,8},{10,11... | collective-permute-start | bytes 6193160 | tf_op jit(solution)/shard_map/ppermute | solution.py:1160
  71.5 0.9 copy-start.16
  71.5 1.0 copy-start.14
  72.5 0.8 copy-start.15
  78.8 1.3 copy-start.10
  124.8 22.3 %collective-permute-start.11 = (bf16[4,864,768]{2,1,0:T(8,128)(2,1)}, bf16[4,864,768]{2,1,0:T(8,128)(2,1)}, u32[]{:S(2)}, u32[]{:S(2)}) collective-permute-start(bf16[4,864,768]{2,1,0:T(8,128)(2,1)} %fusion.9.refs_9_), channel_id=1, source_target_pairs={{0,1},{1,0},{2,3},{3,2},{4,5},{5,4},{6,7},{7,6},{8,9},{9,8},{10,11... | collective-permute-start | bytes 15925256 | tf_op jit(solution)/shard_map/ppermute | solution.py:1160
  129.7 10.6 %collective-permute-start.8 = (bf16[384,192]{1,0:T(8,128)(2,1)}, bf16[384,192]{1,0:T(8,128)(2,1)S(1)}, u32[]{:S(2)}, u32[]{:S(2)}) collective-permute-start(bf16[384,192]{1,0:T(8,128)(2,1)} %get-tuple-element.76), channel_id=1, source_target_pairs={{0,2},{1,3},{2,0},{3,1},{4,6},{5,7},{6,4},{7,5},{8,10},{9,11},{10,... | collective-permute-start | bytes 442376 | tf_op jit(solution)/shard_map/ppermute | solution.py:1160
  129.8 17.3 %collective-permute-start.9 = (bf16[384,192]{1,0:T(8,128)(2,1)}, bf16[384,192]{1,0:T(8,128)(2,1)S(1)}, u32[]{:S(2)}, u32[]{:S(2)}) collective-permute-start(bf16[384,192]{1,0:T(8,128)(2,1)} %get-tuple-element.77), channel_id=1, source_target_pairs={{0,4},{1,5},{2,6},{3,7},{4,0},{5,1},{6,2},{7,3},{8,12},{9,13},{10,... | collective-permute-start | bytes 442376 | tf_op jit(solution)/shard_map/ppermute | solution.py:1160
  132.6 14.5 %collective-permute-start.10 = (bf16[384,192]{1,0:T(8,128)(2,1)}, bf16[384,192]{1,0:T(8,128)(2,1)S(1)}, u32[]{:S(2)}, u32[]{:S(2)}) collective-permute-start(bf16[384,192]{1,0:T(8,128)(2,1)} %get-tuple-element.78), channel_id=1, source_target_pairs={{0,6},{1,7},{2,4},{3,5},{4,2},{5,3},{6,0},{7,1},{8,14},{9,15},{10,... | collective-permute-start | bytes 442376 | tf_op jit(solution)/shard_map/ppermute | solution.py:1160
  140.3 6.8 %copy-start.26 = (bf16[384,192]{1,0:T(8,128)(2,1)}, bf16[384,192]{1,0:T(8,128)(2,1)S(1)}, u32[]{:S(2)}) copy-start(bf16[384,192]{1,0:T(8,128)(2,1)S(1)} %collective-permute-done.8.refs_2_) | copy-start | bytes 442372
  147.1 0.7 copy-start.28
  147.1 0.7 copy-start.30
  169.6 13.3 %collective-permute-start.19 = (bf16[384,5760]{1,0:T(8,128)(2,1)}, bf16[384,5760]{1,0:T(8,128)(2,1)S(1)}, u32[]{:S(2)}, u32[]{:S(2)}) collective-permute-start(bf16[384,5760]{1,0:T(8,128)(2,1)} %get-tuple-element.102), channel_id=1, source_target_pairs={{0,1},{1,0},{2,3},{3,2},{4,5},{5,4},{6,7},{7,6},{8,9},{9,8},{10,11... | collective-permute-start | bytes 13271048 | tf_op jit(solution)/shard_map/ppermute | solution.py:1160
  169.7 13.2 %collective-permute-start.12 = (bf16[384,192]{1,0:T(8,128)(2,1)}, bf16[384,192]{1,0:T(8,128)(2,1)S(1)}, u32[]{:S(2)}, u32[]{:S(2)}) collective-permute-start(bf16[384,192]{1,0:T(8,128)(2,1)} %get-tuple-element.86), channel_id=1, source_target_pairs={{0,2},{1,3},{2,0},{3,1},{4,6},{5,7},{6,4},{7,5},{8,10},{9,11},{10,... | collective-permute-start | bytes 442376 | tf_op jit(solution)/shard_map/ppermute | solution.py:1160
  173.5 26.3 %collective-permute-start.13 = (bf16[384,192]{1,0:T(8,128)(2,1)}, bf16[384,192]{1,0:T(8,128)(2,1)S(1)}, u32[]{:S(2)}, u32[]{:S(2)}) collective-permute-start(bf16[384,192]{1,0:T(8,128)(2,1)} %get-tuple-element.87), channel_id=1, source_target_pairs={{0,4},{1,5},{2,6},{3,7},{4,0},{5,1},{6,2},{7,3},{8,12},{9,13},{10,... | collective-permute-start | bytes 442376 | tf_op jit(solution)/shard_map/ppermute | solution.py:1160
  174.4 25.5 %collective-permute-start.14 = (bf16[384,192]{1,0:T(8,128)(2,1)}, bf16[384,192]{1,0:T(8,128)(2,1)S(1)}, u32[]{:S(2)}, u32[]{:S(2)}) collective-permute-start(bf16[384,192]{1,0:T(8,128)(2,1)} %get-tuple-element.88), channel_id=1, source_target_pairs={{0,6},{1,7},{2,4},{3,5},{4,2},{5,3},{6,0},{7,1},{8,14},{9,15},{10,... | collective-permute-start | bytes 442376 | tf_op jit(solution)/shard_map/ppermute | solution.py:1160
  182.8 2.1 copy-start.9
  198.4 44.9 %collective-permute-start.20 = (bf16[2,896,768]{2,1,0:T(8,128)(2,1)}, bf16[2,896,768]{2,1,0:T(8,128)(2,1)S(1)}, u32[]{:S(2)}, u32[]{:S(2)}) collective-permute-start(bf16[2,896,768]{2,1,0:T(8,128)(2,1)} %get-tuple-element.105), channel_id=1, source_target_pairs={{0,8},{1,17},{2,10},{3,19},{4,12},{5,21},{6,14},{7,23},{8,0},{9,25... | collective-permute-start | bytes 8257544 | tf_op jit(solution)/shard_map/ppermute | solution.py:1160
  199.8 0.7 copy-start.27
  199.8 0.8 copy-start.29
  230.9 7.6 %collective-permute-start.15 = (bf16[4,384,384]{2,1,0:T(8,128)(2,1)}, bf16[4,384,384]{2,1,0:T(8,128)(2,1)S(1)}, u32[]{:S(2)}, u32[]{:S(2)}) collective-permute-start(bf16[4,384,384]{2,1,0:T(8,128)(2,1)} %get-tuple-element.93), channel_id=1, source_target_pairs={{0,1},{1,0},{2,3},{3,2},{4,5},{5,4},{6,7},{7,6},{8,9},{9,8},{10,11... | collective-permute-start | bytes 3538952 | tf_op jit(solution)/shard_map/ppermute | solution.py:1160
  238.5 1.0 copy-start.12
  243.2 1.5 copy-start
  244.8 4.7 %copy-start.19 = (bf16[384,576]{1,0:T(8,128)(2,1)S(1)}, bf16[384,576]{1,0:T(8,128)(2,1)}, u32[]{:S(2)}) copy-start(bf16[384,576]{1,0:T(8,128)(2,1)} %get-tuple-element.95.refs_3_) | copy-start | bytes 1327108
  244.8 4.7 %copy-start.20 = (bf16[384,576]{1,0:T(8,128)(2,1)S(1)}, bf16[384,576]{1,0:T(8,128)(2,1)}, u32[]{:S(2)}) copy-start(bf16[384,576]{1,0:T(8,128)(2,1)} %get-tuple-element.96.refs_4_) | copy-start | bytes 1327108
  244.8 7.1 %copy-start.21 = (bf16[384,576]{1,0:T(8,128)(2,1)S(1)}, bf16[384,576]{1,0:T(8,128)(2,1)}, u32[]{:S(2)}) copy-start(bf16[384,576]{1,0:T(8,128)(2,1)} %get-tuple-element.97.refs_5_) | copy-start | bytes 1327108
  248.9 24.0 %collective-permute-start.21 = (bf16[896,768]{1,0:T(8,128)(2,1)}, bf16[896,768]{1,0:T(8,128)(2,1)S(1)}, u32[]{:S(2)}, u32[]{:S(2)}) collective-permute-start(bf16[896,768]{1,0:T(8,128)(2,1)} %shard_map.287), channel_id=1, source_target_pairs={{0,16},{1,9},{2,18},{3,11},{4,20},{5,13},{6,22},{7,15},{8,24},{9,1... | collective-permute-start | bytes 4128776 | tf_op jit(solution)/shard_map/ppermute | solution.py:1160
  249.4 23.4 %collective-permute-start.16 = (bf16[384,576]{1,0:T(8,128)(2,1)S(1)}, bf16[384,576]{1,0:T(8,128)(2,1)S(1)}, u32[]{:S(2)}, u32[]{:S(2)}) collective-permute-start(bf16[384,576]{1,0:T(8,128)(2,1)S(1)} %copy-done.19), channel_id=1, source_target_pairs={{0,2},{1,3},{2,0},{3,1},{4,6},{5,7},{6,4},{7,5},{8,10},{9,11},{10,... | collective-permute-start | bytes 1327112 | tf_op jit(solution)/shard_map/ppermute | solution.py:1160
  249.5 36.1 %collective-permute-start.17 = (bf16[384,576]{1,0:T(8,128)(2,1)S(1)}, bf16[384,576]{1,0:T(8,128)(2,1)S(1)}, u32[]{:S(2)}, u32[]{:S(2)}) collective-permute-start(bf16[384,576]{1,0:T(8,128)(2,1)S(1)} %copy-done.20), channel_id=1, source_target_pairs={{0,4},{1,5},{2,6},{3,7},{4,0},{5,1},{6,2},{7,3},{8,12},{9,13},{10,... | collective-permute-start | bytes 1327112 | tf_op jit(solution)/shard_map/ppermute | solution.py:1160
  251.8 33.8 %collective-permute-start.18 = (bf16[384,576]{1,0:T(8,128)(2,1)S(1)}, bf16[384,576]{1,0:T(8,128)(2,1)S(1)}, u32[]{:S(2)}, u32[]{:S(2)}) collective-permute-start(bf16[384,576]{1,0:T(8,128)(2,1)S(1)} %copy-done.21), channel_id=1, source_target_pairs={{0,6},{1,7},{2,4},{3,5},{4,2},{5,3},{6,0},{7,1},{8,14},{9,15},{10,... | collective-permute-start | bytes 1327112 | tf_op jit(solution)/shard_map/ppermute | solution.py:1160
  272.9 0.8 copy-start.3
  273.7 1.1 copy-start.2
  285.6 0.8 copy-start.17
  285.6 0.9 copy-start.18
  295.3 95.6 %all-reduce.3.cloned.1.call-start = ((), (), s32[]{:S(2)}) async-start(), calls=%async_computation | async-start | bytes 2752512 | tf_op jit(solution)/shard_map/psum | solution.py:1407
  295.3 2.2 collective-permute-start.22
  298.9 6.7 %collective-permute-start.23 = (bf16[2,112,576]{2,1,0:T(8,128)(2,1)S(1)}, bf16[2,112,576]{2,1,0:T(8,128)(2,1)S(1)}, u32[]{:S(2)}, u32[]{:S(2)}) collective-permute-start(bf16[2,112,576]{2,1,0:T(8,128)(2,1)S(1)} %slice.101), channel_id=1, source_target_pairs={{0,8},{1,17},{2,10},{3,19},{4,12},{5,21},{6,14},{7,23},{8,0},{9,25... | collective-permute-start | bytes 774152 | tf_op jit(solution)/shard_map/ppermute | solution.py:1160
  305.6 19.2 %copy-start.5 = (bf16[2,112,576]{2,1,0:T(8,128)(2,1)}, bf16[2,112,576]{2,1,0:T(8,128)(2,1)S(1)}, u32[]{:S(2)}) copy-start(bf16[2,112,576]{2,1,0:T(8,128)(2,1)S(1)} %collective-permute-done.23.refs_9_) | copy-start | bytes 774148
  305.6 5.2 %collective-permute-start.24 = (bf16[112,576]{1,0:T(8,128)(2,1)S(1)}, bf16[112,576]{1,0:T(8,128)(2,1)S(1)}, u32[]{:S(2)}, u32[]{:S(2)}) collective-permute-start(bf16[112,576]{1,0:T(8,128)(2,1)S(1)} %fusion.4), channel_id=1, source_target_pairs={{0,16},{1,9},{2,18},{3,11},{4,20},{5,13},{6,22},{7,15},{8,24},{9,1... | collective-permute-start | bytes 387080 | tf_op jit(solution)/shard_map/ppermute | solution.py:1160
  310.9 1.4 collective-permute-start.25
  312.3 19.3 %copy-start.6 = (bf16[2,112,576]{2,1,0:T(8,128)(2,1)}, bf16[2,112,576]{2,1,0:T(8,128)(2,1)S(1)}, u32[]{:S(2)}) copy-start(bf16[2,112,576]{2,1,0:T(8,128)(2,1)S(1)} %pad_maximum_fusion.refs_1_) | copy-start | bytes 774148
  312.4 19.3 %collective-permute-start.28 = (bf16[2,112,576]{2,1,0:T(8,128)(2,1)S(1)}, bf16[2,112,576]{2,1,0:T(8,128)(2,1)S(1)}, u32[]{:S(2)}, u32[]{:S(2)}) collective-permute-start(bf16[2,112,576]{2,1,0:T(8,128)(2,1)S(1)} %pad_maximum_fusion.refs_1_), channel_id=1, source_target_pairs={{0,6},{1,7},{2,4},{3,5},{4,2},{5,3},{6,0},{7,1},{8,14},{9,15},{10,... | collective-permute-start | bytes 774152 | tf_op jit(solution)/shard_map/ppermute | solution.py:1160
  314.3 48.4 %collective-permute-start.27 = (bf16[2,112,576]{2,1,0:T(8,128)(2,1)S(1)}, bf16[2,112,576]{2,1,0:T(8,128)(2,1)S(1)}, u32[]{:S(2)}, u32[]{:S(2)}) collective-permute-start(bf16[2,112,576]{2,1,0:T(8,128)(2,1)S(1)} %pad_maximum_fusion.refs_1_), channel_id=1, source_target_pairs={{0,4},{1,5},{2,6},{3,7},{4,0},{5,1},{6,2},{7,3},{8,12},{9,13},{10,... | collective-permute-start | bytes 774152 | tf_op jit(solution)/shard_map/ppermute | solution.py:1160
  324.8 37.9 %collective-permute-start.26 = (bf16[2,112,576]{2,1,0:T(8,128)(2,1)S(1)}, bf16[2,112,576]{2,1,0:T(8,128)(2,1)S(1)}, u32[]{:S(2)}, u32[]{:S(2)}) collective-permute-start(bf16[2,112,576]{2,1,0:T(8,128)(2,1)S(1)} %pad_maximum_fusion.refs_1_), channel_id=1, source_target_pairs={{0,2},{1,3},{2,0},{3,1},{4,6},{5,7},{6,4},{7,5},{8,10},{9,11},{10,... | collective-permute-start | bytes 774152 | tf_op jit(solution)/shard_map/ppermute | solution.py:1160
  331.7 31.0 %copy-start.22 = (bf16[2,112,576]{2,1,0:T(8,128)(2,1)}, bf16[2,112,576]{2,1,0:T(8,128)(2,1)S(1)}, u32[]{:S(2)}) copy-start(bf16[2,112,576]{2,1,0:T(8,128)(2,1)S(1)} %collective-permute-done.28.refs_4_) | copy-start | bytes 774148
  362.7 0.7 copy-start.23
  363.4 0.7 copy-start.24
  392.2 3.3 collective-permute-start.29
  395.5 1.1 copy-start.11
  (1 other events, 0.7 us)
Sparse Core Ops, SparseCore 0:
  11.2 37.7 all-gather.4
  51.3 61.9 all-gather.6
  300.6 90.2 all-reduce.2
